TPU v7x, 512 devices: a whole 4x8x8 slice. The times are simulated.
512 devices in a mesh: box: 64 (over x, y, core), samp: 8 (over z).
Axes of the slice: x: 4, y: 8, z: 8, core: 2. Of those that a mesh axis runs over, the one named last changes fastest.
Arguments:
- fine_pattern: float32 [2, 1536, 64, 128], P(None, 'box', 'samp'), may hold values from -6 to 6
- fine_partner: int32 [1536, 16], P('box'), may hold values from 0 to 1535, as said below
- fine_offset: int32 [1536, 16], P('box'), may hold values from 0 to 15
- fine_count: int32 [1536], P('box'), may hold values from 1 to 16, as said below
- coarse_partner: int32 [192, 16], P('box'), may hold values from 0 to 191, as said below
- coarse_offset: int32 [192, 16], P('box'), may hold values from 0 to 15
- coarse_count: int32 [192], P('box'), may hold values from 1 to 16, as said below
- fine_table: float32 [2, 16, 64, 128], P(None, None, 'samp'), may hold values from -1.5 to 1.5
- coarse_table: float32 [2, 16, 128, 256], P(None, None, 'samp'), may hold values from -1.5 to 1.5
- theta_start: int32 [128], P('samp'), may hold values from 0 to 60, as said below
- theta_weight: float32 [128, 4], P('samp'), may hold values from -0.5 to 1
- phi_interp: float32 [256, 128], replicated, may hold values from -0.1875 to 0.1875
- shift_phase: float32 [8, 128, 256], P(None, 'samp'), may hold values from -3.140625 to 3.140625
Outputs:
- fine_incoming: float32 [2, 1536, 64, 128], P(None, 'box', 'samp')
- coarse_incoming: float32 [2, 192, 128, 256], P(None, 'box', 'samp')
Inputs may be any that keep to these rules, and one draw needn't show every extreme that they name: `fine_partner`: partners of a box on box index d lie on box indices d - 1 to d + 1, are distinct, never the box itself or the boxes next to it in order; some box on each inner index has partners on both ends of that range. Slots at and after the box's count hold the box itself. `fine_count`: counts are limited by the boxes available in the range above. `coarse_partner`: partners of a box on box index d lie on box indices d - 4 to d + 4, are distinct, never the box itself or the boxes next to it in order; some box on each inner index has partners on both ends of that range. Slots at and after the box's count hold the box itself. `coarse_count`: counts are limited by the boxes available in the range above. `theta_start`: for upper-level row i, the start lies between floor(i / 2) - 2 and floor(i / 2) - 1, clamped to the grid.
All inputs are finite; a program needn't handle non-finite values.
Results may differ from a plain program's by a relative error of at most 0.00007.
Values sent between devices are 32-bit elements; how exact they have to be, the bound alone decides.
No kernel may reach another device: no remote copies, remote signals or barrier semaphores. Data moves between devices by JAX's collectives and lax.ppermute only.
A program may use at most 64 MiB of HBM per device.

v0:
```python
import jax
import jax.numpy as jnp
from jax import lax
from jax.sharding import PartitionSpec as P


def padded(x, sides, width):
    for axis, dim in sides:
        peers, length = (lax.axis_size(axis), x.shape[dim])
        up = [(i, (i + 1) % peers) for i in range(peers - 1)]
        down = [(j, i) for i, j in up]
        last = lax.slice_in_dim(x, length - width, length, axis=dim)
        initial = lax.slice_in_dim(x, 0, width, axis=dim)
        before = lax.ppermute(last, axis, up)
        after = lax.ppermute(initial, axis, down)
        x = jnp.concatenate([before, x, after], axis=dim)
    return x


def translate(window, base, table, partner, offset, count):
    slots = partner.shape[1]
    local = partner - base
    start = jnp.zeros((2, partner.shape[0]) + window.shape[2:], jnp.float32)

    def step(block, total):
        columns = lax.dynamic_slice_in_dim(local, block * 8, 8, 1)
        offsets = lax.dynamic_slice_in_dim(offset, block * 8, 8, 1)
        numbers = block * 8 + jnp.arange(8, dtype=jnp.int32)
        alive = (numbers[None, :] < count[:, None]).astype(jnp.float32)[:, :, None, None]
        source = window[:, columns]
        operator = table[:, offsets]
        real_part = jnp.sum((operator[0] * source[0] - operator[1] * source[1]) * alive, axis=1)
        imag_part = jnp.sum((operator[0] * source[1] + operator[1] * source[0]) * alive, axis=1)
        return total + jnp.stack([real_part, imag_part])

    return lax.fori_loop(0, slots // 8, step, start)


def aggregate(source, start_row, theta_weight, phi_interp, shift_phase):
    grid = jnp.arange(source.shape[2], dtype=jnp.int32)
    stencil = start_row[:, None] + jnp.arange(4, dtype=jnp.int32)[None, :]
    picked = (stencil[:, :, None] == grid[None, None, :]).astype(jnp.float32)
    theta_matrix = jnp.sum(theta_weight[:, :, None] * picked, axis=1)
    narrow = jnp.einsum("xbrp,ir->xbip", source, theta_matrix, precision=lax.Precision.HIGHEST)
    widened = jnp.einsum("xbip,qp->xbiq", narrow, phi_interp, precision=lax.Precision.HIGHEST)
    widened = widened.reshape(2, widened.shape[1] // 8, 8, widened.shape[2], widened.shape[3])
    cosine = jnp.cos(shift_phase)[None]
    sine = jnp.sin(shift_phase)[None]
    real_part = jnp.sum(cosine * widened[0] - sine * widened[1], axis=1)
    imag_part = jnp.sum(cosine * widened[1] + sine * widened[0], axis=1)
    return jnp.stack([real_part, imag_part])


def reach_of(slots, boxes):
    return (slots + 3 + 2 * boxes - 1) // (2 * boxes)


def shards(
    fine_pattern,
    fine_partner,
    fine_offset,
    fine_count,
    coarse_partner,
    coarse_offset,
    coarse_count,
    fine_table,
    coarse_table,
    theta_start,
    theta_weight,
    phi_interp,
    shift_phase,
):
    place = lax.axis_index("box")
    slots = fine_partner.shape[1]
    fine_boxes = fine_pattern.shape[1]
    fine_margin = reach_of(slots, fine_boxes) * fine_boxes
    fine_window = padded(fine_pattern, (("box", 1),), fine_margin)
    fine_incoming = translate(
        fine_window,
        place * fine_boxes - fine_margin,
        fine_table,
        fine_partner,
        fine_offset,
        fine_count,
    )
    rows_dev = fine_pattern.shape[2]
    rimmed = padded(fine_pattern, (("samp", 2),), 2)
    first_row = lax.axis_index("samp") * rows_dev - 2
    coarse_pattern = aggregate(
        rimmed, theta_start - first_row, theta_weight, phi_interp, shift_phase
    )
    all_partner, all_offset, all_count = (
        lax.all_gather(coarse_partner, "box", axis=0, tiled=True),
        lax.all_gather(coarse_offset, "box", axis=0, tiled=True),
        lax.all_gather(coarse_count, "box", axis=0, tiled=True),
    )
    by_column = lax.all_to_all(coarse_pattern, "box", split_axis=3, concat_axis=1, tiled=True)
    width = by_column.shape[3]
    table_part = lax.dynamic_slice_in_dim(coarse_table, place * width, width, 3)
    column_incoming = translate(by_column, 0, table_part, all_partner, all_offset, all_count)
    coarse_incoming = lax.all_to_all(
        column_incoming, "box", split_axis=1, concat_axis=3, tiled=True
    )
    return (fine_incoming, coarse_incoming)


def solution(mesh):
    return jax.shard_map(
        shards,
        mesh=mesh,
        in_specs=(
            P(None, "box", "samp", None),
            P("box", None),
            P("box", None),
            P("box"),
            P("box", None),
            P("box", None),
            P("box"),
            P(None, None, "samp", None),
            P(None, None, "samp", None),
            P("samp"),
            P("samp", None),
            P(),
            P(None, "samp", None),
        ),
        out_specs=(P(None, "box", "samp", None), P(None, "box", "samp", None)),
        check_vma=False,
    )
```

profile of v0, /device:TPU:205, one launch (start us, length us, event | category | flops | bytes accessed | tf_op | source)
XLA Modules:
  0.0 263.9 jit_solution(5153806677165130719)
XLA Ops:
  0.6 3.9 %collective-permute-start = (f32[2,24,8,128]{3,2,1,0:T(8,128)}, f32[2,24,8,128]{3,2,1,0:T(8,128)S(1)}, u32[]{:S(2)}, u32[]{:S(2)}) collective-permute-start(f32[2,24,8,128]{3,2,1,0:T(8,128)} %param.17), channel_id=1, source_target_pairs={{0,8},{8,16},{16,24},{24,32},{32,40},{40,48},{48,56},{56,64},{64,7... | collective-permute-start | bytes 589832 | tf_op jit(solution)/shard_map/ppermute | solution.py:14
  4.6 1.9 collective-permute-start.1
  6.5 1.1 fusion.16
  7.5 5.2 %collective-permute-start.2 = (f32[2,24,2,128]{3,2,1,0:T(2,128)S(1)}, f32[2,24,2,128]{3,2,1,0:T(2,128)S(1)}, u32[]{:S(2)}, u32[]{:S(2)}) collective-permute-start(f32[2,24,2,128]{3,2,1,0:T(2,128)S(1)} %get-tuple-element.390), channel_id=1, source_target_pairs={{0,1},{1,2},{2,3},{3,4},{4,5},{5,6},{6,7},{8,9},{9,10},{10,11},{11... | collective-permute-start | bytes 147464 | tf_op jit(solution)/shard_map/ppermute | solution.py:14
  12.8 1.9 collective-permute-start.3
  14.7 0.7 broadcast_subtract_fusion.1
  15.4 1.4 fusion.17
  16.7 0.8 copy.109
  17.5 0.6 broadcast_subtract_fusion
  18.1 0.7 select_reduce_fusion
  18.8 1.5 convolution_bitcast_fusion
  20.3 1.7 fusion.11
  22.3 0.6 copy.113
  22.8 1.7 reshape.198
  24.5 13.4 %all-to-all-start = ((f32[64,1,384]{2,1,0:T(1,128)}), f32[64,1,384]{2,1,0:T(1,128)S(1)}, u32[]{:S(2)}, u32[]{:S(2)}) async-start(f32[64,1,384]{2,1,0:T(1,128)} %reshape.198), calls=%async_computation | async-start | bytes 196608 | tf_op jit(solution)/shard_map/all_to_all | solution.py:97
  38.4 49.0 %all-gather = s32[64,3,16]{2,1,0:T(4,128)S(1)} all-gather(s32[1,3,16]{2,1,0:T(4,128)S(1)} %bitcast.133), channel_id=1, replica_groups=mesh['box'=64,'samp'=8] {'box'}, dimensions={0}, use_global_device_ids=true | all-gather | bytes 12480 | tf_op jit(solution)/shard_map/all_gather | solution.py:94
  87.4 47.7 %all-gather.1 = s32[64,3,16]{2,1,0:T(4,128)S(1)} all-gather(s32[1,3,16]{2,1,0:T(4,128)S(1)} %bitcast.134), channel_id=1, replica_groups=mesh['box'=64,'samp'=8] {'box'}, dimensions={0}, use_global_device_ids=true | all-gather | bytes 12480 | tf_op jit(solution)/shard_map/all_gather | solution.py:93
  135.1 1.3 dynamic-slice
  137.4 13.7 %all-reduce = s32[192]{0:T(256)S(1)} all-reduce(s32[192]{0:T(256)S(1)} %dynamic-update-slice), channel_id=1, replica_groups=mesh['box'=64,'samp'=8] {'box'}, use_global_device_ids=true, to_apply=%add | all-reduce | flops 192 | bytes 1536
  151.1 0.9 pad_maximum_fusion
  152.0 0.6 broadcast.197
  152.6 0.9 reduce
  153.5 1.0 reshape.199
  154.8 74.8 %while.29 = (s32[]{:T(128)}, f32[2,192,16,4]{1,2,3,0:T(8,128)S(1)}, s32[192,16]{1,0:T(8,128)S(1)}, f32[2,16,16,4]{2,3,1,0:T(4,128)S(1)}, s32[192,16]{1,0:T(8,128...) while((s32[]{:T(128)}, f32[2,192,16,4]{1,2,3,0:T(8,128)S(1)}, ...), condition=%wide.region_10.0_spmd.clone, body=%wide.region_7.0_spmd.clone.sunk | while | flops 1048591 | bytes 8569837 | solution.py:36
  155.1 7.1 %gather_fusion.2 = f32[1536,2,16,4]{2,3,1,0:T(4,128)} fusion(f32[2,192,16,4]{2,3,1,0:T(4,128)S(1)} %get-tuple-element.552, s32[2048]{0:T(1024)S(1)} %pad_clamp_fusion.10), kind=kCustom, calls=%fused_computation.3.clone.clone.1 | custom fusion | bytes 1579008 | tf_op jit(solution)/shard_map/while/body/eval_jaxpr/gather | solution.py:30
  162.2 6.7 %copy.142 = f32[1536,2,16,4]{2,0,3,1:T(8,128)} copy(f32[1536,2,16,4]{2,3,1,0:T(4,128)} %gather_fusion.2) | data formatting | bytes 1572864 | tf_op jit(solution)/shard_map/while/body/eval_jaxpr/gather | solution.py:30
  169.0 7.2 %gather_fusion.3 = f32[1536,2,16,4]{2,3,1,0:T(4,128)} fusion(f32[2,16,16,4]{2,3,1,0:T(4,128)S(1)} %get-tuple-element.550, s32[2048]{0:T(1024)S(1)} %pad_clamp_fusion.11), kind=kCustom, calls=%fused_computation.2.clone.clone.1 | custom fusion | bytes 1579008 | tf_op jit(solution)/shard_map/while/body/eval_jaxpr/gather | solution.py:31
  176.2 6.7 %copy.143 = f32[1536,2,16,4]{2,0,3,1:T(8,128)} copy(f32[1536,2,16,4]{2,3,1,0:T(4,128)} %gather_fusion.3) | data formatting | bytes 1572864 | tf_op jit(solution)/shard_map/while/body/eval_jaxpr/gather | solution.py:31
  183.0 8.8 %fusion.22 = (f32[192,16,4]{1,0,2:T(8,128)S(1)}, f32[192,16,4]{1,0,2:T(8,128)S(1)}) fusion(f32[2,192,8,16,4]{3,2,1,4,0:T(8,128)} %bitcast.114, f32[2,192,8,16,4]{3,2,1,4,0:T(8,128)} %bitcast.115, f32[192,8]{1,0:T(8,128)S(1)} %copy.144), kind=kLoop, calls=%fused_computation.27.clone.1 | loop fusion | flops 958464 | bytes 1677312 | tf_op jit(solution)/shard_map/while/body/eval_jaxpr/reduce_sum | solution.py:32
  192.5 7.1 %gather_fusion.2 = f32[1536,2,16,4]{2,3,1,0:T(4,128)} fusion(f32[2,192,16,4]{2,3,1,0:T(4,128)S(1)} %get-tuple-element.552, s32[2048]{0:T(1024)S(1)} %pad_clamp_fusion.10), kind=kCustom, calls=%fused_computation.3.clone.clone.1 | custom fusion | bytes 1579008 | tf_op jit(solution)/shard_map/while/body/eval_jaxpr/gather | solution.py:30
  199.6 6.7 %copy.142 = f32[1536,2,16,4]{2,0,3,1:T(8,128)} copy(f32[1536,2,16,4]{2,3,1,0:T(4,128)} %gather_fusion.2) | data formatting | bytes 1572864 | tf_op jit(solution)/shard_map/while/body/eval_jaxpr/gather | solution.py:30
  206.4 7.2 %gather_fusion.3 = f32[1536,2,16,4]{2,3,1,0:T(4,128)} fusion(f32[2,16,16,4]{2,3,1,0:T(4,128)S(1)} %get-tuple-element.550, s32[2048]{0:T(1024)S(1)} %pad_clamp_fusion.11), kind=kCustom, calls=%fused_computation.2.clone.clone.1 | custom fusion | bytes 1579008 | tf_op jit(solution)/shard_map/while/body/eval_jaxpr/gather | solution.py:31
  213.6 6.7 %copy.143 = f32[1536,2,16,4]{2,0,3,1:T(8,128)} copy(f32[1536,2,16,4]{2,3,1,0:T(4,128)} %gather_fusion.3) | data formatting | bytes 1572864 | tf_op jit(solution)/shard_map/while/body/eval_jaxpr/gather | solution.py:31
  220.4 8.8 %fusion.22 = (f32[192,16,4]{1,0,2:T(8,128)S(1)}, f32[192,16,4]{1,0,2:T(8,128)S(1)}) fusion(f32[2,192,8,16,4]{3,2,1,4,0:T(8,128)} %bitcast.114, f32[2,192,8,16,4]{3,2,1,4,0:T(8,128)} %bitcast.115, f32[192,8]{1,0:T(8,128)S(1)} %copy.144), kind=kLoop, calls=%fused_computation.27.clone.1 | loop fusion | flops 958464 | bytes 1677312 | tf_op jit(solution)/shard_map/while/body/eval_jaxpr/reduce_sum | solution.py:32
  230.0 1.3 reshape.200
  231.3 14.2 %all-to-all-start.1 = ((f32[64,1,384]{2,1,0:T(1,128)}), f32[64,1,384]{2,1,0:T(1,128)S(1)}, u32[]{:S(2)}, u32[]{:S(2)}) async-start(f32[64,1,384]{2,1,0:T(1,128)} %reshape.200), calls=%async_computation.1 | async-start | bytes 196608 | tf_op jit(solution)/shard_map/all_to_all | solution.py:101
  245.5 15.8 %while.28 = (s32[]{:T(128)}, f32[2,24,8,128]{3,2,1,0:T(8,128)S(1)}, s32[24,16]{0,1:T(8,128)S(1)}, f32[2,16,8,128]{3,2,1,0:T(8,128)S(1)}, s32[24,16]{1,0:T(8,128)...) while((s32[]{:T(128)}, f32[2,24,8,128]{3,2,1,0:T(8,128)S(1)}, ...), condition=%wide.region_3.0_spmd.clone, body=%wide.region_0.0_spmd.clone.sunk | while | flops 2067983 | bytes 15751021 | solution.py:36
  245.7 1.9 gather_fusion.1
  247.6 1.6 copy.141
  249.4 1.9 gather_fusion
  251.4 1.9 fusion.21
  253.6 1.9 gather_fusion.1
  255.5 1.6 copy.141
  257.3 1.9 gather_fusion
  259.3 1.9 fusion.21
  261.3 0.9 reduce.1
  262.3 0.6 reshape.201
  263.0 0.9 copy.119
  (92 shorter events, 4.5 us)
Async XLA Ops:
  0.6 37.3 %copy-start = (f32[2,16,16,256]{3,2,1,0:T(8,128)S(1)}, f32[2,16,16,256]{3,2,1,0:T(8,128)}, u32[]{:S(2)}) copy-start(f32[2,16,16,256]{3,2,1,0:T(8,128)} %param.25) | copy-start | bytes 1572868
  0.6 150.5 %collective-permute-start = (f32[2,24,8,128]{3,2,1,0:T(8,128)}, f32[2,24,8,128]{3,2,1,0:T(8,128)S(1)}, u32[]{:S(2)}, u32[]{:S(2)}) collective-permute-start(f32[2,24,8,128]{3,2,1,0:T(8,128)} %param.17), channel_id=1, source_target_pairs={{0,8},{8,16},{16,24},{24,32},{32,40},{40,48},{48,56},{56,64},{64,7... | collective-permute-start | bytes 589832 | tf_op jit(solution)/shard_map/ppermute | solution.py:14
  4.6 146.6 %collective-permute-start.1 = (f32[2,24,8,128]{3,2,1,0:T(8,128)}, f32[2,24,8,128]{3,2,1,0:T(8,128)S(1)}, u32[]{:S(2)}, u32[]{:S(2)}) collective-permute-start(f32[2,24,8,128]{3,2,1,0:T(8,128)} %param.17), channel_id=1, source_target_pairs={{8,0},{16,8},{24,16},{32,24},{40,32},{48,40},{56,48},{64,56},{72,6... | collective-permute-start | bytes 589832 | tf_op jit(solution)/shard_map/ppermute | solution.py:15
  7.5 11.3 %collective-permute-start.2 = (f32[2,24,2,128]{3,2,1,0:T(2,128)S(1)}, f32[2,24,2,128]{3,2,1,0:T(2,128)S(1)}, u32[]{:S(2)}, u32[]{:S(2)}) collective-permute-start(f32[2,24,2,128]{3,2,1,0:T(2,128)S(1)} %get-tuple-element.390), channel_id=1, source_target_pairs={{0,1},{1,2},{2,3},{3,4},{4,5},{5,6},{6,7},{8,9},{9,10},{10,11},{11... | collective-permute-start | bytes 147464 | tf_op jit(solution)/shard_map/ppermute | solution.py:14
  12.8 6.1 %collective-permute-start.3 = (f32[2,24,2,128]{3,2,1,0:T(2,128)S(1)}, f32[2,24,2,128]{3,2,1,0:T(2,128)S(1)}, u32[]{:S(2)}, u32[]{:S(2)}) collective-permute-start(f32[2,24,2,128]{3,2,1,0:T(2,128)S(1)} %get-tuple-element.391), channel_id=1, source_target_pairs={{1,0},{2,1},{3,2},{4,3},{5,4},{6,5},{7,6},{9,8},{10,9},{11,10},{12... | collective-permute-start | bytes 147464 | tf_op jit(solution)/shard_map/ppermute | solution.py:15
  22.0 16.4 %copy-start.9 = (s32[3,16]{1,0:T(4,128)S(1)}, s32[3,16]{1,0:T(4,128)}, u32[]{:S(2)}) copy-start(s32[3,16]{1,0:T(4,128)} %param.22) | copy-start | bytes 580
  22.0 65.4 %copy-start.10 = (s32[3,16]{1,0:T(4,128)S(1)}, s32[3,16]{1,0:T(4,128)}, u32[]{:S(2)}) copy-start(s32[3,16]{1,0:T(4,128)} %param.21) | copy-start | bytes 580
  22.0 115.2 %copy-start.11 = (s32[3]{0:T(128)S(1)}, s32[3]{0:T(128)}, u32[]{:S(2)}) copy-start(s32[3]{0:T(128)} %param.23) | copy-start | bytes 40
  22.0 129.1 %copy-start.5 = (f32[2,24,8,128]{3,2,1,0:T(8,128)S(1)}, f32[2,24,8,128]{3,2,1,0:T(8,128)}, u32[]{:S(2)}) copy-start(f32[2,24,8,128]{3,2,1,0:T(8,128)} %param.17) | copy-start | bytes 589828
  24.5 127.5 %all-to-all-start = ((f32[64,1,384]{2,1,0:T(1,128)}), f32[64,1,384]{2,1,0:T(1,128)S(1)}, u32[]{:S(2)}, u32[]{:S(2)}) async-start(f32[64,1,384]{2,1,0:T(1,128)} %reshape.198), calls=%async_computation | async-start | bytes 196608 | tf_op jit(solution)/shard_map/all_to_all | solution.py:97
  154.7 90.7 %copy-start.1 = (f32[2,16,8,128]{3,2,1,0:T(8,128)S(1)}, f32[2,16,8,128]{3,2,1,0:T(8,128)}, u32[]{:S(2)}) copy-start(f32[2,16,8,128]{3,2,1,0:T(8,128)} %param.24) | copy-start | bytes 393220
  154.7 90.7 %copy-start.3 = (f32[2,24,8,128]{3,2,1,0:T(8,128)S(1)}, f32[2,24,8,128]{3,2,1,0:T(8,128)}, u32[]{:S(2)}) copy-start(f32[2,24,8,128]{3,2,1,0:T(8,128)} %custom-call) | copy-start | bytes 589828
  154.8 90.7 %copy-start.6 = (s32[24,16]{1,0:T(8,128)S(1)}, s32[24,16]{1,0:T(8,128)}, u32[]{:S(2)}) copy-start(s32[24,16]{1,0:T(8,128)} %broadcast_subtract_fusion) | copy-start | bytes 4612
  154.8 90.7 %copy-start.7 = (s32[24,16]{0,1:T(8,128)S(1)}, s32[24,16]{0,1:T(8,128)}, u32[]{:S(2)}) copy-start(s32[24,16]{0,1:T(8,128)} %param.19) | copy-start | bytes 4612
  154.8 90.7 %copy-start.8 = (s32[24]{0:T(128)S(1)}, s32[24]{0:T(128)}, u32[]{:S(2)}) copy-start(s32[24]{0:T(128)} %param.20) | copy-start | bytes 292
  231.3 30.1 %all-to-all-start.1 = ((f32[64,1,384]{2,1,0:T(1,128)}), f32[64,1,384]{2,1,0:T(1,128)S(1)}, u32[]{:S(2)}, u32[]{:S(2)}) async-start(f32[64,1,384]{2,1,0:T(1,128)} %reshape.200), calls=%async_computation.1 | async-start | bytes 196608 | tf_op jit(solution)/shard_map/all_to_all | solution.py:101
  245.7 3.7 %copy-start.2 = (f32[2,72,8,128]{3,2,1,0:T(8,128)S(1)}, f32[2,72,8,128]{3,2,1,0:T(8,128)}, u32[]{:S(2)}) copy-start(f32[2,72,8,128]{3,2,1,0:T(8,128)} %get-tuple-element.519) | copy-start | bytes 1769476 | tf_op jit(solution)/shard_map/while
  253.6 3.7 %copy-start.2 = (f32[2,72,8,128]{3,2,1,0:T(8,128)S(1)}, f32[2,72,8,128]{3,2,1,0:T(8,128)}, u32[]{:S(2)}) copy-start(f32[2,72,8,128]{3,2,1,0:T(8,128)} %get-tuple-element.519) | copy-start | bytes 1769476 | tf_op jit(solution)/shard_map/while
  261.3 2.6 copy-start.4
where the time goes:
time: 265 us; the launch traced here: 264 us
  blocking collectives  110 us (42%)
  local copies, waits for them, and re-layouts  80.6 us (30%)
  starting transfers between devices  40.5 us (15%)
  other arithmetic  27.2 us (10%)
  matrix products  3.14 us (1%)
    all_gather x1, blocking collectives, shards(): lax.all_gather(coarse_offset, 'box', axis=0, tiled=True)  49 us
    all_gather x1, blocking collectives, shards(): lax.all_gather(coarse_partner, 'box', axis=0, tiled=True)  47.7 us
    gather x8, local copies, waits for them, and re-layouts, step(): operator = table[:, offsets]  34.7 us
    gather x6, local copies, waits for them, and re-layouts, step(): source = window[:, columns]  31.4 us
    reduce_sum x4, other arithmetic, step(): jnp.sum((operator[0] * source[0] - operator[1] * source[1]) * alive, axis=1)  21.4 us
    all_to_all x1, starting transfers between devices, shards(): lax.all_to_all(column_incoming, 'box', split_axis=1, concat_axis=3, tiled...  14.2 us
    unnamed x1, blocking collectives  13.7 us
    all_to_all x1, starting transfers between devices, shards(): lax.all_to_all(coarse_pattern, 'box', split_axis=3, concat_axis=1, tiled=...  13.4 us
  transfers between devices with their start and end apart: 6, of which 0 were waited for; matrix products, arithmetic and copies ran while one was open for 11% of the time, Pallas kernels for 0%

commit v1 on v0

v1 whole, which is shorter than its diff:
```python
import functools

import jax
import jax.numpy as jnp
from jax import lax
from jax.experimental import pallas as pl
from jax.experimental.pallas import tpu as pltpu
from jax.sharding import PartitionSpec as P

VMEM = pltpu.VMEM
SMEM = pltpu.SMEM
PARAMS = pltpu.CompilerParams(vmem_limit_bytes=16 * 1024 * 1024)


def spec(space):
    return pl.BlockSpec(memory_space=space)


def swap_cores(x):
    n = lax.axis_size("box")
    return lax.ppermute(x, "box", [(i, i ^ 1) for i in range(n)])


def swap_chips(x):
    n = lax.axis_size("box")
    pairs = [(i, i + 1) for i in range(1, n - 1, 2)]
    return lax.ppermute(x, "box", pairs + [(j, i) for i, j in pairs])


def from_chips(x, distance):
    n = lax.axis_size("box")
    pairs = []
    for i in range(n):
        j = i - 2 * distance if i % 2 == 0 else i + 2 * distance
        if 0 <= j < n:
            pairs.append((j, i))
    return lax.ppermute(x, "box", pairs)


def rim_kernel(pattern_ref, first_ref, last_ref):
    for x in range(2):
        for row in range(2):
            first_ref[x, row] = pattern_ref[x, pl.ds(row, 24, stride=8), :]
            last_ref[x, row] = pattern_ref[x, pl.ds(6 + row, 24, stride=8), :]


def rims(pattern):
    shape = jax.ShapeDtypeStruct((2, 2, 24, 128), jnp.float32)
    return pl.pallas_call(
        rim_kernel,
        out_shape=(shape, shape),
        in_specs=[spec(VMEM)],
        out_specs=(spec(VMEM), spec(VMEM)),
        compiler_params=PARAMS,
    )(pattern.reshape(2, 192, 128))


def aggregate_kernel(pattern_ref, before_ref, after_ref, start_ref, weight_ref, phi_ref, cos_ref, sin_ref, out_ref):
    start = jnp.concatenate([start_ref[...]] * 8, axis=0)
    weight = jnp.concatenate([weight_ref[...]] * 8, axis=0)
    line = lax.broadcasted_iota(jnp.int32, (128, 96), 0)
    column = lax.broadcasted_iota(jnp.int32, (128, 96), 1)
    own = column < 64
    rim = (column - 64) // 8
    row = jnp.where(own, column % 8, jnp.where(rim < 2, rim - 2, rim + 6))
    child = jnp.where(own, column // 8, column % 8)
    row = jnp.where(child == line // 16, row, -100)
    theta = jnp.zeros((128, 96), jnp.float32)
    for q in range(4):
        theta = theta + jnp.where(start + q == row, weight[:, q : q + 1], 0.0)
    phi = phi_ref[...]
    for k in range(3):
        wide = []
        for x in range(2):
            parts = [pattern_ref[x, 64 * k : 64 * k + 64]]
            for rim_ref in (before_ref, after_ref):
                parts += [rim_ref[x, r, 8 * k : 8 * k + 8] for r in range(2)]
            source = jnp.concatenate(parts, axis=0)
            narrow = jnp.dot(
                theta, source, precision=lax.Precision.HIGHEST, preferred_element_type=jnp.float32
            )
            wide.append(
                lax.dot_general(
                    narrow,
                    phi,
                    (((1,), (1,)), ((), ())),
                    precision=lax.Precision.HIGHEST,
                    preferred_element_type=jnp.float32,
                )
            )
        cosine, sine = cos_ref[...], sin_ref[...]
        real_part = (cosine * wide[0] - sine * wide[1]).reshape(8, 16, 256)
        imag_part = (cosine * wide[1] + sine * wide[0]).reshape(8, 16, 256)
        out_ref[0, k] = jnp.sum(real_part, axis=0)
        out_ref[1, k] = jnp.sum(imag_part, axis=0)


def aggregate(pattern, before, after, start, weight, phi, phase):
    phase = phase.reshape(128, 256)
    return pl.pallas_call(
        aggregate_kernel,
        out_shape=jax.ShapeDtypeStruct((2, 3, 16, 256), jnp.float32),
        in_specs=[spec(VMEM)] * 8,
        out_specs=spec(VMEM),
        compiler_params=PARAMS,
    )(pattern.reshape(2, 192, 128), before, after, start, weight, phi, jnp.cos(phase), jnp.sin(phase))


def pairs_sum(window, table, partner_ref, offset_ref, count, b, base):
    sums = None
    for j in range(16):
        place = partner_ref[b, j] - base
        which = jnp.where(j < count, offset_ref[b, j], 16)
        a, c = table[0, which], table[1, which]
        f, g = window[0, place], window[1, place]
        terms = (a * f, c * g, a * g, c * f)
        sums = terms if sums is None else tuple(s + t for s, t in zip(sums, terms))
    return sums[0] - sums[1], sums[2] + sums[3]


def fine_kernel(partner_ref, offset_ref, count_ref, own, inner, outer, table, out_ref, window, operators, sems):
    me = lax.axis_index("box")
    odd = lax.rem(me, 2)
    copies = [
        pltpu.make_async_copy(own, window.at[:, pl.ds(24, 24)], sems.at[0]),
        pltpu.make_async_copy(inner, window.at[:, pl.ds(48 * (1 - odd), 24)], sems.at[1]),
        pltpu.make_async_copy(outer, window.at[:, pl.ds(48 * odd, 24)], sems.at[2]),
        pltpu.make_async_copy(table, operators.at[:, pl.ds(0, 16)], sems.at[3]),
    ]
    for copy in copies:
        copy.start()
    operators[:, 16] = jnp.zeros((2, 8, 128), jnp.float32)
    for copy in copies:
        copy.wait()
    base = (me - 1) * 24

    def step(b, carry):
        real_part, imag_part = pairs_sum(window, operators, partner_ref, offset_ref, count_ref[b], b, base)
        out_ref[0, b] = real_part
        out_ref[1, b] = imag_part
        return carry

    lax.fori_loop(0, 24, step, 0)


def fine_translate(pattern, inner, outer, table, partner, offset, count):
    return pl.pallas_call(
        fine_kernel,
        out_shape=jax.ShapeDtypeStruct((2, 24, 8, 128), jnp.float32),
        in_specs=[spec(SMEM)] * 3 + [spec(pl.ANY)] * 4,
        out_specs=spec(VMEM),
        scratch_shapes=[
            pltpu.VMEM((2, 72, 8, 128), jnp.float32),
            pltpu.VMEM((2, 17, 8, 128), jnp.float32),
            pltpu.SemaphoreType.DMA((4,)),
        ],
        compiler_params=PARAMS,
        cost_estimate=pl.CostEstimate(flops=4_000_000, bytes_accessed=4_000_000, transcendentals=0),
    )(partner, offset, count, pattern, inner, outer, table)


def coarse_kernel(partner_ref, offset_ref, count_ref, pair, near, other, table, out_ref, window, operators, sems):
    me = lax.axis_index("box")
    odd = lax.rem(me, 2)

    def slot(block):
        return window.at[:, pl.ds(3 * block, 3)]

    def part(ref, block):
        return ref.at[:, pl.ds(3 * block, 3)]

    copies = [
        pltpu.make_async_copy(part(pair, 0), slot(4 + odd), sems.at[0]),
        pltpu.make_async_copy(part(pair, 1), slot(5 - odd), sems.at[1]),
        pltpu.make_async_copy(table, operators.at[:, pl.ds(0, 16)], sems.at[2]),
    ]
    for p in range(4):
        copies.append(pltpu.make_async_copy(part(near, p), slot(p + odd * (9 - 2 * p)), sems.at[3 + p]))
        copies.append(pltpu.make_async_copy(part(other, p), slot(9 - p - odd * (9 - 2 * p)), sems.at[7 + p]))
    for copy in copies:
        copy.start()
    operators[:, 16] = jnp.zeros((2, 16, 256), jnp.float32)
    for copy in copies:
        copy.wait()
    base = (me // 2 - 2) * 6

    def step(b, carry):
        real_part, imag_part = pairs_sum(window, operators, partner_ref, offset_ref, count_ref[b], b, base)
        out_ref[0, b] = real_part
        out_ref[1, b] = imag_part
        return carry

    lax.fori_loop(0, 3, step, 0)


def coarse_translate(pair, near, other, table, partner, offset, count):
    return pl.pallas_call(
        coarse_kernel,
        out_shape=jax.ShapeDtypeStruct((2, 3, 16, 256), jnp.float32),
        in_specs=[spec(SMEM)] * 3 + [spec(pl.ANY)] * 4,
        out_specs=spec(VMEM),
        scratch_shapes=[
            pltpu.VMEM((2, 30, 16, 256), jnp.float32),
            pltpu.VMEM((2, 17, 16, 256), jnp.float32),
            pltpu.SemaphoreType.DMA((11,)),
        ],
        compiler_params=PARAMS,
    )(partner, offset, count, pair, near, other, table)


def shards(
    fine_pattern,
    fine_partner,
    fine_offset,
    fine_count,
    coarse_partner,
    coarse_offset,
    coarse_count,
    fine_table,
    coarse_table,
    theta_start,
    theta_weight,
    phi_interp,
    shift_phase,
):
    samp = lax.axis_size("samp")
    first, last = rims(fine_pattern)
    up = [(i, i + 1) for i in range(samp - 1)]
    before = lax.ppermute(last, "samp", up)
    after = lax.ppermute(first, "samp", [(j, i) for i, j in up])
    outer = swap_chips(fine_pattern)
    inner = swap_cores(fine_pattern)
    start = (theta_start - lax.axis_index("samp") * 8)[:, None]
    coarse = aggregate(fine_pattern, before, after, start, theta_weight, phi_interp, shift_phase)
    pair = jnp.concatenate([coarse, swap_cores(coarse)], axis=1)
    near = jnp.concatenate([from_chips(pair, 2), from_chips(pair, 1)], axis=1)
    other = swap_cores(near)
    fine_incoming = fine_translate(
        fine_pattern, inner, outer, fine_table, fine_partner, fine_offset, fine_count
    )
    coarse_incoming = coarse_translate(
        pair, near, other, coarse_table, coarse_partner, coarse_offset, coarse_count
    )
    return (fine_incoming, coarse_incoming)


def solution(mesh):
    return jax.shard_map(
        shards,
        mesh=mesh,
        in_specs=(
            P(None, "box", "samp", None),
            P("box", None),
            P("box", None),
            P("box"),
            P("box", None),
            P("box", None),
            P("box"),
            P(None, None, "samp", None),
            P(None, None, "samp", None),
            P("samp"),
            P("samp", None),
            P(),
            P(None, "samp", None),
        ),
        out_specs=(P(None, "box", "samp", None), P(None, "box", "samp", None)),
        check_vma=False,
    )
```

time: 265 us -> 53.7 us (0.20)
  the two profiles are of different devices: /device:TPU:205 before, /device:TPU:198 now
where the time goes in v1:
time: 53.7 us; the launch traced here: 53.3 us
  starting transfers between devices  26 us (48%)
  waiting for transfers between devices  16.1 us (30%)
  Pallas kernels  7.26 us (14%)
  local copies, waits for them, and re-layouts  3.02 us (6%)
  between operations  0.87 us (2%)
    ppermute x2, starting transfers between devices, from_chips(): return lax.ppermute(x, 'box', pairs)  7.98 us
    ppermute x2, waiting for transfers between devices, from_chips(): return lax.ppermute(x, 'box', pairs)  6.75 us
    ppermute x3, starting transfers between devices, swap_cores(): return lax.ppermute(x, 'box', [(i, i ^ 1) for i in range(n)])  6.38 us
    ppermute x1, starting transfers between devices, shards(): before = lax.ppermute(last, 'samp', up)  5.62 us
    ppermute x1, waiting for transfers between devices, swap_chips(): return lax.ppermute(x, 'box', pairs + [(j, i) for i, j in pairs])  4.78 us
    ppermute x1, starting transfers between devices, swap_chips(): return lax.ppermute(x, 'box', pairs + [(j, i) for i, j in pairs])  4.13 us
    pallas_call x1, Pallas kernels, fine_translate(): pl.pallas_call(fine_kernel, out_shape=jax.ShapeDtypeStruct((2, 24, 8, 128...  3.33 us
    ppermute x1, waiting for transfers between devices, shards(): after = lax.ppermute(first, 'samp', [(j, i) for i, j in up])  3.33 us
  transfers between devices with their start and end apart: 8, of which 5 were waited for; matrix products, arithmetic and copies ran while one was open for 1% of the time, Pallas kernels for 6%

profile of v1, /device:TPU:198, one launch (start us, length us, event | category | flops | bytes accessed | tf_op | source)
XLA Modules:
  0.0 53.3 jit_solution(15209190380711211367)
XLA Ops:
  0.6 0.0 copy-start
  0.6 0.9 %copy-done = f32[2,24,8,128]{3,2,1,0:T(8,128)S(1)} copy-done((f32[2,24,8,128]{3,2,1,0:T(8,128)S(1)}, f32[2,24,8,128]{3,2,1,0:T(8,128)}, u32[]{:S(2)}) %copy-start) | copy-done | bytes 196632
  1.6 0.0 copy-start.9
  1.6 5.6 %collective-permute-start.2 = (f32[2,2,24,128]{3,2,1,0:T(8,128)S(1)}, f32[2,2,24,128]{3,2,1,0:T(8,128)S(1)}, u32[]{:S(2)}, u32[]{:S(2)}) collective-permute-start(f32[2,2,24,128]{3,2,1,0:T(8,128)S(1)} %get-tuple-element.4), channel_id=1, source_target_pairs={{0,1},{1,2},{2,3},{3,4},{4,5},{5,6},{6,7},{8,9},{9,10},{10,11},{11... | collective-permute-start | bytes 147464 | tf_op jit(solution)/shard_map/ppermute | solution.py:229
  7.2 1.9 %collective-permute-start.3 = (f32[2,2,24,128]{3,2,1,0:T(8,128)S(1)}, f32[2,2,24,128]{3,2,1,0:T(8,128)S(1)}, u32[]{:S(2)}, u32[]{:S(2)}) collective-permute-start(f32[2,2,24,128]{3,2,1,0:T(8,128)S(1)} %get-tuple-element.5), channel_id=1, source_target_pairs={{1,0},{2,1},{3,2},{4,3},{5,4},{6,5},{7,6},{9,8},{10,9},{11,10},{12... | collective-permute-start | bytes 147464 | tf_op jit(solution)/shard_map/ppermute | solution.py:230
  9.1 0.0 copy-done.9
  9.2 0.0 copy-start.1
  9.2 0.0 copy-start.3
  9.2 0.5 fusion
  9.7 0.0 copy-start.13
  9.7 0.6 %copy-done.13 = s32[16]{0:T(128)S(1)} copy-done((s32[16]{0:T(128)S(1)}, s32[16]{0:T(128)}, u32[]{:S(2)}) %copy-start.13) | copy-done | bytes 88
  10.3 0.0 copy-start.12
  10.3 0.1 copy.17.start_ref
  10.4 0.6 %copy-done.12 = f32[16,4]{0,1:T(4,128)S(1)} copy-done((f32[16,4]{0,1:T(4,128)S(1)}, f32[16,4]{0,1:T(4,128)}, u32[]{:S(2)}) %copy-start.12) | copy-done | bytes 280
  11.0 0.1 copy.18.weight_ref
  11.1 0.0 collective-permute-done.2.before_ref
  11.1 3.3 %collective-permute-done.3.after_ref = f32[2,2,24,128]{3,2,1,0:T(8,128)S(1)} collective-permute-done((f32[2,2,24,128]{3,2,1,0:T(8,128)S(1)}, f32[2,2,24,128]{3,2,1,0:T(8,128)S(1)}, u32[]{:S(2)}, u32[]{:S(2)}) %collective-permute-start.3) | collective-permute-done | bytes 49184 | tf_op jit(solution)/shard_map/ppermute | solution.py:230
  14.4 0.0 copy-done.1
  14.4 0.0 copy-done.3
  14.4 1.5 %shard_map.142 = f32[2,3,16,256]{3,2,1,0:T(8,128)S(1)} custom-call(f32[2,192,128]{2,1,0:T(8,128)S(1)} %bitcast.6, f32[2,2,24,128]{3,2,1,0:T(8,128)S(1)} %collective-permute-done.2.before_ref, f32[2,2,24,128]{3,2,1,0:T(8,128)S(1)} %collective-permute-done.3.after_ref, s32[16,1]{1,0:T(8,128)S(1)} %copy.17.start_ref, f32[16,4]{1,0:T(8,128)S(1)} %copy.18.weight_ref, ...), custom_call_target="tpu_custom_call" | custom-call | tf_op jit(solution)/shard_map/pallas_call | solution.py:100
  16.0 1.9 %collective-permute-start.4 = (f32[2,3,16,256]{3,2,1,0:T(8,128)S(1)}, f32[2,3,16,256]{3,2,1,0:T(8,128)S(1)}, u32[]{:S(2)}, u32[]{:S(2)}) collective-permute-start(f32[2,3,16,256]{3,2,1,0:T(8,128)S(1)} %shard_map.142), channel_id=1, source_target_pairs={{0,8},{8,0},{16,24},{24,16},{32,40},{40,32},{48,56},{56,48},{64,72... | collective-permute-start | bytes 294920 | tf_op jit(solution)/shard_map/ppermute | solution.py:21
  17.9 1.3 %collective-permute-done.4 = f32[2,3,16,256]{3,2,1,0:T(8,128)S(1)} collective-permute-done((f32[2,3,16,256]{3,2,1,0:T(8,128)S(1)}, f32[2,3,16,256]{3,2,1,0:T(8,128)S(1)}, u32[]{:S(2)}, u32[]{:S(2)}) %collective-permute-start.4) | collective-permute-done | bytes 98336 | tf_op jit(solution)/shard_map/ppermute | solution.py:21
  19.2 4.5 %collective-permute-start.5 = (f32[2,6,16,256]{3,2,1,0:T(8,128)S(1)}, f32[2,6,16,256]{3,2,1,0:T(8,128)S(1)}, u32[]{:S(2)}, u32[]{:S(2)}) collective-permute-start(f32[2,6,16,256]{3,2,1,0:T(8,128)S(1)} %pad_maximum_fusion.pair), channel_id=1, source_target_pairs={{40,8},{56,24},{0,32},{72,40},{16,48},{88,56},{32,64},{104,72},{48... | collective-permute-start | bytes 589832 | tf_op jit(solution)/shard_map/ppermute | solution.py:37
  23.7 3.5 %collective-permute-start.6 = (f32[2,6,16,256]{3,2,1,0:T(8,128)S(1)}, f32[2,6,16,256]{3,2,1,0:T(8,128)S(1)}, u32[]{:S(2)}, u32[]{:S(2)}) collective-permute-start(f32[2,6,16,256]{3,2,1,0:T(8,128)S(1)} %pad_maximum_fusion.pair), channel_id=1, source_target_pairs={{24,8},{0,16},{40,24},{16,32},{56,40},{32,48},{72,56},{48,64},{88,... | collective-permute-start | bytes 589832 | tf_op jit(solution)/shard_map/ppermute | solution.py:37
  27.2 3.5 %collective-permute-done.5 = f32[2,6,16,256]{3,2,1,0:T(8,128)S(1)} collective-permute-done((f32[2,6,16,256]{3,2,1,0:T(8,128)S(1)}, f32[2,6,16,256]{3,2,1,0:T(8,128)S(1)}, u32[]{:S(2)}, u32[]{:S(2)}) %collective-permute-start.5) | collective-permute-done | bytes 196640 | tf_op jit(solution)/shard_map/ppermute | solution.py:37
  30.7 0.0 copy-start.10
  30.7 0.0 copy-start.4
  30.7 3.3 %collective-permute-done.6 = f32[2,6,16,256]{3,2,1,0:T(8,128)S(1)} collective-permute-done((f32[2,6,16,256]{3,2,1,0:T(8,128)S(1)}, f32[2,6,16,256]{3,2,1,0:T(8,128)S(1)}, u32[]{:S(2)}, u32[]{:S(2)}) %collective-permute-start.6) | collective-permute-done | bytes 196640 | tf_op jit(solution)/shard_map/ppermute | solution.py:37
  34.0 0.0 copy-start.11
  34.0 0.0 copy-start.2
  34.0 2.1 %collective-permute-start.7 = (f32[2,12,16,256]{3,2,1,0:T(8,128)S(1)}, f32[2,12,16,256]{3,2,1,0:T(8,128)S(1)}, u32[]{:S(2)}, u32[]{:S(2)}) collective-permute-start(f32[2,12,16,256]{3,2,1,0:T(8,128)S(1)} %constant_dynamic-update-slice_fusion.near), channel_id=1, source_target_pairs={{0,8},{8,0},{16,24},{24,16},{32,40},{40,32},{48,56},{56,48},{64,72... | collective-permute-start | bytes 1179656 | tf_op jit(solution)/shard_map/ppermute | solution.py:21
  36.1 2.4 %collective-permute-start = (f32[2,24,8,128]{3,2,1,0:T(8,128)S(1)}, f32[2,24,8,128]{3,2,1,0:T(8,128)S(1)}, u32[]{:S(2)}, u32[]{:S(2)}) collective-permute-start(f32[2,24,8,128]{3,2,1,0:T(8,128)S(1)} %copy-done.1), channel_id=1, source_target_pairs={{0,8},{8,0},{16,24},{24,16},{32,40},{40,32},{48,56},{56,48},{64,72... | collective-permute-start | bytes 589832 | tf_op jit(solution)/shard_map/ppermute | solution.py:21
  38.5 4.1 %collective-permute-start.1 = (f32[2,24,8,128]{3,2,1,0:T(8,128)S(1)}, f32[2,24,8,128]{3,2,1,0:T(8,128)S(1)}, u32[]{:S(2)}, u32[]{:S(2)}) collective-permute-start(f32[2,24,8,128]{3,2,1,0:T(8,128)S(1)} %copy-done.1), channel_id=1, source_target_pairs={{8,16},{24,32},{40,48},{56,64},{72,80},{88,96},{104,112},{120,128}... | collective-permute-start | bytes 589832 | tf_op jit(solution)/shard_map/ppermute | solution.py:27
  42.6 0.0 copy-done.10
  42.6 0.1 copy.15.partner_ref
  42.7 0.0 copy-done.11
  42.7 0.1 copy.16.offset_ref
  42.8 0.0 collective-permute-done.inner
  42.8 4.8 %collective-permute-done.1.outer = f32[2,24,8,128]{3,2,1,0:T(8,128)S(1)} collective-permute-done((f32[2,24,8,128]{3,2,1,0:T(8,128)S(1)}, f32[2,24,8,128]{3,2,1,0:T(8,128)S(1)}, u32[]{:S(2)}, u32[]{:S(2)}) %collective-permute-start.1) | collective-permute-done | bytes 196640 | tf_op jit(solution)/shard_map/ppermute | solution.py:27
  47.6 0.0 copy-done.4
  47.6 0.0 copy-done.7
  47.6 3.3 %shard_map.140 = f32[2,24,8,128]{3,2,1,0:T(8,128)} custom-call(s32[24,16]{1,0:T(8,128)S(1)} %copy.15.partner_ref, s32[24,16]{1,0:T(8,128)S(1)} %copy.16.offset_ref, s32[24]{0:T(128)S(1)} %copy-done.7, f32[2,24,8,128]{3,2,1,0:T(8,128)S(1)} %copy-done.1, f32[2,24,8,128]{3,2,1,0:T(8,128)S(1)} %collective-permute-done.inner, ...), custom_call_target="tpu_custom_call" | custom-call | flops 4000000 | bytes 4000000 | tf_op jit(solution)/shard_map/pallas_call | solution.py:147
  50.9 0.0 collective-permute-done.7.other
  50.9 0.0 copy-done.2
  50.9 0.0 copy-done.5
  51.0 0.0 copy-done.6
  51.0 0.0 copy-done.8
  51.0 2.4 %shard_map.143 = f32[2,3,16,256]{3,2,1,0:T(8,128)} custom-call(s32[3,16]{1,0:T(4,128)S(1)} %copy-done.5, s32[3,16]{1,0:T(4,128)S(1)} %copy-done.6, s32[3]{0:T(128)S(1)} %copy-done.8, f32[2,6,16,256]{3,2,1,0:T(8,128)S(1)} %pad_maximum_fusion.pair, f32[2,12,16,256]{3,2,1,0:T(8,128)S(1)} %constant_dynamic-update-slice_fusion.near, ...), custom_call_target="tpu_custom_call" | custom-call | tf_op jit(solution)/shard_map/pallas_call | solution.py:197
  (9 shorter events, 0.1 us)
Async XLA Ops:
  0.6 0.9 %copy-start = (f32[2,24,8,128]{3,2,1,0:T(8,128)S(1)}, f32[2,24,8,128]{3,2,1,0:T(8,128)}, u32[]{:S(2)}) copy-start(f32[2,24,8,128]{3,2,1,0:T(8,128)} %own.1) | copy-start | bytes 589828
  1.6 7.6 %copy-start.9 = (f32[8,16,256]{2,1,0:T(8,128)S(1)}, f32[8,16,256]{2,1,0:T(8,128)}, u32[]{:S(2)}) copy-start(f32[8,16,256]{2,1,0:T(8,128)} %param.25) | copy-start | bytes 393220
  1.6 9.5 %collective-permute-start.2 = (f32[2,2,24,128]{3,2,1,0:T(8,128)S(1)}, f32[2,2,24,128]{3,2,1,0:T(8,128)S(1)}, u32[]{:S(2)}, u32[]{:S(2)}) collective-permute-start(f32[2,2,24,128]{3,2,1,0:T(8,128)S(1)} %get-tuple-element.4), channel_id=1, source_target_pairs={{0,1},{1,2},{2,3},{3,4},{4,5},{5,6},{6,7},{8,9},{9,10},{10,11},{11... | collective-permute-start | bytes 147464 | tf_op jit(solution)/shard_map/ppermute | solution.py:229
  7.2 7.2 %collective-permute-start.3 = (f32[2,2,24,128]{3,2,1,0:T(8,128)S(1)}, f32[2,2,24,128]{3,2,1,0:T(8,128)S(1)}, u32[]{:S(2)}, u32[]{:S(2)}) collective-permute-start(f32[2,2,24,128]{3,2,1,0:T(8,128)S(1)} %get-tuple-element.5), channel_id=1, source_target_pairs={{1,0},{2,1},{3,2},{4,3},{5,4},{6,5},{7,6},{9,8},{10,9},{11,10},{12... | collective-permute-start | bytes 147464 | tf_op jit(solution)/shard_map/ppermute | solution.py:230
  9.2 5.3 %copy-start.1 = (f32[2,24,8,128]{3,2,1,0:T(8,128)S(1)}, f32[2,24,8,128]{3,2,1,0:T(8,128)}, u32[]{:S(2)}) copy-start(f32[2,24,8,128]{3,2,1,0:T(8,128)} %own.1) | copy-start | bytes 589828
  9.2 5.2 %copy-start.3 = (f32[256,128]{1,0:T(8,128)S(1)}, f32[256,128]{1,0:T(8,128)}, u32[]{:S(2)}) copy-start(f32[256,128]{1,0:T(8,128)} %phi_ref.1) | copy-start | bytes 393220
  9.7 0.7 %copy-start.13 = (s32[16]{0:T(128)S(1)}, s32[16]{0:T(128)}, u32[]{:S(2)}) copy-start(s32[16]{0:T(128)} %param.22) | copy-start | bytes 196
  10.3 0.7 %copy-start.12 = (f32[16,4]{0,1:T(4,128)S(1)}, f32[16,4]{0,1:T(4,128)}, u32[]{:S(2)}) copy-start(f32[16,4]{0,1:T(4,128)} %param.23) | copy-start | bytes 772
  16.0 3.2 %collective-permute-start.4 = (f32[2,3,16,256]{3,2,1,0:T(8,128)S(1)}, f32[2,3,16,256]{3,2,1,0:T(8,128)S(1)}, u32[]{:S(2)}, u32[]{:S(2)}) collective-permute-start(f32[2,3,16,256]{3,2,1,0:T(8,128)S(1)} %shard_map.142), channel_id=1, source_target_pairs={{0,8},{8,0},{16,24},{24,16},{32,40},{40,32},{48,56},{56,48},{64,72... | collective-permute-start | bytes 294920 | tf_op jit(solution)/shard_map/ppermute | solution.py:21
  19.2 11.5 %collective-permute-start.5 = (f32[2,6,16,256]{3,2,1,0:T(8,128)S(1)}, f32[2,6,16,256]{3,2,1,0:T(8,128)S(1)}, u32[]{:S(2)}, u32[]{:S(2)}) collective-permute-start(f32[2,6,16,256]{3,2,1,0:T(8,128)S(1)} %pad_maximum_fusion.pair), channel_id=1, source_target_pairs={{40,8},{56,24},{0,32},{72,40},{16,48},{88,56},{32,64},{104,72},{48... | collective-permute-start | bytes 589832 | tf_op jit(solution)/shard_map/ppermute | solution.py:37
  23.7 10.3 %collective-permute-start.6 = (f32[2,6,16,256]{3,2,1,0:T(8,128)S(1)}, f32[2,6,16,256]{3,2,1,0:T(8,128)S(1)}, u32[]{:S(2)}, u32[]{:S(2)}) collective-permute-start(f32[2,6,16,256]{3,2,1,0:T(8,128)S(1)} %pad_maximum_fusion.pair), channel_id=1, source_target_pairs={{24,8},{0,16},{40,24},{16,32},{56,40},{32,48},{72,56},{48,64},{88,... | collective-permute-start | bytes 589832 | tf_op jit(solution)/shard_map/ppermute | solution.py:37
  30.7 12.0 %copy-start.10 = (s32[24,16]{0,1:T(8,128)S(1)}, s32[24,16]{0,1:T(8,128)}, u32[]{:S(2)}) copy-start(s32[24,16]{0,1:T(8,128)} %param.14) | copy-start | bytes 4612
  30.7 16.9 %copy-start.4 = (f32[2,16,8,128]{3,2,1,0:T(8,128)S(1)}, f32[2,16,8,128]{3,2,1,0:T(8,128)}, u32[]{:S(2)}) copy-start(f32[2,16,8,128]{3,2,1,0:T(8,128)} %table.2) | copy-start | bytes 393220
  34.0 8.7 %copy-start.11 = (s32[24,16]{0,1:T(8,128)S(1)}, s32[24,16]{0,1:T(8,128)}, u32[]{:S(2)}) copy-start(s32[24,16]{0,1:T(8,128)} %param.15) | copy-start | bytes 4612
  34.0 13.6 %copy-start.7 = (s32[24]{0:T(128)S(1)}, s32[24]{0:T(128)}, u32[]{:S(2)}) copy-start(s32[24]{0:T(128)} %count_ref.2) | copy-start | bytes 292
  34.0 16.9 %copy-start.2 = (f32[2,16,16,256]{3,2,1,0:T(8,128)S(1)}, f32[2,16,16,256]{3,2,1,0:T(8,128)}, u32[]{:S(2)}) copy-start(f32[2,16,16,256]{3,2,1,0:T(8,128)} %table.3) | copy-start | bytes 1572868
  34.0 16.9 %collective-permute-start.7 = (f32[2,12,16,256]{3,2,1,0:T(8,128)S(1)}, f32[2,12,16,256]{3,2,1,0:T(8,128)S(1)}, u32[]{:S(2)}, u32[]{:S(2)}) collective-permute-start(f32[2,12,16,256]{3,2,1,0:T(8,128)S(1)} %constant_dynamic-update-slice_fusion.near), channel_id=1, source_target_pairs={{0,8},{8,0},{16,24},{24,16},{32,40},{40,32},{48,56},{56,48},{64,72... | collective-permute-start | bytes 1179656 | tf_op jit(solution)/shard_map/ppermute | solution.py:21
  36.1 6.7 %collective-permute-start = (f32[2,24,8,128]{3,2,1,0:T(8,128)S(1)}, f32[2,24,8,128]{3,2,1,0:T(8,128)S(1)}, u32[]{:S(2)}, u32[]{:S(2)}) collective-permute-start(f32[2,24,8,128]{3,2,1,0:T(8,128)S(1)} %copy-done.1), channel_id=1, source_target_pairs={{0,8},{8,0},{16,24},{24,16},{32,40},{40,32},{48,56},{56,48},{64,72... | collective-permute-start | bytes 589832 | tf_op jit(solution)/shard_map/ppermute | solution.py:21
  38.5 9.1 %collective-permute-start.1 = (f32[2,24,8,128]{3,2,1,0:T(8,128)S(1)}, f32[2,24,8,128]{3,2,1,0:T(8,128)S(1)}, u32[]{:S(2)}, u32[]{:S(2)}) collective-permute-start(f32[2,24,8,128]{3,2,1,0:T(8,128)S(1)} %copy-done.1), channel_id=1, source_target_pairs={{8,16},{24,32},{40,48},{56,64},{72,80},{88,96},{104,112},{120,128}... | collective-permute-start | bytes 589832 | tf_op jit(solution)/shard_map/ppermute | solution.py:27
  42.8 8.2 %copy-start.5 = (s32[3,16]{1,0:T(4,128)S(1)}, s32[3,16]{1,0:T(4,128)}, u32[]{:S(2)}) copy-start(s32[3,16]{1,0:T(4,128)} %partner_ref.2) | copy-start | bytes 580
  42.8 8.2 %copy-start.6 = (s32[3,16]{1,0:T(4,128)S(1)}, s32[3,16]{1,0:T(4,128)}, u32[]{:S(2)}) copy-start(s32[3,16]{1,0:T(4,128)} %offset_ref.2) | copy-start | bytes 580
  42.8 8.2 %copy-start.8 = (s32[3]{0:T(128)S(1)}, s32[3]{0:T(128)}, u32[]{:S(2)}) copy-start(s32[3]{0:T(128)} %count_ref.3) | copy-start | bytes 40

commit v2 on v1

v2 whole, which is shorter than its diff:
```python
import functools

import jax
import jax.numpy as jnp
from jax import lax
from jax.experimental import pallas as pl
from jax.experimental.pallas import tpu as pltpu
from jax.sharding import PartitionSpec as P

VMEM = pltpu.VMEM
SMEM = pltpu.SMEM
PARAMS = pltpu.CompilerParams(vmem_limit_bytes=16 * 1024 * 1024)


def spec(space):
    return pl.BlockSpec(memory_space=space)


def matched(x, axis, pairs):
    return lax.ppermute(x, axis, pairs + [(j, i) for i, j in pairs])


def swap_cores(x):
    n = lax.axis_size("box")
    return matched(x, "box", [(i, i + 1) for i in range(0, n, 2)])


def swap_chips(x, core, distance):
    n = lax.axis_size("box")
    pairs = [(i + core, i + 2 * distance + 1 - core) for i in range(0, n - 2 * distance, 2)]
    return matched(x, "box", pairs)


def swap_rims(x, start):
    n = lax.axis_size("samp")
    return matched(x, "samp", [(i, i + 1) for i in range(start, n - 1, 2)])


def rim_kernel(pattern_ref, even_ref, odd_ref):
    odd = lax.rem(lax.axis_index("samp"), 2) == 1
    for x in range(2):
        for row in range(2):
            first = pattern_ref[x, pl.ds(row, 24, stride=8), :]
            last = pattern_ref[x, pl.ds(6 + row, 24, stride=8), :]
            even_ref[x, row] = jnp.where(odd, first, last)
            odd_ref[x, row] = jnp.where(odd, last, first)


def rims(pattern):
    shape = jax.ShapeDtypeStruct((2, 2, 24, 128), jnp.float32)
    return pl.pallas_call(
        rim_kernel,
        out_shape=(shape, shape),
        in_specs=[spec(VMEM)],
        out_specs=(spec(VMEM), spec(VMEM)),
        compiler_params=PARAMS,
    )(pattern)


def aggregate_kernel(pattern_ref, even_ref, odd_ref, start_ref, weight_ref, phi_ref, cos_ref, sin_ref, out_ref, both_ref):
    start = jnp.concatenate([start_ref[...]] * 8, axis=0)
    weight = jnp.concatenate([weight_ref[...]] * 8, axis=0)
    line = lax.broadcasted_iota(jnp.int32, (128, 96), 0)
    column = lax.broadcasted_iota(jnp.int32, (128, 96), 1)
    own = column < 64
    rim = (column - 64) // 8
    odd = lax.rem(lax.axis_index("samp"), 2) == 1
    rim = jnp.where((rim < 2) == odd, rim % 2 - 2, rim % 2 + 8)
    row = jnp.where(own, column % 8, rim)
    child = jnp.where(own, column // 8, column % 8)
    row = jnp.where(child == line // 16, row, -100)
    theta = jnp.zeros((128, 96), jnp.float32)
    for q in range(4):
        theta = theta + jnp.where(start + q == row, weight[:, q : q + 1], 0.0)
    phi = phi_ref[...]
    both_ref[:, 96:] = pattern_ref[...]
    for k in range(3):
        wide = []
        for x in range(2):
            parts = [pattern_ref[x, 64 * k : 64 * k + 64]]
            for rim_ref in (even_ref, odd_ref):
                parts += [rim_ref[x, r, 8 * k : 8 * k + 8] for r in range(2)]
            source = jnp.concatenate(parts, axis=0)
            narrow = jnp.dot(
                theta, source, precision=lax.Precision.HIGHEST, preferred_element_type=jnp.float32
            )
            wide.append(
                lax.dot_general(
                    narrow,
                    phi,
                    (((1,), (1,)), ((), ())),
                    precision=lax.Precision.HIGHEST,
                    preferred_element_type=jnp.float32,
                )
            )
        cosine, sine = cos_ref[...], sin_ref[...]
        real_part = (cosine * wide[0] - sine * wide[1]).reshape(8, 16, 256)
        imag_part = (cosine * wide[1] + sine * wide[0]).reshape(8, 16, 256)
        for x, value in enumerate((real_part, imag_part)):
            value = jnp.sum(value, axis=0)
            for half in range(2):
                rows = pl.ds(32 * k + 16 * half, 16)
                out_ref[x, rows] = value[:, 128 * half : 128 * half + 128]
                both_ref[x, rows] = value[:, 128 * half : 128 * half + 128]


def aggregate(pattern, even, odd, start, weight, phi, phase):
    phase = phase.reshape(128, 256)
    return pl.pallas_call(
        aggregate_kernel,
        out_shape=(
            jax.ShapeDtypeStruct((2, 96, 128), jnp.float32),
            jax.ShapeDtypeStruct((2, 288, 128), jnp.float32),
        ),
        in_specs=[spec(VMEM)] * 8,
        out_specs=(spec(VMEM), spec(VMEM)),
        compiler_params=PARAMS,
    )(pattern, even, odd, start, weight, phi, jnp.cos(phase), jnp.sin(phase))


def pairs_sum(window, table, lines, partner_ref, offset_ref, count, b, base):
    sums = None
    for j in range(16):
        place = pl.multiple_of((partner_ref[b, j] - base) * lines, lines)
        which = pl.multiple_of(jnp.where(j < count, offset_ref[b, j], 16) * lines, lines)
        a, c = table[0, pl.ds(which, lines)], table[1, pl.ds(which, lines)]
        f, g = window[0, pl.ds(place, lines)], window[1, pl.ds(place, lines)]
        terms = (a * f, c * g, a * g, c * f)
        sums = terms if sums is None else tuple(s + t for s, t in zip(sums, terms))
    return sums[0] - sums[1], sums[2] + sums[3]


def fine_kernel(partner_ref, offset_ref, count_ref, own, inner, outer, table, out_ref, window, operators, sems):
    me = lax.axis_index("box")
    odd = lax.rem(me, 2)
    copies = [
        pltpu.make_async_copy(own, window.at[:, pl.ds(192, 192)], sems.at[0]),
        pltpu.make_async_copy(inner, window.at[:, pl.ds(384 * (1 - odd), 192)], sems.at[1]),
        pltpu.make_async_copy(outer.at[:, pl.ds(96, 192)], window.at[:, pl.ds(384 * odd, 192)], sems.at[2]),
        pltpu.make_async_copy(table, operators.at[:, pl.ds(0, 128)], sems.at[3]),
    ]
    for copy in copies:
        copy.start()
    operators[:, 128:] = jnp.zeros((2, 8, 128), jnp.float32)
    for copy in copies:
        copy.wait()
    base = (me - 1) * 24

    def step(b, carry):
        real_part, imag_part = pairs_sum(window, operators, 8, partner_ref, offset_ref, count_ref[b], b, base)
        out_ref[0, b] = real_part
        out_ref[1, b] = imag_part
        return carry

    lax.fori_loop(0, 24, step, 0)


def fine_translate(pattern, inner, outer, table, partner, offset, count):
    return pl.pallas_call(
        fine_kernel,
        out_shape=jax.ShapeDtypeStruct((2, 24, 8, 128), jnp.float32),
        in_specs=[spec(SMEM)] * 3 + [spec(pl.ANY)] * 4,
        out_specs=spec(VMEM),
        scratch_shapes=[
            pltpu.VMEM((2, 576, 128), jnp.float32),
            pltpu.VMEM((2, 136, 128), jnp.float32),
            pltpu.SemaphoreType.DMA((4,)),
        ],
        compiler_params=PARAMS,
        cost_estimate=pl.CostEstimate(flops=4_000_000, bytes_accessed=4_000_000, transcendentals=0),
    )(partner, offset, count, pattern, inner, outer, table.reshape(2, 128, 128))


def coarse_kernel(partner_ref, offset_ref, count_ref, mine, theirs, table, out_ref, window, operators, sems):
    me = lax.axis_index("box")
    odd = lax.rem(me, 2)
    copies = []
    for source, core, first in ((mine, odd, 0), (theirs, 1 - odd, 5)):
        slots = (4 + core, 3 + 3 * core, 7 - 5 * core, 1 + 7 * core, 9 - 9 * core)
        for p, slot in enumerate(slots):
            copies.append(
                pltpu.make_async_copy(
                    source.at[:, pl.ds(96 * p, 96)],
                    window.at[:, pl.ds(pl.multiple_of(96 * slot, 96), 96)],
                    sems.at[first + p],
                )
            )
    for half in range(2):
        copies.append(
            pltpu.make_async_copy(
                table.at[:, :, :, pl.ds(128 * half, 128)],
                operators.at[:, pl.ds(0, 16), pl.ds(16 * half, 16)],
                sems.at[10 + half],
            )
        )
    for copy in copies:
        copy.start()
    operators[:, 16] = jnp.zeros((2, 32, 128), jnp.float32)
    for copy in copies:
        copy.wait()
    base = (me // 2 - 2) * 6
    flat = operators.reshape(2, 17 * 32, 128)

    def step(b, carry):
        parts = pairs_sum(window, flat, 32, partner_ref, offset_ref, count_ref[b], b, base)
        for x in range(2):
            for half in range(2):
                out_ref[x, b, :, 128 * half : 128 * half + 128] = parts[x][16 * half : 16 * half + 16]
        return carry

    lax.fori_loop(0, 3, step, 0)


def coarse_translate(mine, theirs, table, partner, offset, count):
    return pl.pallas_call(
        coarse_kernel,
        out_shape=jax.ShapeDtypeStruct((2, 3, 16, 256), jnp.float32),
        in_specs=[spec(SMEM)] * 3 + [spec(pl.ANY)] * 3,
        out_specs=spec(VMEM),
        scratch_shapes=[
            pltpu.VMEM((2, 960, 128), jnp.float32),
            pltpu.VMEM((2, 17, 32, 128), jnp.float32),
            pltpu.SemaphoreType.DMA((12,)),
        ],
        compiler_params=PARAMS,
    )(partner, offset, count, mine, theirs, table)


def shards(
    fine_pattern,
    fine_partner,
    fine_offset,
    fine_count,
    coarse_partner,
    coarse_offset,
    coarse_count,
    fine_table,
    coarse_table,
    theta_start,
    theta_weight,
    phi_interp,
    shift_phase,
):
    pattern = fine_pattern.reshape(2, 192, 128)
    even, odd = rims(pattern)
    even, odd, pattern = lax.optimization_barrier((even, odd, pattern))
    even, odd = swap_rims(even, 0), swap_rims(odd, 1)
    inner = swap_cores(pattern)
    even, odd, inner = lax.optimization_barrier((even, odd, inner))
    start = (theta_start - lax.axis_index("samp") * 8)[:, None]
    coarse, both = aggregate(pattern, even, odd, start, theta_weight, phi_interp, shift_phase)
    outer = swap_chips(both, 1, 1)
    others = [swap_chips(coarse, 0, 1), swap_chips(coarse, 1, 2), swap_chips(coarse, 0, 2)]
    mine = jnp.concatenate([coarse, outer[:, :96]] + others, axis=1)
    theirs = swap_cores(mine)
    fine_incoming = fine_translate(
        pattern, inner, outer, fine_table, fine_partner, fine_offset, fine_count
    )
    coarse_incoming = coarse_translate(
        mine, theirs, coarse_table, coarse_partner, coarse_offset, coarse_count
    )
    return (fine_incoming, coarse_incoming)


def solution(mesh):
    return jax.shard_map(
        shards,
        mesh=mesh,
        in_specs=(
            P(None, "box", "samp", None),
            P("box", None),
            P("box", None),
            P("box"),
            P("box", None),
            P("box", None),
            P("box"),
            P(None, None, "samp", None),
            P(None, None, "samp", None),
            P("samp"),
            P("samp", None),
            P(),
            P(None, "samp", None),
        ),
        out_specs=(P(None, "box", "samp", None), P(None, "box", "samp", None)),
        check_vma=False,
    )
```

time: 53.7 us -> 48 us (0.89)
  the two profiles are of different devices: /device:TPU:198 before, /device:TPU:197 now
where the time goes in v2:
time: 48 us; the launch traced here: 47.6 us
  starting transfers between devices  27.7 us (58%)
  Pallas kernels  9.58 us (20%)
  waiting for transfers between devices  6.77 us (14%)
  local copies, waits for them, and re-layouts  2.6 us (5%)
  between operations  0.9 us (2%)
    ppermute x8, starting transfers between devices, matched(): return lax.ppermute(x, axis, pairs + [(j, i) for i, j in pairs])  27.7 us
    ppermute x8, waiting for transfers between devices, matched(): return lax.ppermute(x, axis, pairs + [(j, i) for i, j in pairs])  6.77 us
    pallas_call x1, Pallas kernels, fine_translate(): pl.pallas_call(fine_kernel, out_shape=jax.ShapeDtypeStruct((2, 24, 8, 128...  3.74 us
    pallas_call x1, Pallas kernels, aggregate(): pl.pallas_call(aggregate_kernel, out_shape=(jax.ShapeDtypeStruct((2, 96,...  2.49 us
    pallas_call x1, Pallas kernels, coarse_translate(): pl.pallas_call(coarse_kernel, out_shape=jax.ShapeDtypeStruct((2, 3, 16, 2...  2.36 us
    unnamed x31, local copies, waits for them, and re-layouts  2.05 us
    pallas_call x1, Pallas kernels, rims(): pl.pallas_call(rim_kernel, out_shape=(shape, shape), in_specs=[spec(VMEM)...  0.99 us
  transfers between devices with their start and end apart: 8, of which 2 were waited for; matrix products, arithmetic and copies ran while one was open for 2% of the time, Pallas kernels for 8%

profile of v2, /device:TPU:197, one launch (start us, length us, event | category | flops | bytes accessed | tf_op | source)
XLA Modules:
  0.0 47.6 jit_solution(5609732325735239511)
XLA Ops:
  0.6 0.0 copy-start.7
  0.6 1.0 %shard_map.140 = (f32[2,2,24,128]{3,2,1,0:T(8,128)S(1)}, f32[2,2,24,128]{3,2,1,0:T(8,128)S(1)}) custom-call(f32[2,192,128]{2,1,0:T(8,128)} %bitcast.pattern_ref.own), custom_call_target="tpu_custom_call" | custom-call | tf_op jit(solution)/shard_map/pallas_call | solution.py:51
  1.6 1.9 %collective-permute-start = (f32[2,2,24,128]{3,2,1,0:T(8,128)S(1)}, f32[2,2,24,128]{3,2,1,0:T(8,128)S(1)}, u32[]{:S(2)}, u32[]{:S(2)}) collective-permute-start(f32[2,2,24,128]{3,2,1,0:T(8,128)S(1)} %get-tuple-element.15), channel_id=1, source_target_pairs={{0,1},{2,3},{4,5},{6,7},{1,0},{3,2},{5,4},{7,6},{8,9},{10,11},{12,... | collective-permute-start | bytes 147464 | tf_op jit(solution)/shard_map/ppermute | solution.py:20
  3.6 6.4 %collective-permute-start.1 = (f32[2,2,24,128]{3,2,1,0:T(8,128)S(1)}, f32[2,2,24,128]{3,2,1,0:T(8,128)S(1)}, u32[]{:S(2)}, u32[]{:S(2)}) collective-permute-start(f32[2,2,24,128]{3,2,1,0:T(8,128)S(1)} %get-tuple-element.16), channel_id=1, source_target_pairs={{1,2},{3,4},{5,6},{2,1},{4,3},{6,5},{9,10},{11,12},{13,14},{10,9},... | collective-permute-start | bytes 147464 | tf_op jit(solution)/shard_map/ppermute | solution.py:20
  10.0 3.1 %collective-permute-start.2 = (f32[2,192,128]{2,1,0:T(8,128)}, f32[2,192,128]{2,1,0:T(8,128)S(1)}, u32[]{:S(2)}, u32[]{:S(2)}) collective-permute-start(f32[2,192,128]{2,1,0:T(8,128)} %bitcast.pattern_ref.own), channel_id=1, source_target_pairs={{0,8},{16,24},{32,40},{48,56},{64,72},{80,88},{96,104},{112,120},{... | collective-permute-start | bytes 589832 | tf_op jit(solution)/shard_map/ppermute | solution.py:20
  13.1 0.0 copy-done.7
  13.1 0.0 copy-start.1
  13.1 0.5 fusion
  13.6 0.0 copy-start.11
  13.6 0.6 %copy-done.11 = s32[16]{0:T(128)S(1)} copy-done((s32[16]{0:T(128)S(1)}, s32[16]{0:T(128)}, u32[]{:S(2)}) %copy-start.11) | copy-done | bytes 88
  14.3 0.0 copy-start.10
  14.3 0.1 copy.15.start_ref
  14.4 0.6 %copy-done.10 = f32[16,4]{0,1:T(4,128)S(1)} copy-done((f32[16,4]{0,1:T(4,128)S(1)}, f32[16,4]{0,1:T(4,128)}, u32[]{:S(2)}) %copy-start.10) | copy-done | bytes 280
  14.9 0.1 copy.16.weight_ref
  15.0 0.0 collective-permute-done.even_ref
  15.0 0.0 collective-permute-done.1.odd_ref
  15.0 0.0 collective-permute-done.2.inner
  15.0 0.0 copy-done.1
  15.1 2.5 %shard_map.141 = (f32[2,96,128]{2,1,0:T(8,128)S(1)}, f32[2,288,128]{2,1,0:T(8,128)S(1)}) custom-call(f32[2,192,128]{2,1,0:T(8,128)} %bitcast.pattern_ref.own, f32[2,2,24,128]{3,2,1,0:T(8,128)S(1)} %collective-permute-done.even_ref, f32[2,2,24,128]{3,2,1,0:T(8,128)S(1)} %collective-permute-done.1.odd_ref, s32[16,1]{1,0:T(8,128)S(1)} %copy.15.start_ref, ...), custom_call_target="tpu_custom_call" | custom-call | tf_op jit(solution)/shard_map/pallas_call | solution.py:109
  17.6 3.1 %collective-permute-start.3 = (f32[2,288,128]{2,1,0:T(8,128)S(1)}, f32[2,288,128]{2,1,0:T(8,128)S(1)}, u32[]{:S(2)}, u32[]{:S(2)}) collective-permute-start(f32[2,288,128]{2,1,0:T(8,128)S(1)} %get-tuple-element.20), channel_id=1, source_target_pairs={{8,16},{24,32},{40,48},{56,64},{72,80},{88,96},{104,112},{120,128}... | collective-permute-start | bytes 884744 | tf_op jit(solution)/shard_map/ppermute | solution.py:20
  20.7 5.2 %collective-permute-start.4 = (f32[2,96,128]{2,1,0:T(8,128)S(1)}, f32[2,96,128]{2,1,0:T(8,128)S(1)}, u32[]{:S(2)}, u32[]{:S(2)}) collective-permute-start(f32[2,96,128]{2,1,0:T(8,128)S(1)} %get-tuple-element.21), channel_id=1, source_target_pairs={{0,24},{16,40},{32,56},{48,72},{64,88},{80,104},{96,120},{112,136}... | collective-permute-start | bytes 294920 | tf_op jit(solution)/shard_map/ppermute | solution.py:20
  25.9 3.7 %collective-permute-start.5 = (f32[2,96,128]{2,1,0:T(8,128)S(1)}, f32[2,96,128]{2,1,0:T(8,128)S(1)}, u32[]{:S(2)}, u32[]{:S(2)}) collective-permute-start(f32[2,96,128]{2,1,0:T(8,128)S(1)} %get-tuple-element.21), channel_id=1, source_target_pairs={{8,32},{24,48},{40,64},{56,80},{72,96},{88,112},{104,128},{120,144... | collective-permute-start | bytes 294920 | tf_op jit(solution)/shard_map/ppermute | solution.py:20
  29.6 2.3 %collective-permute-start.6 = (f32[2,96,128]{2,1,0:T(8,128)S(1)}, f32[2,96,128]{2,1,0:T(8,128)S(1)}, u32[]{:S(2)}, u32[]{:S(2)}) collective-permute-start(f32[2,96,128]{2,1,0:T(8,128)S(1)} %get-tuple-element.21), channel_id=1, source_target_pairs={{0,40},{16,56},{32,72},{48,88},{64,104},{80,120},{96,136},{112,152... | collective-permute-start | bytes 294920 | tf_op jit(solution)/shard_map/ppermute | solution.py:20
  31.9 0.0 collective-permute-done.3.outer
  32.0 0.0 collective-permute-done.4
  32.0 1.1 %collective-permute-done.5 = f32[2,96,128]{2,1,0:T(8,128)S(1)} collective-permute-done((f32[2,96,128]{2,1,0:T(8,128)S(1)}, f32[2,96,128]{2,1,0:T(8,128)S(1)}, u32[]{:S(2)}, u32[]{:S(2)}) %collective-permute-start.5) | collective-permute-done | bytes 98336 | tf_op jit(solution)/shard_map/ppermute | solution.py:20
  33.1 0.0 copy-start.8
  33.1 0.0 copy-start.2
  33.2 5.6 %collective-permute-done.6 = f32[2,96,128]{2,1,0:T(8,128)S(1)} collective-permute-done((f32[2,96,128]{2,1,0:T(8,128)S(1)}, f32[2,96,128]{2,1,0:T(8,128)S(1)}, u32[]{:S(2)}, u32[]{:S(2)}) %collective-permute-start.6) | collective-permute-done | bytes 98336 | tf_op jit(solution)/shard_map/ppermute | solution.py:20
  38.8 0.0 copy-start.9
  38.8 1.9 %collective-permute-start.7 = (f32[2,480,128]{2,1,0:T(8,128)S(1)}, f32[2,480,128]{2,1,0:T(8,128)S(1)}, u32[]{:S(2)}, u32[]{:S(2)}) collective-permute-start(f32[2,480,128]{2,1,0:T(8,128)S(1)} %constant_dynamic-update-slice_fusion.mine), channel_id=1, source_target_pairs={{0,8},{16,24},{32,40},{48,56},{64,72},{80,88},{96,104},{112,120},{... | collective-permute-start | bytes 1474568 | tf_op jit(solution)/shard_map/ppermute | solution.py:20
  40.7 0.0 copy-done.8
  40.7 0.0 copy-start.5
  40.8 0.1 copy.17.partner_ref
  40.8 0.0 copy-done.9
  40.8 0.1 copy.18.offset_ref
  40.9 0.0 copy-start
  40.9 0.0 copy-done.2
  40.9 0.5 %copy-done.5 = s32[24]{0:T(128)S(1)} copy-done((s32[24]{0:T(128)S(1)}, s32[24]{0:T(128)}, u32[]{:S(2)}) %copy-start.5) | copy-done | bytes 120
  41.4 0.0 copy-start.3
  41.4 0.0 copy-start.4
  41.4 3.7 %shard_map.142 = f32[2,24,8,128]{3,2,1,0:T(8,128)} custom-call(s32[24,16]{1,0:T(8,128)S(1)} %copy.17.partner_ref, s32[24,16]{1,0:T(8,128)S(1)} %copy.18.offset_ref, s32[24]{0:T(128)S(1)} %copy-done.5, f32[2,192,128]{2,1,0:T(8,128)} %bitcast.pattern_ref.own, f32[2,192,128]{2,1,0:T(8,128)S(1)} %collective-permute-done.2.inner, ...), custom_call_target="tpu_custom_call" | custom-call | flops 4000000 | bytes 4000000 | tf_op jit(solution)/shard_map/pallas_call | solution.py:159
  45.2 0.0 collective-permute-done.7.theirs
  45.2 0.0 copy-done
  45.2 0.0 copy-done.3
  45.2 0.0 copy-done.4
  45.2 0.0 copy-done.6
  45.2 2.4 %shard_map.143 = f32[2,3,16,256]{3,2,1,0:T(8,128)} custom-call(s32[3,16]{1,0:T(4,128)S(1)} %copy-done.3, s32[3,16]{1,0:T(4,128)S(1)} %copy-done.4, s32[3]{0:T(128)S(1)} %copy-done.6, f32[2,480,128]{2,1,0:T(8,128)S(1)} %constant_dynamic-update-slice_fusion.mine, f32[2,480,128]{2,1,0:T(8,128)S(1)} %collective-permute-done.7.theirs, f32[2,16,16,256]{3,2,1,0:T(8,128)S(1)} %copy-done), custom_call_target="tpu_custom_call" | custom-call | tf_op jit(solution)/shard_map/pallas_call | solution.py:215
  (7 shorter events, 0.0 us)
Async XLA Ops:
  0.6 12.5 %copy-start.7 = (f32[8,16,256]{2,1,0:T(8,128)S(1)}, f32[8,16,256]{2,1,0:T(8,128)}, u32[]{:S(2)}) copy-start(f32[8,16,256]{2,1,0:T(8,128)} %param.25) | copy-start | bytes 393220
  1.6 13.4 %collective-permute-start = (f32[2,2,24,128]{3,2,1,0:T(8,128)S(1)}, f32[2,2,24,128]{3,2,1,0:T(8,128)S(1)}, u32[]{:S(2)}, u32[]{:S(2)}) collective-permute-start(f32[2,2,24,128]{3,2,1,0:T(8,128)S(1)} %get-tuple-element.15), channel_id=1, source_target_pairs={{0,1},{2,3},{4,5},{6,7},{1,0},{3,2},{5,4},{7,6},{8,9},{10,11},{12,... | collective-permute-start | bytes 147464 | tf_op jit(solution)/shard_map/ppermute | solution.py:20
  3.6 11.5 %collective-permute-start.1 = (f32[2,2,24,128]{3,2,1,0:T(8,128)S(1)}, f32[2,2,24,128]{3,2,1,0:T(8,128)S(1)}, u32[]{:S(2)}, u32[]{:S(2)}) collective-permute-start(f32[2,2,24,128]{3,2,1,0:T(8,128)S(1)} %get-tuple-element.16), channel_id=1, source_target_pairs={{1,2},{3,4},{5,6},{2,1},{4,3},{6,5},{9,10},{11,12},{13,14},{10,9},... | collective-permute-start | bytes 147464 | tf_op jit(solution)/shard_map/ppermute | solution.py:20
  10.0 5.1 %collective-permute-start.2 = (f32[2,192,128]{2,1,0:T(8,128)}, f32[2,192,128]{2,1,0:T(8,128)S(1)}, u32[]{:S(2)}, u32[]{:S(2)}) collective-permute-start(f32[2,192,128]{2,1,0:T(8,128)} %bitcast.pattern_ref.own), channel_id=1, source_target_pairs={{0,8},{16,24},{32,40},{48,56},{64,72},{80,88},{96,104},{112,120},{... | collective-permute-start | bytes 589832 | tf_op jit(solution)/shard_map/ppermute | solution.py:20
  13.1 1.9 %copy-start.1 = (f32[256,128]{1,0:T(8,128)S(1)}, f32[256,128]{1,0:T(8,128)}, u32[]{:S(2)}) copy-start(f32[256,128]{1,0:T(8,128)} %phi_ref.1) | copy-start | bytes 393220
  13.6 0.7 %copy-start.11 = (s32[16]{0:T(128)S(1)}, s32[16]{0:T(128)}, u32[]{:S(2)}) copy-start(s32[16]{0:T(128)} %param.22) | copy-start | bytes 196
  14.3 0.7 %copy-start.10 = (f32[16,4]{0,1:T(4,128)S(1)}, f32[16,4]{0,1:T(4,128)}, u32[]{:S(2)}) copy-start(f32[16,4]{0,1:T(4,128)} %param.23) | copy-start | bytes 772
  17.6 14.4 %collective-permute-start.3 = (f32[2,288,128]{2,1,0:T(8,128)S(1)}, f32[2,288,128]{2,1,0:T(8,128)S(1)}, u32[]{:S(2)}, u32[]{:S(2)}) collective-permute-start(f32[2,288,128]{2,1,0:T(8,128)S(1)} %get-tuple-element.20), channel_id=1, source_target_pairs={{8,16},{24,32},{40,48},{56,64},{72,80},{88,96},{104,112},{120,128}... | collective-permute-start | bytes 884744 | tf_op jit(solution)/shard_map/ppermute | solution.py:20
  20.7 11.3 %collective-permute-start.4 = (f32[2,96,128]{2,1,0:T(8,128)S(1)}, f32[2,96,128]{2,1,0:T(8,128)S(1)}, u32[]{:S(2)}, u32[]{:S(2)}) collective-permute-start(f32[2,96,128]{2,1,0:T(8,128)S(1)} %get-tuple-element.21), channel_id=1, source_target_pairs={{0,24},{16,40},{32,56},{48,72},{64,88},{80,104},{96,120},{112,136}... | collective-permute-start | bytes 294920 | tf_op jit(solution)/shard_map/ppermute | solution.py:20
  25.9 7.2 %collective-permute-start.5 = (f32[2,96,128]{2,1,0:T(8,128)S(1)}, f32[2,96,128]{2,1,0:T(8,128)S(1)}, u32[]{:S(2)}, u32[]{:S(2)}) collective-permute-start(f32[2,96,128]{2,1,0:T(8,128)S(1)} %get-tuple-element.21), channel_id=1, source_target_pairs={{8,32},{24,48},{40,64},{56,80},{72,96},{88,112},{104,128},{120,144... | collective-permute-start | bytes 294920 | tf_op jit(solution)/shard_map/ppermute | solution.py:20
  29.6 9.2 %collective-permute-start.6 = (f32[2,96,128]{2,1,0:T(8,128)S(1)}, f32[2,96,128]{2,1,0:T(8,128)S(1)}, u32[]{:S(2)}, u32[]{:S(2)}) collective-permute-start(f32[2,96,128]{2,1,0:T(8,128)S(1)} %get-tuple-element.21), channel_id=1, source_target_pairs={{0,40},{16,56},{32,72},{48,88},{64,104},{80,120},{96,136},{112,152... | collective-permute-start | bytes 294920 | tf_op jit(solution)/shard_map/ppermute | solution.py:20
  33.1 7.6 %copy-start.8 = (s32[24,16]{0,1:T(8,128)S(1)}, s32[24,16]{0,1:T(8,128)}, u32[]{:S(2)}) copy-start(s32[24,16]{0,1:T(8,128)} %param.14) | copy-start | bytes 4612
  33.1 7.8 %copy-start.2 = (f32[2,16,8,128]{3,2,1,0:T(8,128)S(1)}, f32[2,16,8,128]{3,2,1,0:T(8,128)}, u32[]{:S(2)}) copy-start(f32[2,16,8,128]{3,2,1,0:T(8,128)} %param.20) | copy-start | bytes 393220
  38.8 2.0 %copy-start.9 = (s32[24,16]{0,1:T(8,128)S(1)}, s32[24,16]{0,1:T(8,128)}, u32[]{:S(2)}) copy-start(s32[24,16]{0,1:T(8,128)} %param.15) | copy-start | bytes 4612
  38.8 6.4 %collective-permute-start.7 = (f32[2,480,128]{2,1,0:T(8,128)S(1)}, f32[2,480,128]{2,1,0:T(8,128)S(1)}, u32[]{:S(2)}, u32[]{:S(2)}) collective-permute-start(f32[2,480,128]{2,1,0:T(8,128)S(1)} %constant_dynamic-update-slice_fusion.mine), channel_id=1, source_target_pairs={{0,8},{16,24},{32,40},{48,56},{64,72},{80,88},{96,104},{112,120},{... | collective-permute-start | bytes 1474568 | tf_op jit(solution)/shard_map/ppermute | solution.py:20
  40.7 0.7 %copy-start.5 = (s32[24]{0:T(128)S(1)}, s32[24]{0:T(128)}, u32[]{:S(2)}) copy-start(s32[24]{0:T(128)} %count_ref.2) | copy-start | bytes 292
  40.9 4.3 %copy-start = (f32[2,16,16,256]{3,2,1,0:T(8,128)S(1)}, f32[2,16,16,256]{3,2,1,0:T(8,128)}, u32[]{:S(2)}) copy-start(f32[2,16,16,256]{3,2,1,0:T(8,128)} %table.1) | copy-start | bytes 1572868
  41.4 3.8 %copy-start.3 = (s32[3,16]{1,0:T(4,128)S(1)}, s32[3,16]{1,0:T(4,128)}, u32[]{:S(2)}) copy-start(s32[3,16]{1,0:T(4,128)} %partner_ref.2) | copy-start | bytes 580
  41.4 3.8 %copy-start.4 = (s32[3,16]{1,0:T(4,128)S(1)}, s32[3,16]{1,0:T(4,128)}, u32[]{:S(2)}) copy-start(s32[3,16]{1,0:T(4,128)} %offset_ref.2) | copy-start | bytes 580
  41.4 3.8 %copy-start.6 = (s32[3]{0:T(128)S(1)}, s32[3]{0:T(128)}, u32[]{:S(2)}) copy-start(s32[3]{0:T(128)} %count_ref.3) | copy-start | bytes 40

commit v3 on v2

v3 whole, which is shorter than its diff:
```python
import functools

import jax
import jax.numpy as jnp
from jax import lax
from jax.experimental import pallas as pl
from jax.experimental.pallas import tpu as pltpu
from jax.sharding import PartitionSpec as P

VMEM = pltpu.VMEM
SMEM = pltpu.SMEM
PARAMS = pltpu.CompilerParams(vmem_limit_bytes=16 * 1024 * 1024)


def spec(space):
    return pl.BlockSpec(memory_space=space)


def matched(x, axis, pairs):
    return lax.ppermute(x, axis, pairs + [(j, i) for i, j in pairs])


def swap_cores(x):
    n = lax.axis_size("box")
    return matched(x, "box", [(i, i + 1) for i in range(0, n, 2)])


def swap_chips(x, core, distance):
    n = lax.axis_size("box")
    pairs = [(i + core, i + 2 * distance + 1 - core) for i in range(0, n - 2 * distance, 2)]
    return matched(x, "box", pairs)


def swap_rims(x, start):
    n = lax.axis_size("samp")
    return matched(x, "samp", [(i, i + 1) for i in range(start, n - 1, 2)])


def rim_kernel(own_ref, inner_ref, even_ref, odd_ref):
    odd = lax.rem(lax.axis_index("samp"), 2) == 1
    for x in range(2):
        for row in range(2):
            for which, ref in enumerate((own_ref, inner_ref)):
                first = ref[x, pl.ds(row, 24, stride=8), :]
                last = ref[x, pl.ds(6 + row, 24, stride=8), :]
                boxes = pl.ds(24 * which, 24)
                even_ref[x, row, boxes] = jnp.where(odd, first, last)
                odd_ref[x, row, boxes] = jnp.where(odd, last, first)


def rims(own, inner):
    shape = jax.ShapeDtypeStruct((2, 2, 48, 128), jnp.float32)
    return pl.pallas_call(
        rim_kernel,
        out_shape=(shape, shape),
        in_specs=[spec(VMEM)] * 2,
        out_specs=(spec(VMEM), spec(VMEM)),
        compiler_params=PARAMS,
    )(own, inner)


def split(x):
    high = x.astype(jnp.bfloat16)
    return high, (x - high.astype(jnp.float32)).astype(jnp.bfloat16)


def dot(x, y):
    return jnp.dot(x, y, preferred_element_type=jnp.float32)


def matrices_kernel(start_ref, weight_ref, phi_ref, theta_ref, theta_low_ref, phi_out_ref, phi_low_ref):
    start = jnp.concatenate([start_ref[...]] * 8, axis=0)
    weight = jnp.concatenate([weight_ref[...]] * 8, axis=0)
    line = lax.broadcasted_iota(jnp.int32, (128, 96), 0)
    column = lax.broadcasted_iota(jnp.int32, (128, 96), 1)
    own = column < 64
    rim = (column - 64) // 8
    odd = lax.rem(lax.axis_index("samp"), 2) == 1
    rim = jnp.where((rim < 2) == odd, rim % 2 - 2, rim % 2 + 8)
    row = jnp.where(own, column % 8, rim)
    child = jnp.where(own, column // 8, column % 8)
    row = jnp.where(child == line // 16, row, -100)
    theta = jnp.zeros((128, 96), jnp.float32)
    for q in range(4):
        theta = theta + jnp.where(start + q == row, weight[:, q : q + 1], 0.0)
    high, low = split(theta)
    theta_ref[...] = jnp.concatenate([high, high], axis=1)
    theta_low_ref[...] = low
    high, low = split(phi_ref[...].T)
    phi_out_ref[...] = jnp.concatenate([high, high], axis=0)
    phi_low_ref[...] = low


def matrices(start, weight, phi):
    shapes = ((128, 192), (128, 96), (256, 256), (128, 256))
    return pl.pallas_call(
        matrices_kernel,
        out_shape=tuple(jax.ShapeDtypeStruct(s, jnp.bfloat16) for s in shapes),
        in_specs=[spec(VMEM)] * 3,
        out_specs=(spec(VMEM),) * 4,
        compiler_params=PARAMS,
    )(start, weight, phi)


def aggregate_kernel(
    own_ref, inner_ref, even_ref, odd_ref, theta_ref, theta_low_ref, phi_ref, phi_low_ref, cos_ref, sin_ref, pair_ref, both_ref
):
    me = lax.rem(lax.axis_index("box"), 2)
    theta, theta_low = theta_ref[...], theta_low_ref[...]
    phi, phi_low = phi_ref[...], phi_low_ref[...]
    both_ref[:, 192:] = own_ref[...]
    for which, ref in enumerate((own_ref, inner_ref)):
        place = 96 * (me if which == 0 else 1 - me)
        for k in range(3):
            columns = []
            for x in range(2):
                parts = [ref[x, 64 * k : 64 * k + 64]]
                for rim_ref in (even_ref, odd_ref):
                    parts += [rim_ref[x, r, pl.ds(24 * which + 8 * k, 8)] for r in range(2)]
                columns.append(jnp.concatenate(parts, axis=0))
            high, low = split(jnp.concatenate(columns, axis=1))
            narrow = dot(theta, jnp.concatenate([high, low], axis=0)) + dot(theta_low, high)
            high, low = split(narrow)
            wide = []
            for x in range(2):
                part = slice(128 * x, 128 * x + 128)
                both = jnp.concatenate([high[:, part], low[:, part]], axis=1)
                wide.append(dot(both, phi) + dot(high[:, part], phi_low))
            cosine, sine = cos_ref[...], sin_ref[...]
            real_part = (cosine * wide[0] - sine * wide[1]).reshape(8, 16, 256)
            imag_part = (cosine * wide[1] + sine * wide[0]).reshape(8, 16, 256)
            for x, value in enumerate((real_part, imag_part)):
                value = jnp.sum(value, axis=0)
                for half in range(2):
                    rows = pl.ds(pl.multiple_of(place + 32 * k + 16 * half, 16), 16)
                    pair_ref[x, rows] = value[:, 128 * half : 128 * half + 128]
                    both_ref[x, rows] = value[:, 128 * half : 128 * half + 128]


def aggregate(own, inner, even, odd, mats, cosine, sine):
    return pl.pallas_call(
        aggregate_kernel,
        out_shape=(
            jax.ShapeDtypeStruct((2, 192, 128), jnp.float32),
            jax.ShapeDtypeStruct((2, 384, 128), jnp.float32),
        ),
        in_specs=[spec(VMEM)] * 10,
        out_specs=(spec(VMEM), spec(VMEM)),
        compiler_params=PARAMS,
    )(own, inner, even, odd, *mats, cosine, sine)


def fine_kernel(partner_ref, offset_ref, count_ref, own, inner, outer, table, out_ref, window, operators, sems):
    me = lax.axis_index("box")
    odd = lax.rem(me, 2)
    copies = [
        pltpu.make_async_copy(own, window.at[:, pl.ds(192, 192)], sems.at[0]),
        pltpu.make_async_copy(inner, window.at[:, pl.ds(384 * (1 - odd), 192)], sems.at[1]),
        pltpu.make_async_copy(outer.at[:, pl.ds(192, 192)], window.at[:, pl.ds(384 * odd, 192)], sems.at[2]),
        pltpu.make_async_copy(table, operators.at[:, pl.ds(0, 128)], sems.at[3]),
    ]
    for copy in copies:
        copy.start()
    operators[:, 128:] = jnp.zeros((2, 8, 128), jnp.float32)
    for copy in copies:
        copy.wait()
    base = (me - 1) * 24

    def step(b, carry):
        sums = None
        for j in range(16):
            place = pl.multiple_of((partner_ref[b, j] - base) * 8, 8)
            which = pl.multiple_of(jnp.where(j < count_ref[b], offset_ref[b, j], 16) * 8, 8)
            a, c = operators[0, pl.ds(which, 8)], operators[1, pl.ds(which, 8)]
            f, g = window[0, pl.ds(place, 8)], window[1, pl.ds(place, 8)]
            terms = (a * f, c * g, a * g, c * f)
            sums = terms if sums is None else tuple(s + t for s, t in zip(sums, terms))
        out_ref[0, b] = sums[0] - sums[1]
        out_ref[1, b] = sums[2] + sums[3]
        return carry

    lax.fori_loop(0, 24, step, 0)


def fine_translate(pattern, inner, outer, table, partner, offset, count):
    return pl.pallas_call(
        fine_kernel,
        out_shape=jax.ShapeDtypeStruct((2, 24, 8, 128), jnp.float32),
        in_specs=[spec(SMEM)] * 3 + [spec(pl.ANY)] * 4,
        out_specs=spec(VMEM),
        scratch_shapes=[
            pltpu.VMEM((2, 576, 128), jnp.float32),
            pltpu.VMEM((2, 136, 128), jnp.float32),
            pltpu.SemaphoreType.DMA((4,)),
        ],
        compiler_params=PARAMS,
        cost_estimate=pl.CostEstimate(flops=4_000_000, bytes_accessed=40_000_000, transcendentals=0),
    )(partner, offset, count, pattern, inner, outer, table.reshape(2, 128, 128))


def coarse_sums(window, table, partner_ref, offset_ref, count_ref, b, near):
    me = lax.axis_index("box")
    odd = lax.rem(me, 2) == 1
    base = (me // 2 - 2) * 6
    sums = [None, None]
    for j in range(16):
        place = partner_ref[b, j] - base
        side = jnp.where(odd, place >= 12, place < 18)
        live = jnp.logical_and(j < count_ref[b], side if near else jnp.logical_not(side))
        place = jnp.where(place >= 24, place - 24, jnp.where(place >= 18, place - 12, place))
        place = pl.multiple_of(jnp.where(live, place, 0) * 32, 32)
        scale = jnp.where(live, 1.0, 0.0)
        which = offset_ref[b, j]
        for half in range(2):
            lanes = slice(128 * half, 128 * half + 128)
            a, c = table[0, which, :, lanes] * scale, table[1, which, :, lanes] * scale
            f, g = window[0, pl.ds(place + 16 * half, 16)], window[1, pl.ds(place + 16 * half, 16)]
            terms = (a * f, c * g, a * g, c * f)
            old = sums[half]
            sums[half] = terms if old is None else tuple(s + t for s, t in zip(old, terms))
    return [(s[0] - s[1], s[2] + s[3]) for s in sums]


def near_kernel(partner_ref, offset_ref, count_ref, pair, sides, table, out_ref, window, sems):
    copies = [
        pltpu.make_async_copy(sides, window.at[:, pl.ds(0, 384)], sems.at[0]),
        pltpu.make_async_copy(pair, window.at[:, pl.ds(384, 192)], sems.at[1]),
    ]
    for copy in copies:
        copy.start()
    for copy in copies:
        copy.wait()

    def step(b, carry):
        sums = coarse_sums(window, table, partner_ref, offset_ref, count_ref, b, True)
        for half in range(2):
            for x in range(2):
                out_ref[x, b, :, 128 * half : 128 * half + 128] = sums[half][x]
        return carry

    lax.fori_loop(0, 3, step, 0)


def far_kernel(partner_ref, offset_ref, count_ref, other, table, part_ref, out_ref):
    def step(b, carry):
        sums = coarse_sums(other, table, partner_ref, offset_ref, count_ref, b, False)
        for half in range(2):
            lanes = slice(128 * half, 128 * half + 128)
            for x in range(2):
                out_ref[x, b, :, lanes] = part_ref[x, b, :, lanes] + sums[half][x]
        return carry

    lax.fori_loop(0, 3, step, 0)


def near_translate(pair, sides, table, partner, offset, count):
    return pl.pallas_call(
        near_kernel,
        out_shape=jax.ShapeDtypeStruct((2, 3, 16, 256), jnp.float32),
        in_specs=[spec(SMEM)] * 3 + [spec(pl.ANY)] * 2 + [spec(VMEM)],
        out_specs=spec(VMEM),
        scratch_shapes=[pltpu.VMEM((2, 576, 128), jnp.float32), pltpu.SemaphoreType.DMA((2,))],
        compiler_params=PARAMS,
    )(partner, offset, count, pair, sides, table)


def far_translate(other, table, part, partner, offset, count):
    return pl.pallas_call(
        far_kernel,
        out_shape=jax.ShapeDtypeStruct((2, 3, 16, 256), jnp.float32),
        in_specs=[spec(SMEM)] * 3 + [spec(VMEM)] * 3,
        out_specs=spec(VMEM),
        compiler_params=PARAMS,
    )(partner, offset, count, other, table, part)


def shards(
    fine_pattern,
    fine_partner,
    fine_offset,
    fine_count,
    coarse_partner,
    coarse_offset,
    coarse_count,
    fine_table,
    coarse_table,
    theta_start,
    theta_weight,
    phi_interp,
    shift_phase,
):
    pattern = fine_pattern.reshape(2, 192, 128)
    inner = swap_cores(pattern)
    start = (theta_start - lax.axis_index("samp") * 8)[:, None]
    mats = matrices(start, theta_weight, phi_interp)
    phase = shift_phase.reshape(128, 256)
    waves = (jnp.cos(phase), jnp.sin(phase))
    inner, mats, waves = lax.optimization_barrier((inner, mats, waves))
    even, odd = rims(pattern, inner)
    even, odd = swap_rims(even, 0), swap_rims(odd, 1)
    pair, both = aggregate(pattern, inner, even, odd, mats, *waves)
    outer = swap_chips(both, 1, 1)
    distant = swap_chips(pair, 1, 2)
    fine_incoming = fine_translate(
        pattern, inner, outer, fine_table, fine_partner, fine_offset, fine_count
    )
    distant, fine_incoming = lax.optimization_barrier((distant, fine_incoming))
    sides = jnp.concatenate([distant, outer[:, :192]], axis=1)
    other = swap_cores(sides)
    part = near_translate(pair, sides, coarse_table, coarse_partner, coarse_offset, coarse_count)
    coarse_incoming = far_translate(
        other, coarse_table, part, coarse_partner, coarse_offset, coarse_count
    )
    return (fine_incoming, coarse_incoming)


def solution(mesh):
    return jax.shard_map(
        shards,
        mesh=mesh,
        in_specs=(
            P(None, "box", "samp", None),
            P("box", None),
            P("box", None),
            P("box"),
            P("box", None),
            P("box", None),
            P("box"),
            P(None, None, "samp", None),
            P(None, None, "samp", None),
            P("samp"),
            P("samp", None),
            P(),
            P(None, "samp", None),
        ),
        out_specs=(P(None, "box", "samp", None), P(None, "box", "samp", None)),
        check_vma=False,
    )
```

time: 48 us -> 42.4 us (0.88)
  the two profiles are of different devices: /device:TPU:197 before, /device:TPU:199 now
where the time goes in v3:
time: 42.4 us; the launch traced here: 42 us
  starting transfers between devices  21.4 us (50%)
  Pallas kernels  8.13 us (19%)
  waiting for transfers between devices  7.46 us (18%)
  local copies, waits for them, and re-layouts  4.1 us (10%)
  between operations  0.85 us (2%)
    ppermute x6, starting transfers between devices, matched(): return lax.ppermute(x, axis, pairs + [(j, i) for i, j in pairs])  21.4 us
    ppermute x6, waiting for transfers between devices, matched(): return lax.ppermute(x, axis, pairs + [(j, i) for i, j in pairs])  7.46 us
    unnamed x29, local copies, waits for them, and re-layouts  3.54 us
    pallas_call x1, Pallas kernels, fine_translate(): pl.pallas_call(fine_kernel, out_shape=jax.ShapeDtypeStruct((2, 24, 8, 128...  3.31 us
    pallas_call x1, Pallas kernels, far_translate(): pl.pallas_call(far_kernel, out_shape=jax.ShapeDtypeStruct((2, 3, 16, 256)...  1.69 us
    pallas_call x1, Pallas kernels, aggregate(): pl.pallas_call(aggregate_kernel, out_shape=(jax.ShapeDtypeStruct((2, 192,...  1.57 us
    pallas_call x1, Pallas kernels, near_translate(): pl.pallas_call(near_kernel, out_shape=jax.ShapeDtypeStruct((2, 3, 16, 256...  1.31 us
  transfers between devices with their start and end apart: 6, of which 3 were waited for; matrix products, arithmetic and copies ran while one was open for 2% of the time, Pallas kernels for 12%

profile of v3, /device:TPU:199, one launch (start us, length us, event | category | flops | bytes accessed | tf_op | source)
XLA Modules:
  0.0 42.0 jit_solution(2739965748269783139)
XLA Ops:
  0.6 2.6 %collective-permute-start = (f32[2,192,128]{2,1,0:T(8,128)}, f32[2,192,128]{2,1,0:T(8,128)S(1)}, u32[]{:S(2)}, u32[]{:S(2)}) collective-permute-start(f32[2,192,128]{2,1,0:T(8,128)} %bitcast.6), channel_id=1, source_target_pairs={{0,8},{16,24},{32,40},{48,56},{64,72},{80,88},{96,104},{112,120},{... | collective-permute-start | bytes 589832 | tf_op jit(solution)/shard_map/ppermute | solution.py:20
  3.2 0.0 copy-start.12
  3.2 0.6 %copy-done.12 = s32[16]{0:T(128)S(1)} copy-done((s32[16]{0:T(128)S(1)}, s32[16]{0:T(128)}, u32[]{:S(2)}) %copy-start.12) | copy-done | bytes 88
  3.9 0.0 copy-start.11
  3.9 0.1 copy.15.start_ref
  4.0 0.6 %copy-done.11 = f32[16,4]{0,1:T(4,128)S(1)} copy-done((f32[16,4]{0,1:T(4,128)S(1)}, f32[16,4]{0,1:T(4,128)}, u32[]{:S(2)}) %copy-start.11) | copy-done | bytes 280
  4.6 0.1 copy.16.weight_ref
  4.7 0.0 copy-start.2
  4.7 0.9 %copy-done.2 = f32[256,128]{1,0:T(8,128)S(1)} copy-done((f32[256,128]{1,0:T(8,128)S(1)}, f32[256,128]{1,0:T(8,128)}, u32[]{:S(2)}) %copy-start.2) | copy-done | bytes 131096
  5.6 0.0 copy-start.8
  5.6 0.2 shard_map.140
  5.8 0.7 %copy-done.8 = f32[8,16,256]{2,1,0:T(8,128)S(1)} copy-done((f32[8,16,256]{2,1,0:T(8,128)S(1)}, f32[8,16,256]{2,1,0:T(8,128)}, u32[]{:S(2)}) %copy-start.8) | copy-done | bytes 131096
  6.5 0.0 copy-start.1
  6.5 0.5 %fusion = (f32[8,16,256]{2,1,0:T(8,128)S(1)}, f32[8,16,256]{2,1,0:T(8,128)S(1)}) fusion(f32[8,16,256]{2,1,0:T(8,128)S(1)} %copy-done.8), kind=kLoop, calls=%fused_computation.2 | loop fusion | bytes 393216 | tf_op jit(solution)/shard_map/sin | solution.py:297
  6.9 0.0 collective-permute-done.inner_ref.inner
  6.9 0.5 %copy-done.1 = f32[2,24,8,128]{3,2,1,0:T(8,128)S(1)} copy-done((f32[2,24,8,128]{3,2,1,0:T(8,128)S(1)}, f32[2,24,8,128]{3,2,1,0:T(8,128)}, u32[]{:S(2)}) %copy-start.1) | copy-done | bytes 196632
  7.4 1.9 %collective-permute-start.1 = (f32[2,2,48,128]{3,2,1,0:T(8,128)S(1)}, f32[2,2,48,128]{3,2,1,0:T(8,128)S(1)}, u32[]{:S(2)}, u32[]{:S(2)}) collective-permute-start(f32[2,2,48,128]{3,2,1,0:T(8,128)S(1)} %get-tuple-element.24), channel_id=1, source_target_pairs={{0,1},{2,3},{4,5},{6,7},{1,0},{3,2},{5,4},{7,6},{8,9},{10,11},{12,... | collective-permute-start | bytes 294920 | tf_op jit(solution)/shard_map/ppermute | solution.py:20
  9.4 6.4 %collective-permute-start.2 = (f32[2,2,48,128]{3,2,1,0:T(8,128)S(1)}, f32[2,2,48,128]{3,2,1,0:T(8,128)S(1)}, u32[]{:S(2)}, u32[]{:S(2)}) collective-permute-start(f32[2,2,48,128]{3,2,1,0:T(8,128)S(1)} %get-tuple-element.25), channel_id=1, source_target_pairs={{1,2},{3,4},{5,6},{2,1},{4,3},{6,5},{9,10},{11,12},{13,14},{10,9},... | collective-permute-start | bytes 294920 | tf_op jit(solution)/shard_map/ppermute | solution.py:20
  15.8 0.0 collective-permute-done.1.even_ref
  15.8 2.9 %collective-permute-done.2.odd_ref = f32[2,2,48,128]{3,2,1,0:T(8,128)S(1)} collective-permute-done((f32[2,2,48,128]{3,2,1,0:T(8,128)S(1)}, f32[2,2,48,128]{3,2,1,0:T(8,128)S(1)}, u32[]{:S(2)}, u32[]{:S(2)}) %collective-permute-start.2) | collective-permute-done | bytes 98336 | tf_op jit(solution)/shard_map/ppermute | solution.py:20
  18.7 0.0 copy-start.9
  18.7 0.0 copy-start.3
  18.7 1.6 %shard_map.142 = (f32[2,192,128]{2,1,0:T(8,128)S(1)}, f32[2,384,128]{2,1,0:T(8,128)S(1)}) custom-call(f32[2,192,128]{2,1,0:T(8,128)S(1)} %bitcast.8, f32[2,192,128]{2,1,0:T(8,128)S(1)} %collective-permute-done.inner_ref.inner, f32[2,2,48,128]{3,2,1,0:T(8,128)S(1)} %collective-permute-done.1.even_ref, f32[2,2,48,128]{3,2,1,0:T(8,128)S(1)} %collective-permute-done.2.odd_ref, ...), custom_call_target="tpu_custom_call" | custom-call | tf_op jit(solution)/shard_map/pallas_call | solution.py:141
  20.3 3.9 %collective-permute-start.4 = (f32[2,384,128]{2,1,0:T(8,128)S(1)}, f32[2,384,128]{2,1,0:T(8,128)S(1)}, u32[]{:S(2)}, u32[]{:S(2)}) collective-permute-start(f32[2,384,128]{2,1,0:T(8,128)S(1)} %get-tuple-element.33), channel_id=1, source_target_pairs={{8,16},{24,32},{40,48},{56,64},{72,80},{88,96},{104,112},{120,128}... | collective-permute-start | bytes 1179656 | tf_op jit(solution)/shard_map/ppermute | solution.py:20
  24.2 0.0 copy-start.10
  24.2 2.9 %collective-permute-start.3 = (f32[2,192,128]{2,1,0:T(8,128)S(1)}, f32[2,192,128]{2,1,0:T(8,128)S(1)}, u32[]{:S(2)}, u32[]{:S(2)}) collective-permute-start(f32[2,192,128]{2,1,0:T(8,128)S(1)} %get-tuple-element.32.pair), channel_id=1, source_target_pairs={{8,32},{24,48},{40,64},{56,80},{72,96},{88,112},{104,128},{120,144... | collective-permute-start | bytes 589832 | tf_op jit(solution)/shard_map/ppermute | solution.py:20
  27.1 0.0 copy-done.9
  27.1 0.1 copy.17.partner_ref
  27.2 0.0 copy-done.10
  27.2 0.1 copy.18.offset_ref
  27.3 0.0 copy-start.7
  27.3 2.6 %collective-permute-done.4.outer = f32[2,384,128]{2,1,0:T(8,128)S(1)} collective-permute-done((f32[2,384,128]{2,1,0:T(8,128)S(1)}, f32[2,384,128]{2,1,0:T(8,128)S(1)}, u32[]{:S(2)}, u32[]{:S(2)}) %collective-permute-start.4) | collective-permute-done | bytes 393248 | tf_op jit(solution)/shard_map/ppermute | solution.py:20
  29.9 0.0 copy-done.3
  29.9 0.0 copy-done.7
  29.9 3.3 %shard_map.143 = f32[2,24,8,128]{3,2,1,0:T(8,128)} custom-call(s32[24,16]{1,0:T(8,128)S(1)} %copy.17.partner_ref, s32[24,16]{1,0:T(8,128)S(1)} %copy.18.offset_ref, s32[24]{0:T(128)S(1)} %copy-done.7, f32[2,192,128]{2,1,0:T(8,128)S(1)} %bitcast.9, f32[2,192,128]{2,1,0:T(8,128)S(1)} %collective-permute-done.inner_ref.inner, ...), custom_call_target="tpu_custom_call" | custom-call | flops 4000000 | bytes 40000000 | tf_op jit(solution)/shard_map/pallas_call | solution.py:186
  33.2 0.0 copy-start
  33.2 1.9 %collective-permute-done.3 = f32[2,192,128]{2,1,0:T(8,128)S(1)} collective-permute-done((f32[2,192,128]{2,1,0:T(8,128)S(1)}, f32[2,192,128]{2,1,0:T(8,128)S(1)}, u32[]{:S(2)}, u32[]{:S(2)}) %collective-permute-start.3) | collective-permute-done | bytes 196640 | tf_op jit(solution)/shard_map/ppermute | solution.py:20
  35.2 0.0 copy-start.4
  35.2 0.0 copy-start.5
  35.2 0.0 copy-start.6
  35.2 3.7 %collective-permute-start.5 = (f32[2,384,128]{2,1,0:T(8,128)S(1)}, f32[2,384,128]{2,1,0:T(8,128)S(1)}, u32[]{:S(2)}, u32[]{:S(2)}) collective-permute-start(f32[2,384,128]{2,1,0:T(8,128)S(1)} %pad_maximum_fusion.sides), channel_id=1, source_target_pairs={{0,8},{16,24},{32,40},{48,56},{64,72},{80,88},{96,104},{112,120},{... | collective-permute-start | bytes 1179656 | tf_op jit(solution)/shard_map/ppermute | solution.py:20
  38.9 0.0 copy-done
  39.0 0.0 copy-done.4
  39.0 0.0 copy-done.5
  39.0 0.0 copy-done.6
  39.0 1.3 %shard_map.144.part_ref = f32[2,3,16,256]{3,2,1,0:T(8,128)S(1)} custom-call(s32[3,16]{1,0:T(4,128)S(1)} %copy-done.4, s32[3,16]{1,0:T(4,128)S(1)} %copy-done.5, s32[3]{0:T(128)S(1)} %copy-done.6, f32[2,192,128]{2,1,0:T(8,128)S(1)} %get-tuple-element.32.pair, f32[2,384,128]{2,1,0:T(8,128)S(1)} %pad_maximum_fusion.sides, f32[2,16,16,256]{3,2,1,0:T(8,128)S(1)} %copy-done), custom_call_target="tpu_custom_call" | custom-call | tf_op jit(solution)/shard_map/pallas_call | solution.py:257
  40.3 0.0 collective-permute-done.5.other
  40.3 1.7 %shard_map.145 = f32[2,3,16,256]{3,2,1,0:T(8,128)} custom-call(s32[3,16]{1,0:T(4,128)S(1)} %copy-done.4, s32[3,16]{1,0:T(4,128)S(1)} %copy-done.5, s32[3]{0:T(128)S(1)} %copy-done.6, f32[2,384,128]{2,1,0:T(8,128)S(1)} %collective-permute-done.5.other, f32[2,16,16,256]{3,2,1,0:T(8,128)S(1)} %copy-done, f32[2,3,16,256]{3,2,1,0:T(8,128)S(1)} %shard_map.144.part_ref), custom_call_target="tpu_custom_call" | custom-call | tf_op jit(solution)/shard_map/pallas_call | solution.py:268
  (4 shorter events, 0.1 us)
Async XLA Ops:
  0.6 6.3 %collective-permute-start = (f32[2,192,128]{2,1,0:T(8,128)}, f32[2,192,128]{2,1,0:T(8,128)S(1)}, u32[]{:S(2)}, u32[]{:S(2)}) collective-permute-start(f32[2,192,128]{2,1,0:T(8,128)} %bitcast.6), channel_id=1, source_target_pairs={{0,8},{16,24},{32,40},{48,56},{64,72},{80,88},{96,104},{112,120},{... | collective-permute-start | bytes 589832 | tf_op jit(solution)/shard_map/ppermute | solution.py:20
  3.2 0.7 %copy-start.12 = (s32[16]{0:T(128)S(1)}, s32[16]{0:T(128)}, u32[]{:S(2)}) copy-start(s32[16]{0:T(128)} %param.22) | copy-start | bytes 196
  3.9 0.7 %copy-start.11 = (f32[16,4]{0,1:T(4,128)S(1)}, f32[16,4]{0,1:T(4,128)}, u32[]{:S(2)}) copy-start(f32[16,4]{0,1:T(4,128)} %param.23) | copy-start | bytes 772
  4.7 0.9 %copy-start.2 = (f32[256,128]{1,0:T(8,128)S(1)}, f32[256,128]{1,0:T(8,128)}, u32[]{:S(2)}) copy-start(f32[256,128]{1,0:T(8,128)} %phi_ref.1) | copy-start | bytes 393220
  5.6 0.9 %copy-start.8 = (f32[8,16,256]{2,1,0:T(8,128)S(1)}, f32[8,16,256]{2,1,0:T(8,128)}, u32[]{:S(2)}) copy-start(f32[8,16,256]{2,1,0:T(8,128)} %param.25) | copy-start | bytes 393220
  6.5 0.9 %copy-start.1 = (f32[2,24,8,128]{3,2,1,0:T(8,128)S(1)}, f32[2,24,8,128]{3,2,1,0:T(8,128)}, u32[]{:S(2)}) copy-start(f32[2,24,8,128]{3,2,1,0:T(8,128)} %param.13) | copy-start | bytes 589828
  7.4 8.3 %collective-permute-start.1 = (f32[2,2,48,128]{3,2,1,0:T(8,128)S(1)}, f32[2,2,48,128]{3,2,1,0:T(8,128)S(1)}, u32[]{:S(2)}, u32[]{:S(2)}) collective-permute-start(f32[2,2,48,128]{3,2,1,0:T(8,128)S(1)} %get-tuple-element.24), channel_id=1, source_target_pairs={{0,1},{2,3},{4,5},{6,7},{1,0},{3,2},{5,4},{7,6},{8,9},{10,11},{12,... | collective-permute-start | bytes 294920 | tf_op jit(solution)/shard_map/ppermute | solution.py:20
  9.4 9.3 %collective-permute-start.2 = (f32[2,2,48,128]{3,2,1,0:T(8,128)S(1)}, f32[2,2,48,128]{3,2,1,0:T(8,128)S(1)}, u32[]{:S(2)}, u32[]{:S(2)}) collective-permute-start(f32[2,2,48,128]{3,2,1,0:T(8,128)S(1)} %get-tuple-element.25), channel_id=1, source_target_pairs={{1,2},{3,4},{5,6},{2,1},{4,3},{6,5},{9,10},{11,12},{13,14},{10,9},... | collective-permute-start | bytes 294920 | tf_op jit(solution)/shard_map/ppermute | solution.py:20
  18.7 8.4 %copy-start.9 = (s32[24,16]{0,1:T(8,128)S(1)}, s32[24,16]{0,1:T(8,128)}, u32[]{:S(2)}) copy-start(s32[24,16]{0,1:T(8,128)} %param.14) | copy-start | bytes 4612
  18.7 11.2 %copy-start.3 = (f32[2,16,8,128]{3,2,1,0:T(8,128)S(1)}, f32[2,16,8,128]{3,2,1,0:T(8,128)}, u32[]{:S(2)}) copy-start(f32[2,16,8,128]{3,2,1,0:T(8,128)} %param.20) | copy-start | bytes 393220
  20.3 9.6 %collective-permute-start.4 = (f32[2,384,128]{2,1,0:T(8,128)S(1)}, f32[2,384,128]{2,1,0:T(8,128)S(1)}, u32[]{:S(2)}, u32[]{:S(2)}) collective-permute-start(f32[2,384,128]{2,1,0:T(8,128)S(1)} %get-tuple-element.33), channel_id=1, source_target_pairs={{8,16},{24,32},{40,48},{56,64},{72,80},{88,96},{104,112},{120,128}... | collective-permute-start | bytes 1179656 | tf_op jit(solution)/shard_map/ppermute | solution.py:20
  24.2 3.0 %copy-start.10 = (s32[24,16]{0,1:T(8,128)S(1)}, s32[24,16]{0,1:T(8,128)}, u32[]{:S(2)}) copy-start(s32[24,16]{0,1:T(8,128)} %param.15) | copy-start | bytes 4612
  24.2 11.0 %collective-permute-start.3 = (f32[2,192,128]{2,1,0:T(8,128)S(1)}, f32[2,192,128]{2,1,0:T(8,128)S(1)}, u32[]{:S(2)}, u32[]{:S(2)}) collective-permute-start(f32[2,192,128]{2,1,0:T(8,128)S(1)} %get-tuple-element.32.pair), channel_id=1, source_target_pairs={{8,32},{24,48},{40,64},{56,80},{72,96},{88,112},{104,128},{120,144... | collective-permute-start | bytes 589832 | tf_op jit(solution)/shard_map/ppermute | solution.py:20
  27.3 2.6 %copy-start.7 = (s32[24]{0:T(128)S(1)}, s32[24]{0:T(128)}, u32[]{:S(2)}) copy-start(s32[24]{0:T(128)} %count_ref.3) | copy-start | bytes 292
  33.2 5.7 %copy-start = (f32[2,16,16,256]{3,2,1,0:T(8,128)S(1)}, f32[2,16,16,256]{3,2,1,0:T(8,128)}, u32[]{:S(2)}) copy-start(f32[2,16,16,256]{3,2,1,0:T(8,128)} %table.3) | copy-start | bytes 1572868
  35.2 3.8 %copy-start.4 = (s32[3,16]{1,0:T(4,128)S(1)}, s32[3,16]{1,0:T(4,128)}, u32[]{:S(2)}) copy-start(s32[3,16]{1,0:T(4,128)} %partner_ref.4) | copy-start | bytes 580
  35.2 3.8 %copy-start.5 = (s32[3,16]{1,0:T(4,128)S(1)}, s32[3,16]{1,0:T(4,128)}, u32[]{:S(2)}) copy-start(s32[3,16]{1,0:T(4,128)} %offset_ref.4) | copy-start | bytes 580
  35.2 3.8 %copy-start.6 = (s32[3]{0:T(128)S(1)}, s32[3]{0:T(128)}, u32[]{:S(2)}) copy-start(s32[3]{0:T(128)} %count_ref.5) | copy-start | bytes 40
  35.2 5.1 %collective-permute-start.5 = (f32[2,384,128]{2,1,0:T(8,128)S(1)}, f32[2,384,128]{2,1,0:T(8,128)S(1)}, u32[]{:S(2)}, u32[]{:S(2)}) collective-permute-start(f32[2,384,128]{2,1,0:T(8,128)S(1)} %pad_maximum_fusion.sides), channel_id=1, source_target_pairs={{0,8},{16,24},{32,40},{48,56},{64,72},{80,88},{96,104},{112,120},{... | collective-permute-start | bytes 1179656 | tf_op jit(solution)/shard_map/ppermute | solution.py:20

commit v4 on v3

--- a/solution.py
+++ b/solution.py
@@ -69,20 +69,21 @@
 
 
 def matrices_kernel(start_ref, weight_ref, phi_ref, theta_ref, theta_low_ref, phi_out_ref, phi_low_ref):
-    start = jnp.concatenate([start_ref[...]] * 8, axis=0)
-    weight = jnp.concatenate([weight_ref[...]] * 8, axis=0)
+    samp = lax.axis_index("samp")
+    line = lax.broadcasted_iota(jnp.int32, (16, 96), 0)
+    column = lax.broadcasted_iota(jnp.int32, (16, 96), 1)
+    rim = (column - 64) // 8
+    rim = jnp.where((rim < 2) == (lax.rem(samp, 2) == 1), rim % 2 - 2, rim % 2 + 8)
+    row = jnp.where(column < 64, column % 8, rim) + samp * 8
+    theta = jnp.zeros((16, 96), jnp.float32)
+    for i in range(16):
+        for q in range(4):
+            theta = theta + jnp.where((row == start_ref[i] + q) & (line == i), weight_ref[q, i], 0.0)
+    theta = jnp.concatenate([theta] * 8, axis=0)
     line = lax.broadcasted_iota(jnp.int32, (128, 96), 0)
     column = lax.broadcasted_iota(jnp.int32, (128, 96), 1)
-    own = column < 64
-    rim = (column - 64) // 8
-    odd = lax.rem(lax.axis_index("samp"), 2) == 1
-    rim = jnp.where((rim < 2) == odd, rim % 2 - 2, rim % 2 + 8)
-    row = jnp.where(own, column % 8, rim)
-    child = jnp.where(own, column // 8, column % 8)
-    row = jnp.where(child == line // 16, row, -100)
-    theta = jnp.zeros((128, 96), jnp.float32)
-    for q in range(4):
-        theta = theta + jnp.where(start + q == row, weight[:, q : q + 1], 0.0)
+    child = jnp.where(column < 64, column // 8, column % 8)
+    theta = jnp.where(child == line // 16, theta, 0.0)
     high, low = split(theta)
     theta_ref[...] = jnp.concatenate([high, high], axis=1)
     theta_low_ref[...] = low
@@ -96,19 +97,18 @@
     return pl.pallas_call(
         matrices_kernel,
         out_shape=tuple(jax.ShapeDtypeStruct(s, jnp.bfloat16) for s in shapes),
-        in_specs=[spec(VMEM)] * 3,
+        in_specs=[spec(SMEM), spec(SMEM), spec(VMEM)],
         out_specs=(spec(VMEM),) * 4,
         compiler_params=PARAMS,
-    )(start, weight, phi)
+    )(start, weight.T, phi)
 
 
 def aggregate_kernel(
-    own_ref, inner_ref, even_ref, odd_ref, theta_ref, theta_low_ref, phi_ref, phi_low_ref, cos_ref, sin_ref, pair_ref, both_ref
+    own_ref, inner_ref, even_ref, odd_ref, theta_ref, theta_low_ref, phi_ref, phi_low_ref, cos_ref, sin_ref, pair_ref
 ):
     me = lax.rem(lax.axis_index("box"), 2)
     theta, theta_low = theta_ref[...], theta_low_ref[...]
     phi, phi_low = phi_ref[...], phi_low_ref[...]
-    both_ref[:, 192:] = own_ref[...]
     for which, ref in enumerate((own_ref, inner_ref)):
         place = 96 * (me if which == 0 else 1 - me)
         for k in range(3):
@@ -134,18 +134,14 @@
                 for half in range(2):
                     rows = pl.ds(pl.multiple_of(place + 32 * k + 16 * half, 16), 16)
                     pair_ref[x, rows] = value[:, 128 * half : 128 * half + 128]
-                    both_ref[x, rows] = value[:, 128 * half : 128 * half + 128]
 
 
 def aggregate(own, inner, even, odd, mats, cosine, sine):
     return pl.pallas_call(
         aggregate_kernel,
-        out_shape=(
-            jax.ShapeDtypeStruct((2, 192, 128), jnp.float32),
-            jax.ShapeDtypeStruct((2, 384, 128), jnp.float32),
-        ),
+        out_shape=jax.ShapeDtypeStruct((2, 192, 128), jnp.float32),
         in_specs=[spec(VMEM)] * 10,
-        out_specs=(spec(VMEM), spec(VMEM)),
+        out_specs=spec(VMEM),
         compiler_params=PARAMS,
     )(own, inner, even, odd, *mats, cosine, sine)
 
@@ -156,7 +152,7 @@
     copies = [
         pltpu.make_async_copy(own, window.at[:, pl.ds(192, 192)], sems.at[0]),
         pltpu.make_async_copy(inner, window.at[:, pl.ds(384 * (1 - odd), 192)], sems.at[1]),
-        pltpu.make_async_copy(outer.at[:, pl.ds(192, 192)], window.at[:, pl.ds(384 * odd, 192)], sems.at[2]),
+        pltpu.make_async_copy(outer, window.at[:, pl.ds(384 * odd, 192)], sems.at[2]),
         pltpu.make_async_copy(table, operators.at[:, pl.ds(0, 128)], sems.at[3]),
     ]
     for copy in copies:
@@ -291,21 +287,19 @@
 ):
     pattern = fine_pattern.reshape(2, 192, 128)
     inner = swap_cores(pattern)
-    start = (theta_start - lax.axis_index("samp") * 8)[:, None]
-    mats = matrices(start, theta_weight, phi_interp)
-    phase = shift_phase.reshape(128, 256)
-    waves = (jnp.cos(phase), jnp.sin(phase))
-    inner, mats, waves = lax.optimization_barrier((inner, mats, waves))
+    outer = swap_chips(pattern, 1, 1)
     even, odd = rims(pattern, inner)
     even, odd = swap_rims(even, 0), swap_rims(odd, 1)
-    pair, both = aggregate(pattern, inner, even, odd, mats, *waves)
-    outer = swap_chips(both, 1, 1)
-    distant = swap_chips(pair, 1, 2)
+    mats = matrices(theta_start, theta_weight, phi_interp)
+    phase = shift_phase.reshape(128, 256)
+    even, odd, outer = lax.optimization_barrier((even, odd, outer))
+    pair = aggregate(pattern, inner, even, odd, mats, jnp.cos(phase), jnp.sin(phase))
+    distant, next_to = swap_chips(pair, 1, 2), swap_chips(pair, 1, 1)
     fine_incoming = fine_translate(
         pattern, inner, outer, fine_table, fine_partner, fine_offset, fine_count
     )
-    distant, fine_incoming = lax.optimization_barrier((distant, fine_incoming))
-    sides = jnp.concatenate([distant, outer[:, :192]], axis=1)
+    distant, next_to, fine_incoming = lax.optimization_barrier((distant, next_to, fine_incoming))
+    sides = jnp.concatenate([distant, next_to], axis=1)
     other = swap_cores(sides)
     part = near_translate(pair, sides, coarse_table, coarse_partner, coarse_offset, coarse_count)
     coarse_incoming = far_translate(

time: 42.4 us -> 42.1 us (level)
  starting transfers between devices: 21.4 us -> 26.8 us
  waiting for transfers between devices: 7.46 us -> 2.39 us
  local copies, waits for them, and re-layouts: 4.1 us -> 2.95 us
  Pallas kernels: 8.13 us -> 8.69 us
    ppermute x6 -> x7, starting transfers between devices: 21.4 us -> 26.8 us  [matched(): return lax.ppermute(x, axis, pairs + [(j, i) for i, j in pairs])]
    ppermute x6 -> x7, waiting for transfers between devices: 7.46 us -> 2.39 us  [matched(): return lax.ppermute(x, axis, pairs + [(j, i) for i, j in pairs])]
    unnamed x29 -> x31, local copies, waits for them, and re-layouts: 3.54 us -> 2.47 us
    pallas_call x1, Pallas kernels: 0.22 us -> 0.77 us  [matrices(): pl.pallas_call(matrices_kernel, out_shape=tuple((jax.ShapeDtypeStruct(s,...]
  transfers between devices with their start and end apart: 6 -> 7, of which waited for: 3 -> 1; matrix products, arithmetic and copies ran while one was open for 2% -> 1% of each run, Pallas kernels for 12% -> 13%
where the time goes in v4:
time: 42.1 us; the launch traced here: 41.7 us
  starting transfers between devices  26.8 us (64%)
  Pallas kernels  8.69 us (21%)
  local copies, waits for them, and re-layouts  2.95 us (7%)
  waiting for transfers between devices  2.39 us (6%)
  between operations  0.91 us (2%)
    ppermute x7, starting transfers between devices, matched(): return lax.ppermute(x, axis, pairs + [(j, i) for i, j in pairs])  26.8 us
    pallas_call x1, Pallas kernels, fine_translate(): pl.pallas_call(fine_kernel, out_shape=jax.ShapeDtypeStruct((2, 24, 8, 128...  3.3 us
    unnamed x31, local copies, waits for them, and re-layouts  2.47 us
    ppermute x7, waiting for transfers between devices, matched(): return lax.ppermute(x, axis, pairs + [(j, i) for i, j in pairs])  2.39 us
    pallas_call x1, Pallas kernels, far_translate(): pl.pallas_call(far_kernel, out_shape=jax.ShapeDtypeStruct((2, 3, 16, 256)...  1.69 us
    pallas_call x1, Pallas kernels, aggregate(): pl.pallas_call(aggregate_kernel, out_shape=jax.ShapeDtypeStruct((2, 192,...  1.59 us
    pallas_call x1, Pallas kernels, near_translate(): pl.pallas_call(near_kernel, out_shape=jax.ShapeDtypeStruct((2, 3, 16, 256...  1.31 us
  transfers between devices with their start and end apart: 7, of which 1 were waited for; matrix products, arithmetic and copies ran while one was open for 1% of the time, Pallas kernels for 13%

profile of v4, /device:TPU:199, one launch (start us, length us, event | category | flops | bytes accessed | tf_op | source)
XLA Modules:
  0.0 41.7 jit_solution(4471159726177972316)
XLA Ops:
  0.6 2.6 %collective-permute-start = (f32[2,192,128]{2,1,0:T(8,128)}, f32[2,192,128]{2,1,0:T(8,128)S(1)}, u32[]{:S(2)}, u32[]{:S(2)}) collective-permute-start(f32[2,192,128]{2,1,0:T(8,128)} %bitcast.5), channel_id=1, source_target_pairs={{0,8},{16,24},{32,40},{48,56},{64,72},{80,88},{96,104},{112,120},{... | collective-permute-start | bytes 589832 | tf_op jit(solution)/shard_map/ppermute | solution.py:20
  3.2 3.1 %collective-permute-start.3 = (f32[2,192,128]{2,1,0:T(8,128)}, f32[2,192,128]{2,1,0:T(8,128)S(1)}, u32[]{:S(2)}, u32[]{:S(2)}) collective-permute-start(f32[2,192,128]{2,1,0:T(8,128)} %bitcast.6), channel_id=1, source_target_pairs={{8,16},{24,32},{40,48},{56,64},{72,80},{88,96},{104,112},{120,128}... | collective-permute-start | bytes 589832 | tf_op jit(solution)/shard_map/ppermute | solution.py:20
  6.3 0.0 collective-permute-done.inner_ref.inner
  6.3 0.0 copy-start.1
  6.4 1.0 %copy-done.1 = f32[2,24,8,128]{3,2,1,0:T(8,128)S(1)} copy-done((f32[2,24,8,128]{3,2,1,0:T(8,128)S(1)}, f32[2,24,8,128]{3,2,1,0:T(8,128)}, u32[]{:S(2)}) %copy-start.1) | copy-done | bytes 196632
  7.3 0.0 copy-start.11
  7.4 2.1 %collective-permute-start.1 = (f32[2,2,48,128]{3,2,1,0:T(8,128)S(1)}, f32[2,2,48,128]{3,2,1,0:T(8,128)S(1)}, u32[]{:S(2)}, u32[]{:S(2)}) collective-permute-start(f32[2,2,48,128]{3,2,1,0:T(8,128)S(1)} %get-tuple-element.14), channel_id=1, source_target_pairs={{0,1},{2,3},{4,5},{6,7},{1,0},{3,2},{5,4},{7,6},{8,9},{10,11},{12,... | collective-permute-start | bytes 294920 | tf_op jit(solution)/shard_map/ppermute | solution.py:20
  9.4 0.0 copy-start.4
  9.4 0.0 copy-start.2
  9.4 6.5 %collective-permute-start.2 = (f32[2,2,48,128]{3,2,1,0:T(8,128)S(1)}, f32[2,2,48,128]{3,2,1,0:T(8,128)S(1)}, u32[]{:S(2)}, u32[]{:S(2)}) collective-permute-start(f32[2,2,48,128]{3,2,1,0:T(8,128)S(1)} %get-tuple-element.15), channel_id=1, source_target_pairs={{1,2},{3,4},{5,6},{2,1},{4,3},{6,5},{9,10},{11,12},{13,14},{10,9},... | collective-permute-start | bytes 294920 | tf_op jit(solution)/shard_map/ppermute | solution.py:20
  16.0 0.0 copy-done.11
  16.0 0.0 copy-start.7
  16.0 0.5 %fusion = (f32[8,16,256]{2,1,0:T(8,128)S(1)}, f32[8,16,256]{2,1,0:T(8,128)S(1)}) fusion(f32[8,16,256]{2,1,0:T(8,128)S(1)} %copy-done.11), kind=kLoop, calls=%fused_computation.2 | loop fusion | bytes 393216 | tf_op jit(solution)/shard_map/sin | solution.py:296
  16.5 0.0 copy-start.9
  16.5 0.0 copy-done.4
  16.5 0.2 copy-done.7
  16.7 0.5 %copy-done.9 = s32[16]{0:T(128)S(1)} copy-done((s32[16]{0:T(128)S(1)}, s32[16]{0:T(128)}, u32[]{:S(2)}) %copy-start.9) | copy-done | bytes 88
  17.1 0.8 %shard_map.141 = (bf16[128,192]{1,0:T(8,128)(2,1)S(1)}, bf16[128,96]{1,0:T(8,128)(2,1)S(1)}, bf16[256,256]{1,0:T(8,128)(2,1)S(1)}, bf16[128,256]{1,0:T(8,128)(2,1)S(1)}) custom-call(s32[16]{0:T(128)S(1)} %copy-done.9, f32[4,16]{1,0:T(4,128)S(1)} %bitcast.13, f32[256,128]{1,0:T(8,128)S(1)} %copy-done.4), custom_call_target="tpu_custom_call" | custom-call | tf_op jit(solution)/shard_map/pallas_call | solution.py:97
  17.9 0.0 collective-permute-done.3.outer
  17.9 0.0 collective-permute-done.1.even_ref
  17.9 0.0 collective-permute-done.2.odd_ref
  18.0 0.0 copy-done.2
  18.0 0.0 copy-start.12
  18.0 1.6 %shard_map.142.pair = f32[2,192,128]{2,1,0:T(8,128)S(1)} custom-call(f32[2,192,128]{2,1,0:T(8,128)S(1)} %bitcast.8, f32[2,192,128]{2,1,0:T(8,128)S(1)} %collective-permute-done.inner_ref.inner, f32[2,2,48,128]{3,2,1,0:T(8,128)S(1)} %collective-permute-done.1.even_ref, f32[2,2,48,128]{3,2,1,0:T(8,128)S(1)} %collective-permute-done.2.odd_ref, ...), custom_call_target="tpu_custom_call" | custom-call | tf_op jit(solution)/shard_map/pallas_call | solution.py:140
  19.6 0.0 copy-start.13
  19.6 4.5 %collective-permute-start.5 = (f32[2,192,128]{2,1,0:T(8,128)S(1)}, f32[2,192,128]{2,1,0:T(8,128)S(1)}, u32[]{:S(2)}, u32[]{:S(2)}) collective-permute-start(f32[2,192,128]{2,1,0:T(8,128)S(1)} %shard_map.142.pair), channel_id=1, source_target_pairs={{8,16},{24,32},{40,48},{56,64},{72,80},{88,96},{104,112},{120,128}... | collective-permute-start | bytes 589832 | tf_op jit(solution)/shard_map/ppermute | solution.py:20
  24.1 3.1 %collective-permute-start.4 = (f32[2,192,128]{2,1,0:T(8,128)S(1)}, f32[2,192,128]{2,1,0:T(8,128)S(1)}, u32[]{:S(2)}, u32[]{:S(2)}) collective-permute-start(f32[2,192,128]{2,1,0:T(8,128)S(1)} %shard_map.142.pair), channel_id=1, source_target_pairs={{8,32},{24,48},{40,64},{56,80},{72,96},{88,112},{104,128},{120,144... | collective-permute-start | bytes 589832 | tf_op jit(solution)/shard_map/ppermute | solution.py:20
  27.2 0.0 copy-done.12
  27.2 0.1 copy.15.partner_ref
  27.3 0.0 copy-done.13
  27.3 0.1 copy.16.offset_ref
  27.3 0.0 copy-done.3
  27.3 0.7 %copy-done.10 = s32[24]{0:T(128)S(1)} copy-done((s32[24]{0:T(128)S(1)}, s32[24]{0:T(128)}, u32[]{:S(2)}) %copy-start.10) | copy-done | bytes 120
  28.0 3.3 %shard_map.143 = f32[2,24,8,128]{3,2,1,0:T(8,128)} custom-call(s32[24,16]{1,0:T(8,128)S(1)} %copy.15.partner_ref, s32[24,16]{1,0:T(8,128)S(1)} %copy.16.offset_ref, s32[24]{0:T(128)S(1)} %copy-done.10, f32[2,192,128]{2,1,0:T(8,128)S(1)} %bitcast.9, f32[2,192,128]{2,1,0:T(8,128)S(1)} %collective-permute-done.inner_ref.inner, ...), custom_call_target="tpu_custom_call" | custom-call | flops 4000000 | bytes 40000000 | tf_op jit(solution)/shard_map/pallas_call | solution.py:182
  31.3 0.0 copy-start
  31.3 0.0 collective-permute-done.5
  31.3 2.3 %collective-permute-done.4 = f32[2,192,128]{2,1,0:T(8,128)S(1)} collective-permute-done((f32[2,192,128]{2,1,0:T(8,128)S(1)}, f32[2,192,128]{2,1,0:T(8,128)S(1)}, u32[]{:S(2)}, u32[]{:S(2)}) %collective-permute-start.4) | collective-permute-done | bytes 196640 | tf_op jit(solution)/shard_map/ppermute | solution.py:20
  33.7 0.0 copy-start.5
  33.7 0.0 copy-start.6
  33.7 0.0 copy-start.8
  33.7 4.9 %collective-permute-start.6 = (f32[2,384,128]{2,1,0:T(8,128)S(1)}, f32[2,384,128]{2,1,0:T(8,128)S(1)}, u32[]{:S(2)}, u32[]{:S(2)}) collective-permute-start(f32[2,384,128]{2,1,0:T(8,128)S(1)} %constant_dynamic-update-slice_fusion.sides), channel_id=1, source_target_pairs={{0,8},{16,24},{32,40},{48,56},{64,72},{80,88},{96,104},{112,120},{... | collective-permute-start | bytes 1179656 | tf_op jit(solution)/shard_map/ppermute | solution.py:20
  38.7 0.0 copy-done
  38.7 0.0 copy-done.5
  38.7 0.0 copy-done.6
  38.7 0.0 copy-done.8
  38.7 1.3 %shard_map.144.part_ref = f32[2,3,16,256]{3,2,1,0:T(8,128)S(1)} custom-call(s32[3,16]{1,0:T(4,128)S(1)} %copy-done.5, s32[3,16]{1,0:T(4,128)S(1)} %copy-done.6, s32[3]{0:T(128)S(1)} %copy-done.8, f32[2,192,128]{2,1,0:T(8,128)S(1)} %shard_map.142.pair, f32[2,384,128]{2,1,0:T(8,128)S(1)} %constant_dynamic-update-slice_fusion.sides, f32[2,16,16,256]{3,2,1,0:T(8,128)S(1)} %copy-done), custom_call_target="tpu_custom_call" | custom-call | tf_op jit(solution)/shard_map/pallas_call | solution.py:253
  40.0 0.0 collective-permute-done.6.other
  40.0 1.7 %shard_map.145 = f32[2,3,16,256]{3,2,1,0:T(8,128)} custom-call(s32[3,16]{1,0:T(4,128)S(1)} %copy-done.5, s32[3,16]{1,0:T(4,128)S(1)} %copy-done.6, s32[3]{0:T(128)S(1)} %copy-done.8, f32[2,384,128]{2,1,0:T(8,128)S(1)} %collective-permute-done.6.other, f32[2,16,16,256]{3,2,1,0:T(8,128)S(1)} %copy-done, f32[2,3,16,256]{3,2,1,0:T(8,128)S(1)} %shard_map.144.part_ref), custom_call_target="tpu_custom_call" | custom-call | tf_op jit(solution)/shard_map/pallas_call | solution.py:264
  (5 shorter events, 0.1 us)
Async XLA Ops:
  0.6 5.7 %collective-permute-start = (f32[2,192,128]{2,1,0:T(8,128)}, f32[2,192,128]{2,1,0:T(8,128)S(1)}, u32[]{:S(2)}, u32[]{:S(2)}) collective-permute-start(f32[2,192,128]{2,1,0:T(8,128)} %bitcast.5), channel_id=1, source_target_pairs={{0,8},{16,24},{32,40},{48,56},{64,72},{80,88},{96,104},{112,120},{... | collective-permute-start | bytes 589832 | tf_op jit(solution)/shard_map/ppermute | solution.py:20
  3.2 14.7 %collective-permute-start.3 = (f32[2,192,128]{2,1,0:T(8,128)}, f32[2,192,128]{2,1,0:T(8,128)S(1)}, u32[]{:S(2)}, u32[]{:S(2)}) collective-permute-start(f32[2,192,128]{2,1,0:T(8,128)} %bitcast.6), channel_id=1, source_target_pairs={{8,16},{24,32},{40,48},{56,64},{72,80},{88,96},{104,112},{120,128}... | collective-permute-start | bytes 589832 | tf_op jit(solution)/shard_map/ppermute | solution.py:20
  6.3 1.0 %copy-start.1 = (f32[2,24,8,128]{3,2,1,0:T(8,128)S(1)}, f32[2,24,8,128]{3,2,1,0:T(8,128)}, u32[]{:S(2)}) copy-start(f32[2,24,8,128]{3,2,1,0:T(8,128)} %param.13) | copy-start | bytes 589828
  7.3 8.7 %copy-start.11 = (f32[8,16,256]{2,1,0:T(8,128)S(1)}, f32[8,16,256]{2,1,0:T(8,128)}, u32[]{:S(2)}) copy-start(f32[8,16,256]{2,1,0:T(8,128)} %param.25) | copy-start | bytes 393220
  7.4 10.5 %collective-permute-start.1 = (f32[2,2,48,128]{3,2,1,0:T(8,128)S(1)}, f32[2,2,48,128]{3,2,1,0:T(8,128)S(1)}, u32[]{:S(2)}, u32[]{:S(2)}) collective-permute-start(f32[2,2,48,128]{3,2,1,0:T(8,128)S(1)} %get-tuple-element.14), channel_id=1, source_target_pairs={{0,1},{2,3},{4,5},{6,7},{1,0},{3,2},{5,4},{7,6},{8,9},{10,11},{12,... | collective-permute-start | bytes 294920 | tf_op jit(solution)/shard_map/ppermute | solution.py:20
  9.4 7.1 %copy-start.4 = (f32[256,128]{1,0:T(8,128)S(1)}, f32[256,128]{1,0:T(8,128)}, u32[]{:S(2)}) copy-start(f32[256,128]{1,0:T(8,128)} %phi_ref.1) | copy-start | bytes 393220
  9.4 8.5 %copy-start.2 = (f32[2,24,8,128]{3,2,1,0:T(8,128)S(1)}, f32[2,24,8,128]{3,2,1,0:T(8,128)}, u32[]{:S(2)}) copy-start(f32[2,24,8,128]{3,2,1,0:T(8,128)} %param.13) | copy-start | bytes 589828
  9.4 8.5 %collective-permute-start.2 = (f32[2,2,48,128]{3,2,1,0:T(8,128)S(1)}, f32[2,2,48,128]{3,2,1,0:T(8,128)S(1)}, u32[]{:S(2)}, u32[]{:S(2)}) collective-permute-start(f32[2,2,48,128]{3,2,1,0:T(8,128)S(1)} %get-tuple-element.15), channel_id=1, source_target_pairs={{1,2},{3,4},{5,6},{2,1},{4,3},{6,5},{9,10},{11,12},{13,14},{10,9},... | collective-permute-start | bytes 294920 | tf_op jit(solution)/shard_map/ppermute | solution.py:20
  16.0 0.7 %copy-start.7 = (f32[16,4]{0,1:T(4,128)S(1)}, f32[16,4]{0,1:T(4,128)}, u32[]{:S(2)}) copy-start(f32[16,4]{0,1:T(4,128)} %param.23) | copy-start | bytes 772
  16.5 0.7 %copy-start.9 = (s32[16]{0:T(128)S(1)}, s32[16]{0:T(128)}, u32[]{:S(2)}) copy-start(s32[16]{0:T(128)} %start_ref.1) | copy-start | bytes 196
  18.0 9.2 %copy-start.12 = (s32[24,16]{0,1:T(8,128)S(1)}, s32[24,16]{0,1:T(8,128)}, u32[]{:S(2)}) copy-start(s32[24,16]{0,1:T(8,128)} %param.14) | copy-start | bytes 4612
  18.0 9.4 %copy-start.3 = (f32[2,16,8,128]{3,2,1,0:T(8,128)S(1)}, f32[2,16,8,128]{3,2,1,0:T(8,128)}, u32[]{:S(2)}) copy-start(f32[2,16,8,128]{3,2,1,0:T(8,128)} %param.20) | copy-start | bytes 393220
  19.6 7.7 %copy-start.13 = (s32[24,16]{0,1:T(8,128)S(1)}, s32[24,16]{0,1:T(8,128)}, u32[]{:S(2)}) copy-start(s32[24,16]{0,1:T(8,128)} %param.15) | copy-start | bytes 4612
  19.6 11.7 %collective-permute-start.5 = (f32[2,192,128]{2,1,0:T(8,128)S(1)}, f32[2,192,128]{2,1,0:T(8,128)S(1)}, u32[]{:S(2)}, u32[]{:S(2)}) collective-permute-start(f32[2,192,128]{2,1,0:T(8,128)S(1)} %shard_map.142.pair), channel_id=1, source_target_pairs={{8,16},{24,32},{40,48},{56,64},{72,80},{88,96},{104,112},{120,128}... | collective-permute-start | bytes 589832 | tf_op jit(solution)/shard_map/ppermute | solution.py:20
  24.1 9.6 %collective-permute-start.4 = (f32[2,192,128]{2,1,0:T(8,128)S(1)}, f32[2,192,128]{2,1,0:T(8,128)S(1)}, u32[]{:S(2)}, u32[]{:S(2)}) collective-permute-start(f32[2,192,128]{2,1,0:T(8,128)S(1)} %shard_map.142.pair), channel_id=1, source_target_pairs={{8,32},{24,48},{40,64},{56,80},{72,96},{88,112},{104,128},{120,144... | collective-permute-start | bytes 589832 | tf_op jit(solution)/shard_map/ppermute | solution.py:20
  27.3 0.7 %copy-start.10 = (s32[24]{0:T(128)S(1)}, s32[24]{0:T(128)}, u32[]{:S(2)}) copy-start(s32[24]{0:T(128)} %count_ref.3) | copy-start | bytes 292
  31.3 7.4 %copy-start = (f32[2,16,16,256]{3,2,1,0:T(8,128)S(1)}, f32[2,16,16,256]{3,2,1,0:T(8,128)}, u32[]{:S(2)}) copy-start(f32[2,16,16,256]{3,2,1,0:T(8,128)} %table.3) | copy-start | bytes 1572868
  33.7 5.0 %copy-start.5 = (s32[3,16]{1,0:T(4,128)S(1)}, s32[3,16]{1,0:T(4,128)}, u32[]{:S(2)}) copy-start(s32[3,16]{1,0:T(4,128)} %partner_ref.4) | copy-start | bytes 580
  33.7 5.0 %copy-start.6 = (s32[3,16]{1,0:T(4,128)S(1)}, s32[3,16]{1,0:T(4,128)}, u32[]{:S(2)}) copy-start(s32[3,16]{1,0:T(4,128)} %offset_ref.4) | copy-start | bytes 580
  33.7 5.0 %copy-start.8 = (s32[3]{0:T(128)S(1)}, s32[3]{0:T(128)}, u32[]{:S(2)}) copy-start(s32[3]{0:T(128)} %count_ref.5) | copy-start | bytes 40
  33.7 6.3 %collective-permute-start.6 = (f32[2,384,128]{2,1,0:T(8,128)S(1)}, f32[2,384,128]{2,1,0:T(8,128)S(1)}, u32[]{:S(2)}, u32[]{:S(2)}) collective-permute-start(f32[2,384,128]{2,1,0:T(8,128)S(1)} %constant_dynamic-update-slice_fusion.sides), channel_id=1, source_target_pairs={{0,8},{16,24},{32,40},{48,56},{64,72},{80,88},{96,104},{112,120},{... | collective-permute-start | bytes 1179656 | tf_op jit(solution)/shard_map/ppermute | solution.py:20

commit v5 on v4

--- a/solution.py
+++ b/solution.py
@@ -68,7 +68,46 @@
     return jnp.dot(x, y, preferred_element_type=jnp.float32)
 
 
-def matrices_kernel(start_ref, weight_ref, phi_ref, theta_ref, theta_low_ref, phi_out_ref, phi_low_ref):
+SINE = (-1 / 6, 1 / 120, -1 / 5040, 1 / 362880, -1 / 39916800, 1 / 6227020800)
+COSINE = (-1 / 2, 1 / 24, -1 / 720, 1 / 40320, -1 / 3628800, 1 / 479001600)
+
+
+def series(square, terms):
+    total = square * terms[-1]
+    for term in terms[-2::-1]:
+        total = square * (total + term)
+    return total + 1.0
+
+
+def prepare_kernel(
+    start,
+    weight,
+    pattern,
+    phi,
+    phase,
+    own_ref,
+    theta_ref,
+    theta_low_ref,
+    phi_out_ref,
+    phi_low_ref,
+    cos_ref,
+    sin_ref,
+    phi_ref,
+    start_ref,
+    weight_ref,
+    sems,
+):
+    copies = [
+        pltpu.make_async_copy(phi, phi_ref, sems.at[0]),
+        pltpu.make_async_copy(phase, sin_ref, sems.at[1]),
+        pltpu.make_async_copy(pattern, own_ref, sems.at[2]),
+        pltpu.make_async_copy(start, start_ref, sems.at[3]),
+        pltpu.make_async_copy(weight, weight_ref, sems.at[4]),
+    ]
+    for copy in copies[3:] + copies[:3]:
+        copy.start()
+    copies[3].wait()
+    copies[4].wait()
     samp = lax.axis_index("samp")
     line = lax.broadcasted_iota(jnp.int32, (16, 96), 0)
     column = lax.broadcasted_iota(jnp.int32, (16, 96), 1)
@@ -87,20 +126,43 @@
     high, low = split(theta)
     theta_ref[...] = jnp.concatenate([high, high], axis=1)
     theta_low_ref[...] = low
+    copies[0].wait()
     high, low = split(phi_ref[...].T)
     phi_out_ref[...] = jnp.concatenate([high, high], axis=0)
     phi_low_ref[...] = low
-
-
-def matrices(start, weight, phi):
-    shapes = ((128, 192), (128, 96), (256, 256), (128, 256))
-    return pl.pallas_call(
-        matrices_kernel,
-        out_shape=tuple(jax.ShapeDtypeStruct(s, jnp.bfloat16) for s in shapes),
-        in_specs=[spec(SMEM), spec(SMEM), spec(VMEM)],
-        out_specs=(spec(VMEM),) * 4,
-        compiler_params=PARAMS,
-    )(start, weight.T, phi)
+    copies[1].wait()
+    half = sin_ref[...] * 0.5
+    square = half * half
+    sine = half * series(square, SINE)
+    cos_ref[...] = 1.0 - 2.0 * sine * sine
+    sin_ref[...] = 2.0 * sine * series(square, COSINE)
+    copies[2].wait()
+
+
+def prepare(pattern, start, weight, phi, phase):
+    half, full = jnp.bfloat16, jnp.float32
+    shapes = (
+        ((2, 192, 128), full),
+        ((128, 192), half),
+        ((128, 96), half),
+        ((256, 256), half),
+        ((128, 256), half),
+        ((128, 256), full),
+        ((128, 256), full),
+    )
+    return pl.pallas_call(
+        prepare_kernel,
+        out_shape=tuple(jax.ShapeDtypeStruct(*s) for s in shapes),
+        in_specs=[spec(pl.ANY)] * 5,
+        out_specs=(spec(VMEM),) * 7,
+        scratch_shapes=[
+            pltpu.VMEM((256, 128), jnp.float32),
+            pltpu.SMEM((16,), jnp.int32),
+            pltpu.SMEM((4, 16), jnp.float32),
+            pltpu.SemaphoreType.DMA((5,)),
+        ],
+        compiler_params=PARAMS,
+    )(*(pltpu.with_memory_space_constraint(x, pltpu.HBM) for x in (start, weight.T, pattern, phi, phase)))
 
 
 def aggregate_kernel(
@@ -136,14 +198,14 @@
                     pair_ref[x, rows] = value[:, 128 * half : 128 * half + 128]
 
 
-def aggregate(own, inner, even, odd, mats, cosine, sine):
+def aggregate(own, inner, even, odd, mats):
     return pl.pallas_call(
         aggregate_kernel,
         out_shape=jax.ShapeDtypeStruct((2, 192, 128), jnp.float32),
         in_specs=[spec(VMEM)] * 10,
         out_specs=spec(VMEM),
         compiler_params=PARAMS,
-    )(own, inner, even, odd, *mats, cosine, sine)
+    )(own, inner, even, odd, *mats)
 
 
 def fine_kernel(partner_ref, offset_ref, count_ref, own, inner, outer, table, out_ref, window, operators, sems):
@@ -194,19 +256,23 @@
     )(partner, offset, count, pattern, inner, outer, table.reshape(2, 128, 128))
 
 
-def coarse_sums(window, table, partner_ref, offset_ref, count_ref, b, near):
+def coarse_codes(partner_ref, offset_ref, count_ref, b, j):
     me = lax.axis_index("box")
     odd = lax.rem(me, 2) == 1
-    base = (me // 2 - 2) * 6
+    place = partner_ref[b, j] - (me // 2 - 2) * 6
+    side = jnp.where(odd, place >= 12, place < 18)
+    place = jnp.where(place >= 24, place - 24, jnp.where(place >= 18, place - 12, place))
+    code = jnp.where(j < count_ref[b], place * 512 + offset_ref[b, j], -1)
+    return jnp.where(side, code, -1), jnp.where(side, -1, code)
+
+
+def coarse_sums(window, table, codes):
     sums = [None, None]
-    for j in range(16):
-        place = partner_ref[b, j] - base
-        side = jnp.where(odd, place >= 12, place < 18)
-        live = jnp.logical_and(j < count_ref[b], side if near else jnp.logical_not(side))
-        place = jnp.where(place >= 24, place - 24, jnp.where(place >= 18, place - 12, place))
-        place = pl.multiple_of(jnp.where(live, place, 0) * 32, 32)
-        scale = jnp.where(live, 1.0, 0.0)
-        which = offset_ref[b, j]
+    for code in codes:
+        scale = jnp.where(code >= 0, 1.0, 0.0)
+        code = jnp.maximum(code, 0)
+        which = lax.bitwise_and(code, 15)
+        place = pl.multiple_of(lax.shift_right_logical(code, 4), 32)
         for half in range(2):
             lanes = slice(128 * half, 128 * half + 128)
             a, c = table[0, which, :, lanes] * scale, table[1, which, :, lanes] * scale
@@ -217,7 +283,7 @@
     return [(s[0] - s[1], s[2] + s[3]) for s in sums]
 
 
-def near_kernel(partner_ref, offset_ref, count_ref, pair, sides, table, out_ref, window, sems):
+def near_kernel(partner_ref, offset_ref, count_ref, pair, sides, table, out_ref, code_ref, window, sems):
     copies = [
         pltpu.make_async_copy(sides, window.at[:, pl.ds(0, 384)], sems.at[0]),
         pltpu.make_async_copy(pair, window.at[:, pl.ds(384, 192)], sems.at[1]),
@@ -228,7 +294,12 @@
         copy.wait()
 
     def step(b, carry):
-        sums = coarse_sums(window, table, partner_ref, offset_ref, count_ref, b, True)
+        codes = []
+        for j in range(16):
+            near, far = coarse_codes(partner_ref, offset_ref, count_ref, b, j)
+            codes.append(near)
+            code_ref[b, j] = far
+        sums = coarse_sums(window, table, codes)
         for half in range(2):
             for x in range(2):
                 out_ref[x, b, :, 128 * half : 128 * half + 128] = sums[half][x]
@@ -237,9 +308,9 @@
     lax.fori_loop(0, 3, step, 0)
 
 
-def far_kernel(partner_ref, offset_ref, count_ref, other, table, part_ref, out_ref):
+def far_kernel(code_ref, other, table, part_ref, out_ref):
     def step(b, carry):
-        sums = coarse_sums(other, table, partner_ref, offset_ref, count_ref, b, False)
+        sums = coarse_sums(other, table, [code_ref[b, j] for j in range(16)])
         for half in range(2):
             lanes = slice(128 * half, 128 * half + 128)
             for x in range(2):
@@ -252,22 +323,25 @@
 def near_translate(pair, sides, table, partner, offset, count):
     return pl.pallas_call(
         near_kernel,
-        out_shape=jax.ShapeDtypeStruct((2, 3, 16, 256), jnp.float32),
+        out_shape=(
+            jax.ShapeDtypeStruct((2, 3, 16, 256), jnp.float32),
+            jax.ShapeDtypeStruct((3, 16), jnp.int32),
+        ),
         in_specs=[spec(SMEM)] * 3 + [spec(pl.ANY)] * 2 + [spec(VMEM)],
-        out_specs=spec(VMEM),
+        out_specs=(spec(VMEM), spec(SMEM)),
         scratch_shapes=[pltpu.VMEM((2, 576, 128), jnp.float32), pltpu.SemaphoreType.DMA((2,))],
         compiler_params=PARAMS,
     )(partner, offset, count, pair, sides, table)
 
 
-def far_translate(other, table, part, partner, offset, count):
+def far_translate(other, table, part, codes):
     return pl.pallas_call(
         far_kernel,
         out_shape=jax.ShapeDtypeStruct((2, 3, 16, 256), jnp.float32),
-        in_specs=[spec(SMEM)] * 3 + [spec(VMEM)] * 3,
+        in_specs=[spec(SMEM)] + [spec(VMEM)] * 3,
         out_specs=spec(VMEM),
         compiler_params=PARAMS,
-    )(partner, offset, count, other, table, part)
+    )(codes, other, table, part)
 
 
 def shards(
@@ -287,24 +361,24 @@
 ):
     pattern = fine_pattern.reshape(2, 192, 128)
     inner = swap_cores(pattern)
-    outer = swap_chips(pattern, 1, 1)
-    even, odd = rims(pattern, inner)
+    own, *mats = prepare(pattern, theta_start, theta_weight, phi_interp, shift_phase.reshape(128, 256))
+    inner, own, mats = lax.optimization_barrier((inner, own, mats))
+    even, odd = rims(own, inner)
+    even, odd, late = lax.optimization_barrier((even, odd, own))
+    outer = swap_chips(late, 1, 1)
     even, odd = swap_rims(even, 0), swap_rims(odd, 1)
-    mats = matrices(theta_start, theta_weight, phi_interp)
-    phase = shift_phase.reshape(128, 256)
-    even, odd, outer = lax.optimization_barrier((even, odd, outer))
-    pair = aggregate(pattern, inner, even, odd, mats, jnp.cos(phase), jnp.sin(phase))
+    pair = aggregate(own, inner, even, odd, mats)
     distant, next_to = swap_chips(pair, 1, 2), swap_chips(pair, 1, 1)
     fine_incoming = fine_translate(
-        pattern, inner, outer, fine_table, fine_partner, fine_offset, fine_count
+        own, inner, outer, fine_table, fine_partner, fine_offset, fine_count
     )
     distant, next_to, fine_incoming = lax.optimization_barrier((distant, next_to, fine_incoming))
     sides = jnp.concatenate([distant, next_to], axis=1)
     other = swap_cores(sides)
-    part = near_translate(pair, sides, coarse_table, coarse_partner, coarse_offset, coarse_count)
-    coarse_incoming = far_translate(
-        other, coarse_table, part, coarse_partner, coarse_offset, coarse_count
+    part, codes = near_translate(
+        pair, sides, coarse_table, coarse_partner, coarse_offset, coarse_count
     )
+    coarse_incoming = far_translate(other, coarse_table, part, codes)
     return (fine_incoming, coarse_incoming)
 
 

time: 42.1 us -> 40.6 us (0.964)
  local copies, waits for them, and re-layouts: 2.95 us -> 0.87 us
  Pallas kernels: 8.69 us -> 9.89 us
  starting transfers between devices: 26.8 us -> 26.1 us
    unnamed x31 -> x19, local copies, waits for them, and re-layouts: 2.47 us -> 0.85 us
    pallas_call x2, Pallas kernels: 2.07 us -> 3.39 us  [the longest x1 2.19 us: near_translate(): pl.pallas_call(near_kernel, out_shape=(jax.ShapeDtypeStruct((2, 3, 16, 25...]
    ppermute x7, starting transfers between devices: 26.8 us -> 26.1 us  [matched(): return lax.ppermute(x, axis, pairs + [(j, i) for i, j in pairs])]
    sin x1 -> x0, local copies, waits for them, and re-layouts: 0.46 us -> none  [shards(): jnp.sin(phase)]
  transfers between devices with their start and end apart: 7 -> 7, of which waited for: 1 -> 1; matrix products, arithmetic and copies ran while one was open for 1% -> 0% of each run, Pallas kernels for 13% -> 21%
where the time goes in v5:
time: 40.6 us; the launch traced here: 40.2 us
  starting transfers between devices  26.1 us (64%)
  Pallas kernels  9.89 us (24%)
  waiting for transfers between devices  2.42 us (6%)
  local copies, waits for them, and re-layouts  0.87 us (2%)
  between operations  0.87 us (2%)
    ppermute x7, starting transfers between devices, matched(): return lax.ppermute(x, axis, pairs + [(j, i) for i, j in pairs])  26.1 us
    pallas_call x1, Pallas kernels, fine_translate(): pl.pallas_call(fine_kernel, out_shape=jax.ShapeDtypeStruct((2, 24, 8, 128...  3.3 us
    ppermute x7, waiting for transfers between devices, matched(): return lax.ppermute(x, axis, pairs + [(j, i) for i, j in pairs])  2.42 us
    pallas_call x1, Pallas kernels, near_translate(): pl.pallas_call(near_kernel, out_shape=(jax.ShapeDtypeStruct((2, 3, 16, 25...  2.19 us
    pallas_call x1, Pallas kernels, far_translate(): pl.pallas_call(far_kernel, out_shape=jax.ShapeDtypeStruct((2, 3, 16, 256)...  1.59 us
    pallas_call x1, Pallas kernels, aggregate(): pl.pallas_call(aggregate_kernel, out_shape=jax.ShapeDtypeStruct((2, 192,...  1.57 us
    pallas_call x1, Pallas kernels, prepare(): pl.pallas_call(prepare_kernel, out_shape=tuple((jax.ShapeDtypeStruct(*s)...  1.21 us
    unnamed x19, local copies, waits for them, and re-layouts  0.85 us
  transfers between devices with their start and end apart: 7, of which 1 were waited for; matrix products, arithmetic and copies ran while one was open for 0% of the time, Pallas kernels for 21%

profile of v5, /device:TPU:199, one launch (start us, length us, event | category | flops | bytes accessed | tf_op | source)
XLA Modules:
  0.0 40.2 jit_solution(18328756052812457041)
XLA Ops:
  0.6 2.6 %collective-permute-start = (f32[2,192,128]{2,1,0:T(8,128)}, f32[2,192,128]{2,1,0:T(8,128)S(1)}, u32[]{:S(2)}, u32[]{:S(2)}) collective-permute-start(f32[2,192,128]{2,1,0:T(8,128)} %bitcast.5), channel_id=1, source_target_pairs={{0,8},{16,24},{32,40},{48,56},{64,72},{80,88},{96,104},{112,120},{... | collective-permute-start | bytes 589832 | tf_op jit(solution)/shard_map/ppermute | solution.py:20
  3.2 1.2 %shard_map.140 = (f32[2,192,128]{2,1,0:T(8,128)S(1)}, bf16[128,192]{1,0:T(8,128)(2,1)S(1)}, bf16[128,96]{1,0:T(8,128)(2,1)S(1)}, bf16[256,256]{1,0:T(8,128)(2,1)...) custom-call(s32[16]{0:T(128)} %start.1, f32[4,16]{1,0:T(4,128)} %bitcast.8, ...), custom_call_target="tpu_custom_call" | custom-call | tf_op jit(solution)/shard_map/pallas_call | solution.py:153
  4.4 0.0 collective-permute-done.inner_ref.inner
  4.5 0.0 copy-start.6
  4.5 1.9 %collective-permute-start.1 = (f32[2,2,48,128]{3,2,1,0:T(8,128)S(1)}, f32[2,2,48,128]{3,2,1,0:T(8,128)S(1)}, u32[]{:S(2)}, u32[]{:S(2)}) collective-permute-start(f32[2,2,48,128]{3,2,1,0:T(8,128)S(1)} %get-tuple-element.38), channel_id=1, source_target_pairs={{0,1},{2,3},{4,5},{6,7},{1,0},{3,2},{5,4},{7,6},{8,9},{10,11},{12,... | collective-permute-start | bytes 294920 | tf_op jit(solution)/shard_map/ppermute | solution.py:20
  6.5 6.4 %collective-permute-start.2 = (f32[2,2,48,128]{3,2,1,0:T(8,128)S(1)}, f32[2,2,48,128]{3,2,1,0:T(8,128)S(1)}, u32[]{:S(2)}, u32[]{:S(2)}) collective-permute-start(f32[2,2,48,128]{3,2,1,0:T(8,128)S(1)} %get-tuple-element.39), channel_id=1, source_target_pairs={{1,2},{3,4},{5,6},{2,1},{4,3},{6,5},{9,10},{11,12},{13,14},{10,9},... | collective-permute-start | bytes 294920 | tf_op jit(solution)/shard_map/ppermute | solution.py:20
  12.9 4.0 %collective-permute-start.5 = (f32[2,192,128]{2,1,0:T(8,128)S(1)}, f32[2,192,128]{2,1,0:T(8,128)S(1)}, u32[]{:S(2)}, u32[]{:S(2)}) collective-permute-start(f32[2,192,128]{2,1,0:T(8,128)S(1)} %get-tuple-element.46.own_ref.own), channel_id=1, source_target_pairs={{8,16},{24,32},{40,48},{56,64},{72,80},{88,96},{104,112},{120,128}... | collective-permute-start | bytes 589832 | tf_op jit(solution)/shard_map/ppermute | solution.py:20
  16.9 0.0 collective-permute-done.1.even_ref
  16.9 0.0 collective-permute-done.2.odd_ref
  16.9 0.0 copy-start.1
  16.9 1.6 %shard_map.142.pair = f32[2,192,128]{2,1,0:T(8,128)S(1)} custom-call(f32[2,192,128]{2,1,0:T(8,128)S(1)} %get-tuple-element.46.own_ref.own, f32[2,192,128]{2,1,0:T(8,128)S(1)} %collective-permute-done.inner_ref.inner, f32[2,2,48,128]{3,2,1,0:T(8,128)S(1)} %collective-permute-done.1.even_ref, f32[2,2,48,128]{3,2,1,0:T(8,128)S(1)} %collective-permute-done.2.odd_ref, ...), custom_call_target="tpu_custom_call" | custom-call | tf_op jit(solution)/shard_map/pallas_call | solution.py:202
  18.5 0.0 copy-start.7
  18.5 2.8 %collective-permute-start.4 = (f32[2,192,128]{2,1,0:T(8,128)S(1)}, f32[2,192,128]{2,1,0:T(8,128)S(1)}, u32[]{:S(2)}, u32[]{:S(2)}) collective-permute-start(f32[2,192,128]{2,1,0:T(8,128)S(1)} %shard_map.142.pair), channel_id=1, source_target_pairs={{8,16},{24,32},{40,48},{56,64},{72,80},{88,96},{104,112},{120,128}... | collective-permute-start | bytes 589832 | tf_op jit(solution)/shard_map/ppermute | solution.py:20
  21.3 3.8 %collective-permute-start.3 = (f32[2,192,128]{2,1,0:T(8,128)S(1)}, f32[2,192,128]{2,1,0:T(8,128)S(1)}, u32[]{:S(2)}, u32[]{:S(2)}) collective-permute-start(f32[2,192,128]{2,1,0:T(8,128)S(1)} %shard_map.142.pair), channel_id=1, source_target_pairs={{8,32},{24,48},{40,64},{56,80},{72,96},{88,112},{104,128},{120,144... | collective-permute-start | bytes 589832 | tf_op jit(solution)/shard_map/ppermute | solution.py:20
  25.1 0.0 copy-done.6
  25.1 0.1 copy.15.partner_ref
  25.2 0.0 copy-done.7
  25.2 0.1 copy.16.offset_ref
  25.3 0.0 copy-start.4
  25.3 0.0 collective-permute-done.5.outer
  25.3 0.0 copy-done.1
  25.3 0.6 %copy-done.4 = s32[24]{0:T(128)S(1)} copy-done((s32[24]{0:T(128)S(1)}, s32[24]{0:T(128)}, u32[]{:S(2)}) %copy-start.4) | copy-done | bytes 120
  25.9 3.3 %shard_map.143 = f32[2,24,8,128]{3,2,1,0:T(8,128)} custom-call(s32[24,16]{1,0:T(8,128)S(1)} %copy.15.partner_ref, s32[24,16]{1,0:T(8,128)S(1)} %copy.16.offset_ref, s32[24]{0:T(128)S(1)} %copy-done.4, f32[2,192,128]{2,1,0:T(8,128)S(1)} %get-tuple-element.46.own_ref.own, f32[2,192,128]{2,1,0:T(8,128)S(1)} %collective-permute-done.inner_ref.inner, ...), custom_call_target="tpu_custom_call" | custom-call | flops 4000000 | bytes 40000000 | tf_op jit(solution)/shard_map/pallas_call | solution.py:244
  29.2 0.0 copy-start
  29.2 0.0 collective-permute-done.4
  29.3 2.4 %collective-permute-done.3 = f32[2,192,128]{2,1,0:T(8,128)S(1)} collective-permute-done((f32[2,192,128]{2,1,0:T(8,128)S(1)}, f32[2,192,128]{2,1,0:T(8,128)S(1)}, u32[]{:S(2)}, u32[]{:S(2)}) %collective-permute-start.3) | collective-permute-done | bytes 196640 | tf_op jit(solution)/shard_map/ppermute | solution.py:20
  31.6 0.0 copy-start.2
  31.6 0.0 copy-start.3
  31.7 0.0 copy-start.5
  31.7 4.7 %collective-permute-start.6 = (f32[2,384,128]{2,1,0:T(8,128)S(1)}, f32[2,384,128]{2,1,0:T(8,128)S(1)}, u32[]{:S(2)}, u32[]{:S(2)}) collective-permute-start(f32[2,384,128]{2,1,0:T(8,128)S(1)} %constant_dynamic-update-slice_fusion.sides), channel_id=1, source_target_pairs={{0,8},{16,24},{32,40},{48,56},{64,72},{80,88},{96,104},{112,120},{... | collective-permute-start | bytes 1179656 | tf_op jit(solution)/shard_map/ppermute | solution.py:20
  36.4 0.0 copy-done
  36.4 0.0 copy-done.2
  36.4 0.0 copy-done.3
  36.4 0.0 copy-done.5
  36.4 2.2 %shard_map.144 = (f32[2,3,16,256]{3,2,1,0:T(8,128)S(1)}, s32[3,16]{1,0:T(4,128)S(1)}) custom-call(s32[3,16]{1,0:T(4,128)S(1)} %copy-done.2, s32[3,16]{1,0:T(4,128)S(1)} %copy-done.3, s32[3]{0:T(128)S(1)} %copy-done.5, f32[2,192,128]{2,1,0:T(8,128)S(1)} %shard_map.142.pair, f32[2,384,128]{2,1,0:T(8,128)S(1)} %constant_dynamic-update-slice_fusion.sides, ...), custom_call_target="tpu_custom_call" | custom-call | tf_op jit(solution)/shard_map/pallas_call | solution.py:324
  38.6 0.0 collective-permute-done.6.other
  38.6 1.6 %shard_map.145 = f32[2,3,16,256]{3,2,1,0:T(8,128)} custom-call(s32[3,16]{1,0:T(4,128)S(1)} %get-tuple-element.50.code_ref, f32[2,384,128]{2,1,0:T(8,128)S(1)} %collective-permute-done.6.other, f32[2,16,16,256]{3,2,1,0:T(8,128)S(1)} %copy-done, f32[2,3,16,256]{3,2,1,0:T(8,128)S(1)} %get-tuple-element.51.part_ref), custom_call_target="tpu_custom_call" | custom-call | tf_op jit(solution)/shard_map/pallas_call | solution.py:338
  (3 shorter events, 0.1 us)
Async XLA Ops:
  0.6 3.9 %collective-permute-start = (f32[2,192,128]{2,1,0:T(8,128)}, f32[2,192,128]{2,1,0:T(8,128)S(1)}, u32[]{:S(2)}, u32[]{:S(2)}) collective-permute-start(f32[2,192,128]{2,1,0:T(8,128)} %bitcast.5), channel_id=1, source_target_pairs={{0,8},{16,24},{32,40},{48,56},{64,72},{80,88},{96,104},{112,120},{... | collective-permute-start | bytes 589832 | tf_op jit(solution)/shard_map/ppermute | solution.py:20
  4.5 20.6 %copy-start.6 = (s32[24,16]{0,1:T(8,128)S(1)}, s32[24,16]{0,1:T(8,128)}, u32[]{:S(2)}) copy-start(s32[24,16]{0,1:T(8,128)} %param.14) | copy-start | bytes 4612
  4.5 12.4 %collective-permute-start.1 = (f32[2,2,48,128]{3,2,1,0:T(8,128)S(1)}, f32[2,2,48,128]{3,2,1,0:T(8,128)S(1)}, u32[]{:S(2)}, u32[]{:S(2)}) collective-permute-start(f32[2,2,48,128]{3,2,1,0:T(8,128)S(1)} %get-tuple-element.38), channel_id=1, source_target_pairs={{0,1},{2,3},{4,5},{6,7},{1,0},{3,2},{5,4},{7,6},{8,9},{10,11},{12,... | collective-permute-start | bytes 294920 | tf_op jit(solution)/shard_map/ppermute | solution.py:20
  6.5 10.4 %collective-permute-start.2 = (f32[2,2,48,128]{3,2,1,0:T(8,128)S(1)}, f32[2,2,48,128]{3,2,1,0:T(8,128)S(1)}, u32[]{:S(2)}, u32[]{:S(2)}) collective-permute-start(f32[2,2,48,128]{3,2,1,0:T(8,128)S(1)} %get-tuple-element.39), channel_id=1, source_target_pairs={{1,2},{3,4},{5,6},{2,1},{4,3},{6,5},{9,10},{11,12},{13,14},{10,9},... | collective-permute-start | bytes 294920 | tf_op jit(solution)/shard_map/ppermute | solution.py:20
  12.9 12.4 %collective-permute-start.5 = (f32[2,192,128]{2,1,0:T(8,128)S(1)}, f32[2,192,128]{2,1,0:T(8,128)S(1)}, u32[]{:S(2)}, u32[]{:S(2)}) collective-permute-start(f32[2,192,128]{2,1,0:T(8,128)S(1)} %get-tuple-element.46.own_ref.own), channel_id=1, source_target_pairs={{8,16},{24,32},{40,48},{56,64},{72,80},{88,96},{104,112},{120,128}... | collective-permute-start | bytes 589832 | tf_op jit(solution)/shard_map/ppermute | solution.py:20
  16.9 8.4 %copy-start.1 = (f32[2,16,8,128]{3,2,1,0:T(8,128)S(1)}, f32[2,16,8,128]{3,2,1,0:T(8,128)}, u32[]{:S(2)}) copy-start(f32[2,16,8,128]{3,2,1,0:T(8,128)} %param.20) | copy-start | bytes 393220
  18.5 6.7 %copy-start.7 = (s32[24,16]{0,1:T(8,128)S(1)}, s32[24,16]{0,1:T(8,128)}, u32[]{:S(2)}) copy-start(s32[24,16]{0,1:T(8,128)} %param.15) | copy-start | bytes 4612
  18.5 10.7 %collective-permute-start.4 = (f32[2,192,128]{2,1,0:T(8,128)S(1)}, f32[2,192,128]{2,1,0:T(8,128)S(1)}, u32[]{:S(2)}, u32[]{:S(2)}) collective-permute-start(f32[2,192,128]{2,1,0:T(8,128)S(1)} %shard_map.142.pair), channel_id=1, source_target_pairs={{8,16},{24,32},{40,48},{56,64},{72,80},{88,96},{104,112},{120,128}... | collective-permute-start | bytes 589832 | tf_op jit(solution)/shard_map/ppermute | solution.py:20
  21.3 10.3 %collective-permute-start.3 = (f32[2,192,128]{2,1,0:T(8,128)S(1)}, f32[2,192,128]{2,1,0:T(8,128)S(1)}, u32[]{:S(2)}, u32[]{:S(2)}) collective-permute-start(f32[2,192,128]{2,1,0:T(8,128)S(1)} %shard_map.142.pair), channel_id=1, source_target_pairs={{8,32},{24,48},{40,64},{56,80},{72,96},{88,112},{104,128},{120,144... | collective-permute-start | bytes 589832 | tf_op jit(solution)/shard_map/ppermute | solution.py:20
  25.3 0.7 %copy-start.4 = (s32[24]{0:T(128)S(1)}, s32[24]{0:T(128)}, u32[]{:S(2)}) copy-start(s32[24]{0:T(128)} %count_ref.2) | copy-start | bytes 292
  29.2 7.1 %copy-start = (f32[2,16,16,256]{3,2,1,0:T(8,128)S(1)}, f32[2,16,16,256]{3,2,1,0:T(8,128)}, u32[]{:S(2)}) copy-start(f32[2,16,16,256]{3,2,1,0:T(8,128)} %table.3) | copy-start | bytes 1572868
  31.6 4.7 %copy-start.2 = (s32[3,16]{1,0:T(4,128)S(1)}, s32[3,16]{1,0:T(4,128)}, u32[]{:S(2)}) copy-start(s32[3,16]{1,0:T(4,128)} %partner_ref.2) | copy-start | bytes 580
  31.6 4.7 %copy-start.3 = (s32[3,16]{1,0:T(4,128)S(1)}, s32[3,16]{1,0:T(4,128)}, u32[]{:S(2)}) copy-start(s32[3,16]{1,0:T(4,128)} %offset_ref.2) | copy-start | bytes 580
  31.7 4.7 %copy-start.5 = (s32[3]{0:T(128)S(1)}, s32[3]{0:T(128)}, u32[]{:S(2)}) copy-start(s32[3]{0:T(128)} %count_ref.3) | copy-start | bytes 40
  31.7 6.9 %collective-permute-start.6 = (f32[2,384,128]{2,1,0:T(8,128)S(1)}, f32[2,384,128]{2,1,0:T(8,128)S(1)}, u32[]{:S(2)}, u32[]{:S(2)}) collective-permute-start(f32[2,384,128]{2,1,0:T(8,128)S(1)} %constant_dynamic-update-slice_fusion.sides), channel_id=1, source_target_pairs={{0,8},{16,24},{32,40},{48,56},{64,72},{80,88},{96,104},{112,120},{... | collective-permute-start | bytes 1179656 | tf_op jit(solution)/shard_map/ppermute | solution.py:20

commit v6 on v5

--- a/solution.py
+++ b/solution.py
@@ -162,7 +162,7 @@
             pltpu.SemaphoreType.DMA((5,)),
         ],
         compiler_params=PARAMS,
-    )(*(pltpu.with_memory_space_constraint(x, pltpu.HBM) for x in (start, weight.T, pattern, phi, phase)))
+    )(*in_hbm(start, weight.T, pattern, phi, phase))
 
 
 def aggregate_kernel(
@@ -208,15 +208,36 @@
     )(own, inner, even, odd, *mats)
 
 
-def fine_kernel(partner_ref, offset_ref, count_ref, own, inner, outer, table, out_ref, window, operators, sems):
+def fine_kernel(
+    partner,
+    offset,
+    count,
+    table,
+    own,
+    inner,
+    outer,
+    out,
+    window,
+    operators,
+    value_ref,
+    partner_ref,
+    offset_ref,
+    count_ref,
+    sems,
+    out_sems,
+):
     me = lax.axis_index("box")
     odd = lax.rem(me, 2)
-    copies = [
-        pltpu.make_async_copy(own, window.at[:, pl.ds(192, 192)], sems.at[0]),
-        pltpu.make_async_copy(inner, window.at[:, pl.ds(384 * (1 - odd), 192)], sems.at[1]),
-        pltpu.make_async_copy(outer, window.at[:, pl.ds(384 * odd, 192)], sems.at[2]),
-        pltpu.make_async_copy(table, operators.at[:, pl.ds(0, 128)], sems.at[3]),
-    ]
+    moves = (
+        (partner, partner_ref),
+        (offset, offset_ref),
+        (count, count_ref),
+        (table, operators.at[:, pl.ds(0, 128)]),
+        (own, window.at[:, pl.ds(192, 192)]),
+        (inner, window.at[:, pl.ds(384 * (1 - odd), 192)]),
+        (outer, window.at[:, pl.ds(384 * odd, 192)]),
+    )
+    copies = [pltpu.make_async_copy(*move, sems.at[i]) for i, move in enumerate(moves)]
     for copy in copies:
         copy.start()
     operators[:, 128:] = jnp.zeros((2, 8, 128), jnp.float32)
@@ -227,79 +248,86 @@
     def step(b, carry):
         sums = None
         for j in range(16):
-            place = pl.multiple_of((partner_ref[b, j] - base) * 8, 8)
-            which = pl.multiple_of(jnp.where(j < count_ref[b], offset_ref[b, j], 16) * 8, 8)
+            place = pl.multiple_of((partner_ref[j, b] - base) * 8, 8)
+            which = pl.multiple_of(jnp.where(j < count_ref[b], offset_ref[j, b], 16) * 8, 8)
             a, c = operators[0, pl.ds(which, 8)], operators[1, pl.ds(which, 8)]
             f, g = window[0, pl.ds(place, 8)], window[1, pl.ds(place, 8)]
             terms = (a * f, c * g, a * g, c * f)
             sums = terms if sums is None else tuple(s + t for s, t in zip(sums, terms))
-        out_ref[0, b] = sums[0] - sums[1]
-        out_ref[1, b] = sums[2] + sums[3]
+        value_ref[0, b] = sums[0] - sums[1]
+        value_ref[1, b] = sums[2] + sums[3]
         return carry
 
-    lax.fori_loop(0, 24, step, 0)
+    copies = []
+    for part in range(3):
+        lax.fori_loop(8 * part, 8 * part + 8, step, 0)
+        boxes = pl.ds(8 * part, 8)
+        copies.append(pltpu.make_async_copy(value_ref.at[:, boxes], out.at[:, boxes], out_sems.at[part]))
+        copies[part].start()
+    for copy in copies:
+        copy.wait()
+
+
+def in_hbm(*arrays):
+    return tuple(pltpu.with_memory_space_constraint(x, pltpu.HBM) for x in arrays)
 
 
 def fine_translate(pattern, inner, outer, table, partner, offset, count):
     return pl.pallas_call(
         fine_kernel,
         out_shape=jax.ShapeDtypeStruct((2, 24, 8, 128), jnp.float32),
-        in_specs=[spec(SMEM)] * 3 + [spec(pl.ANY)] * 4,
-        out_specs=spec(VMEM),
+        in_specs=[spec(pl.ANY)] * 7,
+        out_specs=spec(pl.ANY),
         scratch_shapes=[
             pltpu.VMEM((2, 576, 128), jnp.float32),
             pltpu.VMEM((2, 136, 128), jnp.float32),
-            pltpu.SemaphoreType.DMA((4,)),
+            pltpu.VMEM((2, 24, 8, 128), jnp.float32),
+            pltpu.SMEM((16, 24), jnp.int32),
+            pltpu.SMEM((16, 24), jnp.int32),
+            pltpu.SMEM((24,), jnp.int32),
+            pltpu.SemaphoreType.DMA((7,)),
+            pltpu.SemaphoreType.DMA((3,)),
         ],
         compiler_params=PARAMS,
-        cost_estimate=pl.CostEstimate(flops=4_000_000, bytes_accessed=40_000_000, transcendentals=0),
-    )(partner, offset, count, pattern, inner, outer, table.reshape(2, 128, 128))
-
-
-def coarse_codes(partner_ref, offset_ref, count_ref, b, j):
-    me = lax.axis_index("box")
-    odd = lax.rem(me, 2) == 1
-    place = partner_ref[b, j] - (me // 2 - 2) * 6
-    side = jnp.where(odd, place >= 12, place < 18)
-    place = jnp.where(place >= 24, place - 24, jnp.where(place >= 18, place - 12, place))
-    code = jnp.where(j < count_ref[b], place * 512 + offset_ref[b, j], -1)
-    return jnp.where(side, code, -1), jnp.where(side, -1, code)
-
-
-def coarse_sums(window, table, codes):
+        cost_estimate=pl.CostEstimate(flops=4_000_000, bytes_accessed=4_000_000, transcendentals=0),
+    )(*in_hbm(partner.T, offset.T, count, table.reshape(2, 128, 128)), pattern, inner, outer)
+
+
+def coarse_box(b, partner_ref, offset_ref, count_ref):
+    base = (lax.axis_index("box") // 2 - 2) * 6
+    return [(j < count_ref[b], partner_ref[b, j] - base, offset_ref[b, j]) for j in range(16)]
+
+
+def coarse_sums(window, table, slots):
     sums = [None, None]
-    for code in codes:
-        scale = jnp.where(code >= 0, 1.0, 0.0)
-        code = jnp.maximum(code, 0)
-        which = lax.bitwise_and(code, 15)
-        place = pl.multiple_of(lax.shift_right_logical(code, 4), 32)
+    for live, place, which in slots:
+        place = pl.multiple_of(jnp.where(live, place, 0) * 32, 32)
+        scale = jnp.where(live, 1.0, 0.0)
         for half in range(2):
             lanes = slice(128 * half, 128 * half + 128)
+            rows = pl.ds(place + 16 * half, 16)
             a, c = table[0, which, :, lanes] * scale, table[1, which, :, lanes] * scale
-            f, g = window[0, pl.ds(place + 16 * half, 16)], window[1, pl.ds(place + 16 * half, 16)]
+            f, g = window[0, rows], window[1, rows]
             terms = (a * f, c * g, a * g, c * f)
             old = sums[half]
             sums[half] = terms if old is None else tuple(s + t for s, t in zip(old, terms))
     return [(s[0] - s[1], s[2] + s[3]) for s in sums]
 
 
-def near_kernel(partner_ref, offset_ref, count_ref, pair, sides, table, out_ref, code_ref, window, sems):
-    copies = [
-        pltpu.make_async_copy(sides, window.at[:, pl.ds(0, 384)], sems.at[0]),
-        pltpu.make_async_copy(pair, window.at[:, pl.ds(384, 192)], sems.at[1]),
-    ]
-    for copy in copies:
-        copy.start()
-    for copy in copies:
-        copy.wait()
+def first_kernel(partner_ref, offset_ref, count_ref, table, pair_ref, out_ref, dense_ref):
+    odd = lax.rem(lax.axis_index("box"), 2) == 1
+    dense_ref[...] = jnp.zeros(dense_ref.shape, jnp.float32)
 
     def step(b, carry):
-        codes = []
-        for j in range(16):
-            near, far = coarse_codes(partner_ref, offset_ref, count_ref, b, j)
-            codes.append(near)
-            code_ref[b, j] = far
-        sums = coarse_sums(window, table, codes)
+        slots = []
+        for live, box, which in coarse_box(b, partner_ref, offset_ref, count_ref):
+            far = jnp.logical_and(live, jnp.where(odd, box < 12, box >= 18))
+            place = jnp.where(odd, jnp.where(box >= 6, box - 6, box + 6), box - 18)
+            row = pl.multiple_of(jnp.where(far, b * 12 + place, 36) * 16, 16)
+            for x in range(2):
+                dense_ref[x, pl.ds(row, 16)] = table[x, which]
+            slots.append((live & (box >= 12) & (box < 18), box - 12, which))
+        sums = coarse_sums(pair_ref, table, slots)
         for half in range(2):
             for x in range(2):
                 out_ref[x, b, :, 128 * half : 128 * half + 128] = sums[half][x]
@@ -308,9 +336,15 @@
     lax.fori_loop(0, 3, step, 0)
 
 
-def far_kernel(code_ref, other, table, part_ref, out_ref):
+def second_kernel(partner_ref, offset_ref, count_ref, table, sides_ref, part_ref, out_ref):
+    odd = lax.rem(lax.axis_index("box"), 2) == 1
+
     def step(b, carry):
-        sums = coarse_sums(other, table, [code_ref[b, j] for j in range(16)])
+        slots = []
+        for live, box, which in coarse_box(b, partner_ref, offset_ref, count_ref):
+            place = jnp.where(odd, box - 18, jnp.where(box >= 6, box - 6, box + 6))
+            slots.append((jnp.logical_and(live, jnp.where(odd, box >= 18, box < 12)), place, which))
+        sums = coarse_sums(sides_ref, table, slots)
         for half in range(2):
             lanes = slice(128 * half, 128 * half + 128)
             for x in range(2):
@@ -320,28 +354,64 @@
     lax.fori_loop(0, 3, step, 0)
 
 
-def near_translate(pair, sides, table, partner, offset, count):
-    return pl.pallas_call(
-        near_kernel,
+def far_kernel(other, dense, part, out, value_ref, sems):
+    copies = []
+    for half in range(2):
+        for top in (0, 8):
+            lanes, lines = pl.ds(128 * half, 128), pl.ds(top, 8)
+            sums = [(part[0, b, lines, lanes], part[1, b, lines, lanes]) for b in range(3)]
+            for s in range(12):
+                rows = pl.ds(32 * s + 16 * half + top, 8)
+                f, g = other[0, rows], other[1, rows]
+                for b in range(3):
+                    places = pl.ds((12 * b + s) * 16 + top, 8)
+                    a, c = dense[0, places, lanes], dense[1, places, lanes]
+                    sums[b] = (sums[b][0] + (a * f - c * g), sums[b][1] + (a * g + c * f))
+            for b in range(3):
+                for x in range(2):
+                    value_ref[x, b, lines, lanes] = sums[b][x]
+            copies.append(
+                pltpu.make_async_copy(
+                    value_ref.at[:, :, lines, lanes], out.at[:, :, lines, lanes], sems.at[len(copies)]
+                )
+            )
+            copies[-1].start()
+    for copy in copies:
+        copy.wait()
+
+
+def first_translate(lists, table, pair):
+    return pl.pallas_call(
+        first_kernel,
         out_shape=(
             jax.ShapeDtypeStruct((2, 3, 16, 256), jnp.float32),
-            jax.ShapeDtypeStruct((3, 16), jnp.int32),
+            jax.ShapeDtypeStruct((2, 37 * 16, 256), jnp.float32),
         ),
-        in_specs=[spec(SMEM)] * 3 + [spec(pl.ANY)] * 2 + [spec(VMEM)],
-        out_specs=(spec(VMEM), spec(SMEM)),
-        scratch_shapes=[pltpu.VMEM((2, 576, 128), jnp.float32), pltpu.SemaphoreType.DMA((2,))],
-        compiler_params=PARAMS,
-    )(partner, offset, count, pair, sides, table)
-
-
-def far_translate(other, table, part, codes):
+        in_specs=[spec(SMEM)] * 3 + [spec(VMEM)] * 2,
+        out_specs=(spec(VMEM), spec(VMEM)),
+        compiler_params=PARAMS,
+    )(*lists, table, pair)
+
+
+def second_translate(lists, table, sides, part):
+    return pl.pallas_call(
+        second_kernel,
+        out_shape=jax.ShapeDtypeStruct((2, 3, 16, 256), jnp.float32),
+        in_specs=[spec(SMEM)] * 3 + [spec(VMEM)] * 3,
+        out_specs=spec(VMEM),
+        compiler_params=PARAMS,
+    )(*lists, table, sides, part)
+
+
+def far_translate(other, dense, part):
     return pl.pallas_call(
         far_kernel,
         out_shape=jax.ShapeDtypeStruct((2, 3, 16, 256), jnp.float32),
-        in_specs=[spec(SMEM)] + [spec(VMEM)] * 3,
-        out_specs=spec(VMEM),
-        compiler_params=PARAMS,
-    )(codes, other, table, part)
+        in_specs=[spec(VMEM)] * 3,
+        out_specs=spec(pl.ANY),
+        scratch_shapes=[pltpu.VMEM((2, 3, 16, 256), jnp.float32), pltpu.SemaphoreType.DMA((4,))],
+        compiler_params=PARAMS,
+    )(other, dense, part)
 
 
 def shards(
@@ -368,17 +438,18 @@
     outer = swap_chips(late, 1, 1)
     even, odd = swap_rims(even, 0), swap_rims(odd, 1)
     pair = aggregate(own, inner, even, odd, mats)
-    distant, next_to = swap_chips(pair, 1, 2), swap_chips(pair, 1, 1)
+    next_to, distant = swap_chips(pair, 1, 1), swap_chips(pair, 1, 2)
     fine_incoming = fine_translate(
         own, inner, outer, fine_table, fine_partner, fine_offset, fine_count
     )
-    distant, next_to, fine_incoming = lax.optimization_barrier((distant, next_to, fine_incoming))
-    sides = jnp.concatenate([distant, next_to], axis=1)
+    lists = (coarse_partner, coarse_offset, coarse_count)
+    part, dense = first_translate(lists, coarse_table, pair)
+    distant, fine_incoming, part, dense = lax.optimization_barrier((distant, fine_incoming, part, dense))
+    next_to, distant = lax.optimization_barrier((next_to, distant))
+    sides = jnp.concatenate([next_to, distant], axis=1)
     other = swap_cores(sides)
-    part, codes = near_translate(
-        pair, sides, coarse_table, coarse_partner, coarse_offset, coarse_count
-    )
-    coarse_incoming = far_translate(other, coarse_table, part, codes)
+    part = second_translate(lists, coarse_table, sides, part)
+    coarse_incoming = far_translate(other, dense, part)
     return (fine_incoming, coarse_incoming)
 
 

time: 40.6 us -> 38.1 us (0.938)
  waiting for transfers between devices: 2.42 us -> 0.33 us
  local copies, waits for them, and re-layouts: 0.87 us -> 0.05 us
  starting transfers between devices: 26.1 us -> 26.9 us
    ppermute x7, waiting for transfers between devices: 2.42 us -> 0.33 us  [matched(): return lax.ppermute(x, axis, pairs + [(j, i) for i, j in pairs])]
    unnamed x19 -> x9, local copies, waits for them, and re-layouts: 0.85 us -> 0.03 us
    ppermute x7, starting transfers between devices: 26.1 us -> 26.9 us  [matched(): return lax.ppermute(x, axis, pairs + [(j, i) for i, j in pairs])]
    pallas_call x1, Pallas kernels: 1.59 us -> 0.88 us  [far_translate(): pl.pallas_call(far_kernel, out_shape=jax.ShapeDtypeStruct((2, 3, 16, 256)...]
    pallas_call x1 -> x2, Pallas kernels: 2.19 us -> 2.9 us  [the longest x1 1.57 us: first_translate(): pl.pallas_call(first_kernel, out_shape=(jax.ShapeDtypeStruct((2, 3, 16, 2...]
  transfers between devices with their start and end apart: 7 -> 7, of which waited for: 1 -> 1; matrix products, arithmetic and copies ran while one was open for 0% -> 0% of each run, Pallas kernels for 21% -> 23%
where the time goes in v6:
time: 38.1 us; the launch traced here: 37.7 us
  starting transfers between devices  26.9 us (71%)
  Pallas kernels  9.56 us (25%)
  between operations  0.83 us (2%)
    ppermute x7, starting transfers between devices, matched(): return lax.ppermute(x, axis, pairs + [(j, i) for i, j in pairs])  26.9 us
    pallas_call x1, Pallas kernels, fine_translate(): pl.pallas_call(fine_kernel, out_shape=jax.ShapeDtypeStruct((2, 24, 8, 128...  2.96 us
    pallas_call x1, Pallas kernels, aggregate(): pl.pallas_call(aggregate_kernel, out_shape=jax.ShapeDtypeStruct((2, 192,...  1.58 us
    pallas_call x1, Pallas kernels, first_translate(): pl.pallas_call(first_kernel, out_shape=(jax.ShapeDtypeStruct((2, 3, 16, 2...  1.57 us
    pallas_call x1, Pallas kernels, second_translate(): pl.pallas_call(second_kernel, out_shape=jax.ShapeDtypeStruct((2, 3, 16, 2...  1.33 us
    pallas_call x1, Pallas kernels, prepare(): pl.pallas_call(prepare_kernel, out_shape=tuple((jax.ShapeDtypeStruct(*s)...  1.21 us
    pallas_call x1, Pallas kernels, far_translate(): pl.pallas_call(far_kernel, out_shape=jax.ShapeDtypeStruct((2, 3, 16, 256)...  0.88 us
  transfers between devices with their start and end apart: 7, of which 1 were waited for; matrix products, arithmetic and copies ran while one was open for 0% of the time, Pallas kernels for 23%

profile of v6, /device:TPU:199, one launch (start us, length us, event | category | flops | bytes accessed | tf_op | source)
XLA Modules:
  0.0 37.7 jit_solution(11380240891468092679)
XLA Ops:
  0.6 0.0 copy-start
  0.6 0.0 copy-start.3
  0.7 0.0 copy-start.2
  0.7 0.0 copy-start.1
  0.7 2.7 %collective-permute-start = (f32[2,192,128]{2,1,0:T(8,128)}, f32[2,192,128]{2,1,0:T(8,128)S(1)}, u32[]{:S(2)}, u32[]{:S(2)}) collective-permute-start(f32[2,192,128]{2,1,0:T(8,128)} %bitcast.6), channel_id=1, source_target_pairs={{0,8},{16,24},{32,40},{48,56},{64,72},{80,88},{96,104},{112,120},{... | collective-permute-start | bytes 589832 | tf_op jit(solution)/shard_map/ppermute | solution.py:20
  3.4 1.2 %shard_map.140 = (f32[2,192,128]{2,1,0:T(8,128)S(1)}, bf16[128,192]{1,0:T(8,128)(2,1)S(1)}, bf16[128,96]{1,0:T(8,128)(2,1)S(1)}, bf16[256,256]{1,0:T(8,128)(2,1)...) custom-call(s32[16]{0:T(128)} %start.1, f32[4,16]{1,0:T(4,128)} %bitcast.12, ...), custom_call_target="tpu_custom_call" | custom-call | tf_op jit(solution)/shard_map/pallas_call | solution.py:153
  4.6 0.0 collective-permute-done.inner_ref.inner
  4.7 1.9 %collective-permute-start.1 = (f32[2,2,48,128]{3,2,1,0:T(8,128)S(1)}, f32[2,2,48,128]{3,2,1,0:T(8,128)S(1)}, u32[]{:S(2)}, u32[]{:S(2)}) collective-permute-start(f32[2,2,48,128]{3,2,1,0:T(8,128)S(1)} %get-tuple-element.41), channel_id=1, source_target_pairs={{0,1},{2,3},{4,5},{6,7},{1,0},{3,2},{5,4},{7,6},{8,9},{10,11},{12,... | collective-permute-start | bytes 294920 | tf_op jit(solution)/shard_map/ppermute | solution.py:20
  6.6 6.4 %collective-permute-start.2 = (f32[2,2,48,128]{3,2,1,0:T(8,128)S(1)}, f32[2,2,48,128]{3,2,1,0:T(8,128)S(1)}, u32[]{:S(2)}, u32[]{:S(2)}) collective-permute-start(f32[2,2,48,128]{3,2,1,0:T(8,128)S(1)} %get-tuple-element.42), channel_id=1, source_target_pairs={{1,2},{3,4},{5,6},{2,1},{4,3},{6,5},{9,10},{11,12},{13,14},{10,9},... | collective-permute-start | bytes 294920 | tf_op jit(solution)/shard_map/ppermute | solution.py:20
  13.0 4.0 %collective-permute-start.4 = (f32[2,192,128]{2,1,0:T(8,128)S(1)}, f32[2,192,128]{2,1,0:T(8,128)S(1)}, u32[]{:S(2)}, u32[]{:S(2)}) collective-permute-start(f32[2,192,128]{2,1,0:T(8,128)S(1)} %get-tuple-element.49.own_ref.own), channel_id=1, source_target_pairs={{8,16},{24,32},{40,48},{56,64},{72,80},{88,96},{104,112},{120,128}... | collective-permute-start | bytes 589832 | tf_op jit(solution)/shard_map/ppermute | solution.py:20
  17.1 0.0 collective-permute-done.1.even_ref
  17.1 0.0 collective-permute-done.2.odd_ref
  17.1 1.6 %shard_map.142.pair_ref = f32[2,192,128]{2,1,0:T(8,128)S(1)} custom-call(f32[2,192,128]{2,1,0:T(8,128)S(1)} %get-tuple-element.49.own_ref.own, f32[2,192,128]{2,1,0:T(8,128)S(1)} %collective-permute-done.inner_ref.inner, f32[2,2,48,128]{3,2,1,0:T(8,128)S(1)} %collective-permute-done.1.even_ref, f32[2,2,48,128]{3,2,1,0:T(8,128)S(1)} %collective-permute-done.2.odd_ref, ...), custom_call_target="tpu_custom_call" | custom-call | tf_op jit(solution)/shard_map/pallas_call | solution.py:202
  18.7 3.8 %collective-permute-start.3 = (f32[2,192,128]{2,1,0:T(8,128)S(1)}, f32[2,192,128]{2,1,0:T(8,128)S(1)}, u32[]{:S(2)}, u32[]{:S(2)}) collective-permute-start(f32[2,192,128]{2,1,0:T(8,128)S(1)} %shard_map.142.pair_ref), channel_id=1, source_target_pairs={{8,32},{24,48},{40,64},{56,80},{72,96},{88,112},{104,128},{120,144... | collective-permute-start | bytes 589832 | tf_op jit(solution)/shard_map/ppermute | solution.py:20
  22.5 3.8 %collective-permute-start.5 = (f32[2,192,128]{2,1,0:T(8,128)S(1)}, f32[2,192,128]{2,1,0:T(8,128)S(1)}, u32[]{:S(2)}, u32[]{:S(2)}) collective-permute-start(f32[2,192,128]{2,1,0:T(8,128)S(1)} %shard_map.142.pair_ref), channel_id=1, source_target_pairs={{8,16},{24,32},{40,48},{56,64},{72,80},{88,96},{104,112},{120,128}... | collective-permute-start | bytes 589832 | tf_op jit(solution)/shard_map/ppermute | solution.py:20
  26.2 0.0 copy-done
  26.2 0.0 copy-done.3
  26.3 0.0 copy-done.2
  26.3 0.0 copy-done.1
  26.3 1.6 %shard_map.144 = (f32[2,3,16,256]{3,2,1,0:T(8,128)S(1)}, f32[2,592,256]{2,1,0:T(8,128)S(1)}) custom-call(s32[3,16]{1,0:T(4,128)S(1)} %copy-done.1, s32[3,16]{1,0:T(4,128)S(1)} %copy-done.2, s32[3]{0:T(128)S(1)} %copy-done.3, f32[2,16,16,256]{3,2,1,0:T(8,128)S(1)} %copy-done, f32[2,192,128]{2,1,0:T(8,128)S(1)} %shard_map.142.pair_ref), custom_call_target="tpu_custom_call" | custom-call | tf_op jit(solution)/shard_map/pallas_call | solution.py:384
  27.9 0.0 collective-permute-done.4.outer
  27.9 3.0 %shard_map.143 = f32[2,24,8,128]{3,2,1,0:T(8,128)} custom-call(s32[16,24]{1,0:T(8,128)} %bitcast.10, s32[16,24]{1,0:T(8,128)} %bitcast.11, s32[24]{0:T(128)} %count.1, f32[2,128,128]{2,1,0:T(8,128)} %bitcast.8, f32[2,192,128]{2,1,0:T(8,128)S(1)} %get-tuple-element.49.own_ref.own, f32[2,192,128]{2,1,0:T(8,128)S(1)} %collective-permute-done.inner_ref.inner, ...), custom_call_target="tpu_custom_call" | custom-call | flops 4000000 | bytes 4000000 | tf_op jit(solution)/shard_map/pallas_call | solution.py:276
  30.8 0.0 collective-permute-done.3
  30.8 0.3 collective-permute-done.5
  31.2 4.3 %collective-permute-start.6 = (f32[2,384,128]{2,1,0:T(8,128)S(1)}, f32[2,384,128]{2,1,0:T(8,128)S(1)}, u32[]{:S(2)}, u32[]{:S(2)}) collective-permute-start(f32[2,384,128]{2,1,0:T(8,128)S(1)} %constant_dynamic-update-slice_fusion.sides_ref), channel_id=1, source_target_pairs={{0,8},{16,24},{32,40},{48,56},{64,72},{80,88},{96,104},{112,120},{... | collective-permute-start | bytes 1179656 | tf_op jit(solution)/shard_map/ppermute | solution.py:20
  35.5 1.3 %shard_map.145.part = f32[2,3,16,256]{3,2,1,0:T(8,128)S(1)} custom-call(s32[3,16]{1,0:T(4,128)S(1)} %copy-done.1, s32[3,16]{1,0:T(4,128)S(1)} %copy-done.2, s32[3]{0:T(128)S(1)} %copy-done.3, f32[2,16,16,256]{3,2,1,0:T(8,128)S(1)} %copy-done, f32[2,384,128]{2,1,0:T(8,128)S(1)} %constant_dynamic-update-slice_fusion.sides_ref, ...), custom_call_target="tpu_custom_call" | custom-call | tf_op jit(solution)/shard_map/pallas_call | solution.py:397
  36.8 0.0 collective-permute-done.6.other
  36.8 0.9 %shard_map.146 = f32[2,3,16,256]{3,2,1,0:T(8,128)} custom-call(f32[2,384,128]{2,1,0:T(8,128)S(1)} %collective-permute-done.6.other, f32[2,592,256]{2,1,0:T(8,128)S(1)} %get-tuple-element.56.dense, f32[2,3,16,256]{3,2,1,0:T(8,128)S(1)} %shard_map.145.part), custom_call_target="tpu_custom_call" | custom-call | tf_op jit(solution)/shard_map/pallas_call | solution.py:407
  (3 shorter events, 0.1 us)
Async XLA Ops:
  0.6 25.6 %copy-start = (f32[2,16,16,256]{3,2,1,0:T(8,128)S(1)}, f32[2,16,16,256]{3,2,1,0:T(8,128)}, u32[]{:S(2)}) copy-start(f32[2,16,16,256]{3,2,1,0:T(8,128)} %table.3) | copy-start | bytes 1572868
  0.6 25.6 %copy-start.3 = (s32[3]{0:T(128)S(1)}, s32[3]{0:T(128)}, u32[]{:S(2)}) copy-start(s32[3]{0:T(128)} %count_ref.3) | copy-start | bytes 40
  0.7 25.6 %copy-start.2 = (s32[3,16]{1,0:T(4,128)S(1)}, s32[3,16]{1,0:T(4,128)}, u32[]{:S(2)}) copy-start(s32[3,16]{1,0:T(4,128)} %offset_ref.3) | copy-start | bytes 580
  0.7 25.6 %copy-start.1 = (s32[3,16]{1,0:T(4,128)S(1)}, s32[3,16]{1,0:T(4,128)}, u32[]{:S(2)}) copy-start(s32[3,16]{1,0:T(4,128)} %partner_ref.3) | copy-start | bytes 580
  0.7 4.0 %collective-permute-start = (f32[2,192,128]{2,1,0:T(8,128)}, f32[2,192,128]{2,1,0:T(8,128)S(1)}, u32[]{:S(2)}, u32[]{:S(2)}) collective-permute-start(f32[2,192,128]{2,1,0:T(8,128)} %bitcast.6), channel_id=1, source_target_pairs={{0,8},{16,24},{32,40},{48,56},{64,72},{80,88},{96,104},{112,120},{... | collective-permute-start | bytes 589832 | tf_op jit(solution)/shard_map/ppermute | solution.py:20
  4.7 12.4 %collective-permute-start.1 = (f32[2,2,48,128]{3,2,1,0:T(8,128)S(1)}, f32[2,2,48,128]{3,2,1,0:T(8,128)S(1)}, u32[]{:S(2)}, u32[]{:S(2)}) collective-permute-start(f32[2,2,48,128]{3,2,1,0:T(8,128)S(1)} %get-tuple-element.41), channel_id=1, source_target_pairs={{0,1},{2,3},{4,5},{6,7},{1,0},{3,2},{5,4},{7,6},{8,9},{10,11},{12,... | collective-permute-start | bytes 294920 | tf_op jit(solution)/shard_map/ppermute | solution.py:20
  6.6 10.4 %collective-permute-start.2 = (f32[2,2,48,128]{3,2,1,0:T(8,128)S(1)}, f32[2,2,48,128]{3,2,1,0:T(8,128)S(1)}, u32[]{:S(2)}, u32[]{:S(2)}) collective-permute-start(f32[2,2,48,128]{3,2,1,0:T(8,128)S(1)} %get-tuple-element.42), channel_id=1, source_target_pairs={{1,2},{3,4},{5,6},{2,1},{4,3},{6,5},{9,10},{11,12},{13,14},{10,9},... | collective-permute-start | bytes 294920 | tf_op jit(solution)/shard_map/ppermute | solution.py:20
  13.0 14.8 %collective-permute-start.4 = (f32[2,192,128]{2,1,0:T(8,128)S(1)}, f32[2,192,128]{2,1,0:T(8,128)S(1)}, u32[]{:S(2)}, u32[]{:S(2)}) collective-permute-start(f32[2,192,128]{2,1,0:T(8,128)S(1)} %get-tuple-element.49.own_ref.own), channel_id=1, source_target_pairs={{8,16},{24,32},{40,48},{56,64},{72,80},{88,96},{104,112},{120,128}... | collective-permute-start | bytes 589832 | tf_op jit(solution)/shard_map/ppermute | solution.py:20
  18.7 12.2 %collective-permute-start.3 = (f32[2,192,128]{2,1,0:T(8,128)S(1)}, f32[2,192,128]{2,1,0:T(8,128)S(1)}, u32[]{:S(2)}, u32[]{:S(2)}) collective-permute-start(f32[2,192,128]{2,1,0:T(8,128)S(1)} %shard_map.142.pair_ref), channel_id=1, source_target_pairs={{8,32},{24,48},{40,64},{56,80},{72,96},{88,112},{104,128},{120,144... | collective-permute-start | bytes 589832 | tf_op jit(solution)/shard_map/ppermute | solution.py:20
  22.5 8.7 %collective-permute-start.5 = (f32[2,192,128]{2,1,0:T(8,128)S(1)}, f32[2,192,128]{2,1,0:T(8,128)S(1)}, u32[]{:S(2)}, u32[]{:S(2)}) collective-permute-start(f32[2,192,128]{2,1,0:T(8,128)S(1)} %shard_map.142.pair_ref), channel_id=1, source_target_pairs={{8,16},{24,32},{40,48},{56,64},{72,80},{88,96},{104,112},{120,128}... | collective-permute-start | bytes 589832 | tf_op jit(solution)/shard_map/ppermute | solution.py:20
  31.2 5.7 %collective-permute-start.6 = (f32[2,384,128]{2,1,0:T(8,128)S(1)}, f32[2,384,128]{2,1,0:T(8,128)S(1)}, u32[]{:S(2)}, u32[]{:S(2)}) collective-permute-start(f32[2,384,128]{2,1,0:T(8,128)S(1)} %constant_dynamic-update-slice_fusion.sides_ref), channel_id=1, source_target_pairs={{0,8},{16,24},{32,40},{48,56},{64,72},{80,88},{96,104},{112,120},{... | collective-permute-start | bytes 1179656 | tf_op jit(solution)/shard_map/ppermute | solution.py:20

commit v7 on v6

--- a/solution.py
+++ b/solution.py
@@ -87,7 +87,7 @@
     phase,
     own_ref,
     theta_ref,
-    theta_low_ref,
+    theta_rim_ref,
     phi_out_ref,
     phi_low_ref,
     cos_ref,
@@ -109,23 +109,34 @@
     copies[3].wait()
     copies[4].wait()
     samp = lax.axis_index("samp")
-    line = lax.broadcasted_iota(jnp.int32, (16, 96), 0)
-    column = lax.broadcasted_iota(jnp.int32, (16, 96), 1)
-    rim = (column - 64) // 8
-    rim = jnp.where((rim < 2) == (lax.rem(samp, 2) == 1), rim % 2 - 2, rim % 2 + 8)
+    odd = lax.rem(samp, 2)
+    line = lax.broadcasted_iota(jnp.int32, (16, 80), 0)
+    column = lax.broadcasted_iota(jnp.int32, (16, 80), 1)
+    rim = (column - 64) // 8 + jnp.where(odd == 1, -2, 8)
     row = jnp.where(column < 64, column % 8, rim) + samp * 8
-    theta = jnp.zeros((16, 96), jnp.float32)
+    theta = jnp.zeros((16, 80), jnp.float32)
     for i in range(16):
         for q in range(4):
             theta = theta + jnp.where((row == start_ref[i] + q) & (line == i), weight_ref[q, i], 0.0)
     theta = jnp.concatenate([theta] * 8, axis=0)
-    line = lax.broadcasted_iota(jnp.int32, (128, 96), 0)
-    column = lax.broadcasted_iota(jnp.int32, (128, 96), 1)
+    line = lax.broadcasted_iota(jnp.int32, (128, 80), 0)
+    column = lax.broadcasted_iota(jnp.int32, (128, 80), 1)
     child = jnp.where(column < 64, column // 8, column % 8)
-    theta = jnp.where(child == line // 16, theta, 0.0)
-    high, low = split(theta)
-    theta_ref[...] = jnp.concatenate([high, high], axis=1)
-    theta_low_ref[...] = low
+    high, low = split(jnp.where(child == line // 16, theta, 0.0))
+    theta_ref[...] = jnp.concatenate([high, high, low], axis=1)
+    line = lax.broadcasted_iota(jnp.int32, (8, 32), 0)
+    column = lax.broadcasted_iota(jnp.int32, (8, 32), 1)
+    row = column // 8 % 2 + jnp.where(odd == 1, 8, -2) + samp * 8
+    theta = jnp.zeros((8, 32), jnp.float32)
+    for i in range(4):
+        for q in range(4):
+            near = (row == start_ref[i + 12 * odd] + q) & (line % 4 == i) & (line // 4 == column // 16)
+            theta = theta + jnp.where(near, weight_ref[q, i + 12 * odd], 0.0)
+    theta = jnp.concatenate([theta] * 8, axis=0)
+    line = lax.broadcasted_iota(jnp.int32, (64, 32), 0)
+    column = lax.broadcasted_iota(jnp.int32, (64, 32), 1)
+    high, low = split(jnp.where(line // 8 == column % 8, theta, 0.0))
+    theta_rim_ref[...] = jnp.concatenate([high, high, low], axis=1)
     copies[0].wait()
     high, low = split(phi_ref[...].T)
     phi_out_ref[...] = jnp.concatenate([high, high], axis=0)
@@ -143,8 +154,8 @@
     half, full = jnp.bfloat16, jnp.float32
     shapes = (
         ((2, 192, 128), full),
-        ((128, 192), half),
-        ((128, 96), half),
+        ((128, 240), half),
+        ((64, 96), half),
         ((256, 256), half),
         ((128, 256), half),
         ((128, 256), full),
@@ -165,47 +176,93 @@
     )(*in_hbm(start, weight.T, pattern, phi, phase))
 
 
+def terms_of(parts):
+    high, low = split(jnp.concatenate([jnp.concatenate(part, axis=0) for part in parts], axis=1))
+    return jnp.concatenate([high, low, high], axis=0)
+
+
+def widen_and_sum(narrow, phi, phi_low, cosine, sine):
+    high, low = split(narrow)
+    wide = []
+    for x in range(2):
+        part = slice(128 * x, 128 * x + 128)
+        both = jnp.concatenate([high[:, part], low[:, part]], axis=1)
+        wide.append(dot(both, phi) + dot(high[:, part], phi_low))
+    shape = (8, narrow.shape[0] // 8, 256)
+    real_part = (cosine * wide[0] - sine * wide[1]).reshape(shape)
+    imag_part = (cosine * wide[1] + sine * wide[0]).reshape(shape)
+    return jnp.sum(real_part, axis=0), jnp.sum(imag_part, axis=0)
+
+
+def pair_row(box):
+    me = lax.rem(lax.axis_index("box"), 2)
+    return 96 * (me if box < 3 else 1 - me) + 32 * (box % 3)
+
+
 def aggregate_kernel(
-    own_ref, inner_ref, even_ref, odd_ref, theta_ref, theta_low_ref, phi_ref, phi_low_ref, cos_ref, sin_ref, pair_ref
+    own_ref, inner_ref, rim_ref, theta_ref, phi_ref, phi_low_ref, cos_ref, sin_ref, pair_ref, cos_rim_ref, sin_rim_ref
 ):
-    me = lax.rem(lax.axis_index("box"), 2)
-    theta, theta_low = theta_ref[...], theta_low_ref[...]
-    phi, phi_low = phi_ref[...], phi_low_ref[...]
-    for which, ref in enumerate((own_ref, inner_ref)):
-        place = 96 * (me if which == 0 else 1 - me)
-        for k in range(3):
-            columns = []
-            for x in range(2):
-                parts = [ref[x, 64 * k : 64 * k + 64]]
-                for rim_ref in (even_ref, odd_ref):
-                    parts += [rim_ref[x, r, pl.ds(24 * which + 8 * k, 8)] for r in range(2)]
-                columns.append(jnp.concatenate(parts, axis=0))
-            high, low = split(jnp.concatenate(columns, axis=1))
-            narrow = dot(theta, jnp.concatenate([high, low], axis=0)) + dot(theta_low, high)
-            high, low = split(narrow)
-            wide = []
-            for x in range(2):
-                part = slice(128 * x, 128 * x + 128)
-                both = jnp.concatenate([high[:, part], low[:, part]], axis=1)
-                wide.append(dot(both, phi) + dot(high[:, part], phi_low))
-            cosine, sine = cos_ref[...], sin_ref[...]
-            real_part = (cosine * wide[0] - sine * wide[1]).reshape(8, 16, 256)
-            imag_part = (cosine * wide[1] + sine * wide[0]).reshape(8, 16, 256)
-            for x, value in enumerate((real_part, imag_part)):
-                value = jnp.sum(value, axis=0)
-                for half in range(2):
-                    rows = pl.ds(pl.multiple_of(place + 32 * k + 16 * half, 16), 16)
-                    pair_ref[x, rows] = value[:, 128 * half : 128 * half + 128]
-
-
-def aggregate(own, inner, even, odd, mats):
+    even = lax.rem(lax.axis_index("samp"), 2) == 0
+    theta, phi, phi_low = theta_ref[...], phi_ref[...], phi_low_ref[...]
+    for box in range(6):
+        ref = own_ref if box < 3 else inner_ref
+        k = box % 3
+        parts = []
+        for x in range(2):
+            rows = [ref[x, 64 * k : 64 * k + 64]]
+            parts.append(rows + [rim_ref[x, r, pl.ds(8 * box, 8)] for r in range(2)])
+        narrow = dot(theta, terms_of(parts))
+        values = widen_and_sum(narrow, phi, phi_low, cos_ref[...], sin_ref[...])
+        for x in range(2):
+            for half in range(2):
+                rows = pl.ds(pl.multiple_of(pair_row(box) + 16 * half, 16), 16)
+                pair_ref[x, rows] = values[x][:, 128 * half : 128 * half + 128]
+    first = (lax.broadcasted_iota(jnp.int32, (8, 256), 0) < 4) == even
+    for ref, out_ref in ((cos_ref, cos_rim_ref), (sin_ref, sin_rim_ref)):
+        for child in range(8):
+            rows = ref[pl.ds(pl.multiple_of(16 * child + jnp.where(even, 0, 8), 8), 8)]
+            out_ref[8 * child : 8 * child + 8] = jnp.where(first, rows, pltpu.roll(rows, 4, 0))
+
+
+def aggregate(own, inner, rim, theta, phi, phi_low, cosine, sine):
+    waves = jax.ShapeDtypeStruct((64, 256), jnp.float32)
     return pl.pallas_call(
         aggregate_kernel,
+        out_shape=(jax.ShapeDtypeStruct((2, 192, 128), jnp.float32), waves, waves),
+        in_specs=[spec(VMEM)] * 8,
+        out_specs=(spec(VMEM),) * 3,
+        compiler_params=PARAMS,
+    )(own, inner, rim, theta, phi, phi_low, cosine, sine)
+
+
+def rim_sums_kernel(part_ref, rim_ref, theta_ref, phi_ref, phi_low_ref, cos_ref, sin_ref, pair_ref):
+    even = lax.rem(lax.axis_index("samp"), 2) == 0
+    pair_ref[...] = part_ref[...]
+    upper = lax.broadcasted_iota(jnp.int32, (8, 128), 0) < 4
+    theta, phi, phi_low = theta_ref[...], phi_ref[...], phi_low_ref[...]
+    for group in range(3):
+        boxes = (2 * group, 2 * group + 1)
+        parts = [[rim_ref[x, r, pl.ds(8 * box, 8)] for box in boxes for r in range(2)] for x in range(2)]
+        narrow = dot(theta, terms_of(parts))
+        values = widen_and_sum(narrow, phi, phi_low, cos_ref[...], sin_ref[...])
+        for x in range(2):
+            for half in range(2):
+                value = values[x][:, 128 * half : 128 * half + 128]
+                turned = pltpu.roll(value, 4, 0)
+                for order, box in enumerate(boxes):
+                    rows = pl.ds(pl.multiple_of(pair_row(box) + 16 * half + jnp.where(even, 0, 8), 8), 8)
+                    here = jnp.where(even, *((value, turned) if order == 0 else (turned, value)))
+                    pair_ref[x, rows] += jnp.where(upper == even, here, 0.0)
+
+
+def rim_sums(part, rim, theta, phi, phi_low, cosine, sine):
+    return pl.pallas_call(
+        rim_sums_kernel,
         out_shape=jax.ShapeDtypeStruct((2, 192, 128), jnp.float32),
-        in_specs=[spec(VMEM)] * 10,
+        in_specs=[spec(VMEM)] * 7,
         out_specs=spec(VMEM),
         compiler_params=PARAMS,
-    )(own, inner, even, odd, *mats)
+    )(part, rim, theta, phi, phi_low, cosine, sine)
 
 
 def fine_kernel(
@@ -431,13 +488,16 @@
 ):
     pattern = fine_pattern.reshape(2, 192, 128)
     inner = swap_cores(pattern)
-    own, *mats = prepare(pattern, theta_start, theta_weight, phi_interp, shift_phase.reshape(128, 256))
-    inner, own, mats = lax.optimization_barrier((inner, own, mats))
+    own, theta, theta_rim, phi, phi_low, cosine, sine = prepare(
+        pattern, theta_start, theta_weight, phi_interp, shift_phase.reshape(128, 256)
+    )
+    inner, own, theta = lax.optimization_barrier((inner, own, theta))
     even, odd = rims(own, inner)
     even, odd, late = lax.optimization_barrier((even, odd, own))
     outer = swap_chips(late, 1, 1)
     even, odd = swap_rims(even, 0), swap_rims(odd, 1)
-    pair = aggregate(own, inner, even, odd, mats)
+    part, *waves = aggregate(own, inner, even, theta, phi, phi_low, cosine, sine)
+    pair = rim_sums(part, odd, theta_rim, phi, phi_low, *waves)
     next_to, distant = swap_chips(pair, 1, 1), swap_chips(pair, 1, 2)
     fine_incoming = fine_translate(
         own, inner, outer, fine_table, fine_partner, fine_offset, fine_count

time: 38.1 us -> 38.7 us (1.016)
  Pallas kernels: 9.56 us -> 10.1 us
    pallas_call x1 -> x2, Pallas kernels: 1.58 us -> 2.09 us  [the longest x1 1.41 us: aggregate(): pl.pallas_call(aggregate_kernel, out_shape=(jax.ShapeDtypeStruct((2, 192,...]
  transfers between devices with their start and end apart: 7 -> 7, of which waited for: 1 -> 1; matrix products, arithmetic and copies ran while one was open for 0% -> 0% of each run, Pallas kernels for 23% -> 24%
where the time goes in v7:
time: 38.7 us; the launch traced here: 38.3 us
  starting transfers between devices  27.1 us (70%)
  Pallas kernels  10.1 us (26%)
  between operations  0.85 us (2%)
    ppermute x7, starting transfers between devices, matched(): return lax.ppermute(x, axis, pairs + [(j, i) for i, j in pairs])  27.1 us
    pallas_call x1, Pallas kernels, fine_translate(): pl.pallas_call(fine_kernel, out_shape=jax.ShapeDtypeStruct((2, 24, 8, 128...  2.96 us
    pallas_call x1, Pallas kernels, first_translate(): pl.pallas_call(first_kernel, out_shape=(jax.ShapeDtypeStruct((2, 3, 16, 2...  1.57 us
    pallas_call x1, Pallas kernels, aggregate(): pl.pallas_call(aggregate_kernel, out_shape=(jax.ShapeDtypeStruct((2, 192,...  1.41 us
    pallas_call x1, Pallas kernels, second_translate(): pl.pallas_call(second_kernel, out_shape=jax.ShapeDtypeStruct((2, 3, 16, 2...  1.33 us
    pallas_call x1, Pallas kernels, prepare(): pl.pallas_call(prepare_kernel, out_shape=tuple((jax.ShapeDtypeStruct(*s)...  1.21 us
    pallas_call x1, Pallas kernels, far_translate(): pl.pallas_call(far_kernel, out_shape=jax.ShapeDtypeStruct((2, 3, 16, 256)...  0.88 us
  transfers between devices with their start and end apart: 7, of which 1 were waited for; matrix products, arithmetic and copies ran while one was open for 0% of the time, Pallas kernels for 24%

profile of v7, /device:TPU:199, one launch (start us, length us, event | category | flops | bytes accessed | tf_op | source)
XLA Modules:
  0.0 38.3 jit_solution(13718644780771281801)
XLA Ops:
  0.6 2.6 %collective-permute-start = (f32[2,192,128]{2,1,0:T(8,128)}, f32[2,192,128]{2,1,0:T(8,128)S(1)}, u32[]{:S(2)}, u32[]{:S(2)}) collective-permute-start(f32[2,192,128]{2,1,0:T(8,128)} %bitcast.6), channel_id=1, source_target_pairs={{0,8},{16,24},{32,40},{48,56},{64,72},{80,88},{96,104},{112,120},{... | collective-permute-start | bytes 589832 | tf_op jit(solution)/shard_map/ppermute | solution.py:20
  3.2 1.2 %shard_map.140 = (f32[2,192,128]{2,1,0:T(8,128)S(1)}, bf16[128,240]{1,0:T(8,128)(2,1)S(1)}, bf16[64,96]{1,0:T(8,128)(2,1)S(1)}, bf16[256,256]{1,0:T(8,128)(2,1)S...) custom-call(s32[16]{0:T(128)} %start.1, f32[4,16]{1,0:T(4,128)} %bitcast.12, ...), custom_call_target="tpu_custom_call" | custom-call | tf_op jit(solution)/shard_map/pallas_call | solution.py:164
  4.4 0.0 copy-start
  4.4 0.0 copy-start.1
  4.5 0.0 copy-start.2
  4.5 0.0 copy-start.3
  4.5 0.0 collective-permute-done.inner_ref.inner
  4.5 2.1 %collective-permute-start.1 = (f32[2,2,48,128]{3,2,1,0:T(8,128)S(1)}, f32[2,2,48,128]{3,2,1,0:T(8,128)S(1)}, u32[]{:S(2)}, u32[]{:S(2)}) collective-permute-start(f32[2,2,48,128]{3,2,1,0:T(8,128)S(1)} %get-tuple-element.34), channel_id=1, source_target_pairs={{0,1},{2,3},{4,5},{6,7},{1,0},{3,2},{5,4},{7,6},{8,9},{10,11},{12,... | collective-permute-start | bytes 294920 | tf_op jit(solution)/shard_map/ppermute | solution.py:20
  6.6 6.4 %collective-permute-start.2 = (f32[2,2,48,128]{3,2,1,0:T(8,128)S(1)}, f32[2,2,48,128]{3,2,1,0:T(8,128)S(1)}, u32[]{:S(2)}, u32[]{:S(2)}) collective-permute-start(f32[2,2,48,128]{3,2,1,0:T(8,128)S(1)} %get-tuple-element.41), channel_id=1, source_target_pairs={{1,2},{3,4},{5,6},{2,1},{4,3},{6,5},{9,10},{11,12},{13,14},{10,9},... | collective-permute-start | bytes 294920 | tf_op jit(solution)/shard_map/ppermute | solution.py:20
  13.0 3.9 %collective-permute-start.4 = (f32[2,192,128]{2,1,0:T(8,128)S(1)}, f32[2,192,128]{2,1,0:T(8,128)S(1)}, u32[]{:S(2)}, u32[]{:S(2)}) collective-permute-start(f32[2,192,128]{2,1,0:T(8,128)S(1)} %get-tuple-element.45.own_ref.own), channel_id=1, source_target_pairs={{8,16},{24,32},{40,48},{56,64},{72,80},{88,96},{104,112},{120,128}... | collective-permute-start | bytes 589832 | tf_op jit(solution)/shard_map/ppermute | solution.py:20
  16.9 0.0 collective-permute-done.1.rim_ref
  16.9 1.4 %shard_map.142 = (f32[2,192,128]{2,1,0:T(8,128)S(1)}, f32[64,256]{1,0:T(8,128)S(1)}, f32[64,256]{1,0:T(8,128)S(1)}) custom-call(f32[2,192,128]{2,1,0:T(8,128)S(1)} %get-tuple-element.45.own_ref.own, f32[2,192,128]{2,1,0:T(8,128)S(1)} %collective-permute-done.inner_ref.inner, f32[2,2,48,128]{3,2,1,0:T(8,128)S(1)} %collective-permute-done.1.rim_ref, ...), custom_call_target="tpu_custom_call" | custom-call | tf_op jit(solution)/shard_map/pallas_call | solution.py:229
  18.3 0.0 collective-permute-done.2.rim_ref
  18.3 0.7 %shard_map.143.pair_ref = f32[2,192,128]{2,1,0:T(8,128)S(1)} custom-call(f32[2,192,128]{2,1,0:T(8,128)S(1)} %get-tuple-element.40.part_ref, f32[2,2,48,128]{3,2,1,0:T(8,128)S(1)} %collective-permute-done.2.rim_ref, bf16[64,96]{1,0:T(8,128)(2,1)S(1)} %get-tuple-element.42.theta_ref, bf16[256,256]{1,0:T(8,128)(2,1)S(1)} %get-tuple-element.36.phi_ref, ...), custom_call_target="tpu_custom_call" | custom-call | tf_op jit(solution)/shard_map/pallas_call | solution.py:259
  19.0 2.9 %collective-permute-start.3 = (f32[2,192,128]{2,1,0:T(8,128)S(1)}, f32[2,192,128]{2,1,0:T(8,128)S(1)}, u32[]{:S(2)}, u32[]{:S(2)}) collective-permute-start(f32[2,192,128]{2,1,0:T(8,128)S(1)} %shard_map.143.pair_ref), channel_id=1, source_target_pairs={{8,32},{24,48},{40,64},{56,80},{72,96},{88,112},{104,128},{120,144... | collective-permute-start | bytes 589832 | tf_op jit(solution)/shard_map/ppermute | solution.py:20
  21.9 4.6 %collective-permute-start.5 = (f32[2,192,128]{2,1,0:T(8,128)S(1)}, f32[2,192,128]{2,1,0:T(8,128)S(1)}, u32[]{:S(2)}, u32[]{:S(2)}) collective-permute-start(f32[2,192,128]{2,1,0:T(8,128)S(1)} %shard_map.143.pair_ref), channel_id=1, source_target_pairs={{8,16},{24,32},{40,48},{56,64},{72,80},{88,96},{104,112},{120,128}... | collective-permute-start | bytes 589832 | tf_op jit(solution)/shard_map/ppermute | solution.py:20
  26.6 0.0 copy-done
  26.6 0.0 copy-done.1
  26.6 0.0 copy-done.2
  26.6 0.0 copy-done.3
  26.6 1.6 %shard_map.145 = (f32[2,3,16,256]{3,2,1,0:T(8,128)S(1)}, f32[2,592,256]{2,1,0:T(8,128)S(1)}) custom-call(s32[3,16]{1,0:T(4,128)S(1)} %copy-done.1, s32[3,16]{1,0:T(4,128)S(1)} %copy-done.2, s32[3]{0:T(128)S(1)} %copy-done.3, f32[2,16,16,256]{3,2,1,0:T(8,128)S(1)} %copy-done, f32[2,192,128]{2,1,0:T(8,128)S(1)} %shard_map.143.pair_ref), custom_call_target="tpu_custom_call" | custom-call | tf_op jit(solution)/shard_map/pallas_call | solution.py:441
  28.2 0.0 collective-permute-done.4.outer
  28.2 3.0 %shard_map.144 = f32[2,24,8,128]{3,2,1,0:T(8,128)} custom-call(s32[16,24]{1,0:T(8,128)} %bitcast.10, s32[16,24]{1,0:T(8,128)} %bitcast.11, s32[24]{0:T(128)} %count.1, f32[2,128,128]{2,1,0:T(8,128)} %bitcast.8, f32[2,192,128]{2,1,0:T(8,128)S(1)} %get-tuple-element.45.own_ref.own, f32[2,192,128]{2,1,0:T(8,128)S(1)} %collective-permute-done.inner_ref.inner, ...), custom_call_target="tpu_custom_call" | custom-call | flops 4000000 | bytes 4000000 | tf_op jit(solution)/shard_map/pallas_call | solution.py:333
  31.2 0.0 collective-permute-done.3
  31.2 0.3 collective-permute-done.5
  31.5 4.6 %collective-permute-start.6 = (f32[2,384,128]{2,1,0:T(8,128)S(1)}, f32[2,384,128]{2,1,0:T(8,128)S(1)}, u32[]{:S(2)}, u32[]{:S(2)}) collective-permute-start(f32[2,384,128]{2,1,0:T(8,128)S(1)} %constant_dynamic-update-slice_fusion.sides_ref), channel_id=1, source_target_pairs={{0,8},{16,24},{32,40},{48,56},{64,72},{80,88},{96,104},{112,120},{... | collective-permute-start | bytes 1179656 | tf_op jit(solution)/shard_map/ppermute | solution.py:20
  36.1 1.3 %shard_map.146.part = f32[2,3,16,256]{3,2,1,0:T(8,128)S(1)} custom-call(s32[3,16]{1,0:T(4,128)S(1)} %copy-done.1, s32[3,16]{1,0:T(4,128)S(1)} %copy-done.2, s32[3]{0:T(128)S(1)} %copy-done.3, f32[2,16,16,256]{3,2,1,0:T(8,128)S(1)} %copy-done, f32[2,384,128]{2,1,0:T(8,128)S(1)} %constant_dynamic-update-slice_fusion.sides_ref, ...), custom_call_target="tpu_custom_call" | custom-call | tf_op jit(solution)/shard_map/pallas_call | solution.py:454
  37.4 0.0 collective-permute-done.6.other
  37.4 0.9 %shard_map.147 = f32[2,3,16,256]{3,2,1,0:T(8,128)} custom-call(f32[2,384,128]{2,1,0:T(8,128)S(1)} %collective-permute-done.6.other, f32[2,592,256]{2,1,0:T(8,128)S(1)} %get-tuple-element.52.dense, f32[2,3,16,256]{3,2,1,0:T(8,128)S(1)} %shard_map.146.part), custom_call_target="tpu_custom_call" | custom-call | tf_op jit(solution)/shard_map/pallas_call | solution.py:464
  (3 shorter events, 0.1 us)
Async XLA Ops:
  0.6 3.9 %collective-permute-start = (f32[2,192,128]{2,1,0:T(8,128)}, f32[2,192,128]{2,1,0:T(8,128)S(1)}, u32[]{:S(2)}, u32[]{:S(2)}) collective-permute-start(f32[2,192,128]{2,1,0:T(8,128)} %bitcast.6), channel_id=1, source_target_pairs={{0,8},{16,24},{32,40},{48,56},{64,72},{80,88},{96,104},{112,120},{... | collective-permute-start | bytes 589832 | tf_op jit(solution)/shard_map/ppermute | solution.py:20
  4.4 22.1 %copy-start = (f32[2,16,16,256]{3,2,1,0:T(8,128)S(1)}, f32[2,16,16,256]{3,2,1,0:T(8,128)}, u32[]{:S(2)}) copy-start(f32[2,16,16,256]{3,2,1,0:T(8,128)} %table.3) | copy-start | bytes 1572868
  4.4 22.1 %copy-start.1 = (s32[3,16]{1,0:T(4,128)S(1)}, s32[3,16]{1,0:T(4,128)}, u32[]{:S(2)}) copy-start(s32[3,16]{1,0:T(4,128)} %partner_ref.3) | copy-start | bytes 580
  4.5 22.1 %copy-start.2 = (s32[3,16]{1,0:T(4,128)S(1)}, s32[3,16]{1,0:T(4,128)}, u32[]{:S(2)}) copy-start(s32[3,16]{1,0:T(4,128)} %offset_ref.3) | copy-start | bytes 580
  4.5 22.1 %copy-start.3 = (s32[3]{0:T(128)S(1)}, s32[3]{0:T(128)}, u32[]{:S(2)}) copy-start(s32[3]{0:T(128)} %count_ref.3) | copy-start | bytes 40
  4.5 12.3 %collective-permute-start.1 = (f32[2,2,48,128]{3,2,1,0:T(8,128)S(1)}, f32[2,2,48,128]{3,2,1,0:T(8,128)S(1)}, u32[]{:S(2)}, u32[]{:S(2)}) collective-permute-start(f32[2,2,48,128]{3,2,1,0:T(8,128)S(1)} %get-tuple-element.34), channel_id=1, source_target_pairs={{0,1},{2,3},{4,5},{6,7},{1,0},{3,2},{5,4},{7,6},{8,9},{10,11},{12,... | collective-permute-start | bytes 294920 | tf_op jit(solution)/shard_map/ppermute | solution.py:20
  6.6 11.7 %collective-permute-start.2 = (f32[2,2,48,128]{3,2,1,0:T(8,128)S(1)}, f32[2,2,48,128]{3,2,1,0:T(8,128)S(1)}, u32[]{:S(2)}, u32[]{:S(2)}) collective-permute-start(f32[2,2,48,128]{3,2,1,0:T(8,128)S(1)} %get-tuple-element.41), channel_id=1, source_target_pairs={{1,2},{3,4},{5,6},{2,1},{4,3},{6,5},{9,10},{11,12},{13,14},{10,9},... | collective-permute-start | bytes 294920 | tf_op jit(solution)/shard_map/ppermute | solution.py:20
  13.0 15.2 %collective-permute-start.4 = (f32[2,192,128]{2,1,0:T(8,128)S(1)}, f32[2,192,128]{2,1,0:T(8,128)S(1)}, u32[]{:S(2)}, u32[]{:S(2)}) collective-permute-start(f32[2,192,128]{2,1,0:T(8,128)S(1)} %get-tuple-element.45.own_ref.own), channel_id=1, source_target_pairs={{8,16},{24,32},{40,48},{56,64},{72,80},{88,96},{104,112},{120,128}... | collective-permute-start | bytes 589832 | tf_op jit(solution)/shard_map/ppermute | solution.py:20
  19.0 12.2 %collective-permute-start.3 = (f32[2,192,128]{2,1,0:T(8,128)S(1)}, f32[2,192,128]{2,1,0:T(8,128)S(1)}, u32[]{:S(2)}, u32[]{:S(2)}) collective-permute-start(f32[2,192,128]{2,1,0:T(8,128)S(1)} %shard_map.143.pair_ref), channel_id=1, source_target_pairs={{8,32},{24,48},{40,64},{56,80},{72,96},{88,112},{104,128},{120,144... | collective-permute-start | bytes 589832 | tf_op jit(solution)/shard_map/ppermute | solution.py:20
  21.9 9.5 %collective-permute-start.5 = (f32[2,192,128]{2,1,0:T(8,128)S(1)}, f32[2,192,128]{2,1,0:T(8,128)S(1)}, u32[]{:S(2)}, u32[]{:S(2)}) collective-permute-start(f32[2,192,128]{2,1,0:T(8,128)S(1)} %shard_map.143.pair_ref), channel_id=1, source_target_pairs={{8,16},{24,32},{40,48},{56,64},{72,80},{88,96},{104,112},{120,128}... | collective-permute-start | bytes 589832 | tf_op jit(solution)/shard_map/ppermute | solution.py:20
  31.5 5.9 %collective-permute-start.6 = (f32[2,384,128]{2,1,0:T(8,128)S(1)}, f32[2,384,128]{2,1,0:T(8,128)S(1)}, u32[]{:S(2)}, u32[]{:S(2)}) collective-permute-start(f32[2,384,128]{2,1,0:T(8,128)S(1)} %constant_dynamic-update-slice_fusion.sides_ref), channel_id=1, source_target_pairs={{0,8},{16,24},{32,40},{48,56},{64,72},{80,88},{96,104},{112,120},{... | collective-permute-start | bytes 1179656 | tf_op jit(solution)/shard_map/ppermute | solution.py:20

commit v8 on v6

--- a/solution.py
+++ b/solution.py
@@ -168,11 +168,9 @@
 def aggregate_kernel(
     own_ref, inner_ref, even_ref, odd_ref, theta_ref, theta_low_ref, phi_ref, phi_low_ref, cos_ref, sin_ref, pair_ref
 ):
-    me = lax.rem(lax.axis_index("box"), 2)
     theta, theta_low = theta_ref[...], theta_low_ref[...]
     phi, phi_low = phi_ref[...], phi_low_ref[...]
     for which, ref in enumerate((own_ref, inner_ref)):
-        place = 96 * (me if which == 0 else 1 - me)
         for k in range(3):
             columns = []
             for x in range(2):
@@ -194,7 +192,7 @@
             for x, value in enumerate((real_part, imag_part)):
                 value = jnp.sum(value, axis=0)
                 for half in range(2):
-                    rows = pl.ds(pl.multiple_of(place + 32 * k + 16 * half, 16), 16)
+                    rows = pl.ds(96 * which + 32 * k + 16 * half, 16)
                     pair_ref[x, rows] = value[:, 128 * half : 128 * half + 128]
 
 
@@ -293,80 +291,84 @@
     )(*in_hbm(partner.T, offset.T, count, table.reshape(2, 128, 128)), pattern, inner, outer)
 
 
-def coarse_box(b, partner_ref, offset_ref, count_ref):
-    base = (lax.axis_index("box") // 2 - 2) * 6
-    return [(j < count_ref[b], partner_ref[b, j] - base, offset_ref[b, j]) for j in range(16)]
-
-
-def coarse_sums(window, table, slots):
-    sums = [None, None]
-    for live, place, which in slots:
-        place = pl.multiple_of(jnp.where(live, place, 0) * 32, 32)
-        scale = jnp.where(live, 1.0, 0.0)
+SIDE, SOURCES = 12, 21
+
+
+def first_kernel(partner_ref, offset_ref, count_ref, table, pair_ref, out_ref, dense_ref):
+    me = lax.axis_index("box")
+    odd = lax.rem(me, 2) == 1
+    base = (me // 2 - 2) * 6
+    firsts = [jnp.where(odd, *of) for of in ((18, 6), (12, 0), (0, 12), (6, 18))]
+    turned = jnp.where(odd, 18, 12)
+    dense_ref[...] = jnp.zeros(dense_ref.shape, jnp.float32)
+
+    def pick(box, values):
+        before = jnp.where(box < 6, values[0], values[1])
+        return jnp.where(box < 12, before, jnp.where(box < 24, values[2], values[3]))
+
+    def step(b, carry):
+        sums = [None, None]
+        for j in range(16):
+            live = j < count_ref[b]
+            box, which = partner_ref[b, j] - base, offset_ref[b, j]
+            here = jnp.logical_and(box >= 12, box < 18)
+            place = box - jnp.where(here, 12, pick(box, (0, 6, 18, 24)))
+            place = jnp.where(box < turned, jnp.where(place < 3, place + 3, place - 3), place)
+            away = jnp.logical_and(live, jnp.logical_not(here))
+            entry = jnp.where(away, b * SOURCES + pick(box, firsts) + place, 3 * SOURCES)
+            row = pl.multiple_of(entry * 16, 16)
+            for x in range(2):
+                dense_ref[x, pl.ds(row, 16)] = table[x, which]
+            here = jnp.logical_and(live, here)
+            place = pl.multiple_of(jnp.where(here, place, 0) * 32, 32)
+            scale = jnp.where(here, 1.0, 0.0)
+            for half in range(2):
+                lanes = slice(128 * half, 128 * half + 128)
+                rows = pl.ds(place + 16 * half, 16)
+                a, c = table[0, which, :, lanes] * scale, table[1, which, :, lanes] * scale
+                f, g = pair_ref[0, rows], pair_ref[1, rows]
+                terms = (a * f, c * g, a * g, c * f)
+                old = sums[half]
+                sums[half] = terms if old is None else tuple(s + t for s, t in zip(old, terms))
         for half in range(2):
             lanes = slice(128 * half, 128 * half + 128)
-            rows = pl.ds(place + 16 * half, 16)
-            a, c = table[0, which, :, lanes] * scale, table[1, which, :, lanes] * scale
-            f, g = window[0, rows], window[1, rows]
-            terms = (a * f, c * g, a * g, c * f)
-            old = sums[half]
-            sums[half] = terms if old is None else tuple(s + t for s, t in zip(old, terms))
-    return [(s[0] - s[1], s[2] + s[3]) for s in sums]
-
-
-def first_kernel(partner_ref, offset_ref, count_ref, table, pair_ref, out_ref, dense_ref):
-    odd = lax.rem(lax.axis_index("box"), 2) == 1
-    dense_ref[...] = jnp.zeros(dense_ref.shape, jnp.float32)
-
-    def step(b, carry):
-        slots = []
-        for live, box, which in coarse_box(b, partner_ref, offset_ref, count_ref):
-            far = jnp.logical_and(live, jnp.where(odd, box < 12, box >= 18))
-            place = jnp.where(odd, jnp.where(box >= 6, box - 6, box + 6), box - 18)
-            row = pl.multiple_of(jnp.where(far, b * 12 + place, 36) * 16, 16)
-            for x in range(2):
-                dense_ref[x, pl.ds(row, 16)] = table[x, which]
-            slots.append((live & (box >= 12) & (box < 18), box - 12, which))
-        sums = coarse_sums(pair_ref, table, slots)
-        for half in range(2):
-            for x in range(2):
-                out_ref[x, b, :, 128 * half : 128 * half + 128] = sums[half][x]
+            out_ref[0, b, :, lanes] = sums[half][0] - sums[half][1]
+            out_ref[1, b, :, lanes] = sums[half][2] + sums[half][3]
         return carry
 
     lax.fori_loop(0, 3, step, 0)
 
 
-def second_kernel(partner_ref, offset_ref, count_ref, table, sides_ref, part_ref, out_ref):
-    odd = lax.rem(lax.axis_index("box"), 2) == 1
-
-    def step(b, carry):
-        slots = []
-        for live, box, which in coarse_box(b, partner_ref, offset_ref, count_ref):
-            place = jnp.where(odd, box - 18, jnp.where(box >= 6, box - 6, box + 6))
-            slots.append((jnp.logical_and(live, jnp.where(odd, box >= 18, box < 12)), place, which))
-        sums = coarse_sums(sides_ref, table, slots)
-        for half in range(2):
-            lanes = slice(128 * half, 128 * half + 128)
-            for x in range(2):
-                out_ref[x, b, :, lanes] = part_ref[x, b, :, lanes] + sums[half][x]
-        return carry
-
-    lax.fori_loop(0, 3, step, 0)
+def dense_sums(part, dense, sources, lines, lanes, half, top):
+    sums = [(part[0, b, lines, lanes], part[1, b, lines, lanes]) for b in range(3)]
+    for ref, row, entry in sources:
+        rows = pl.ds(row + 16 * half + top, 8)
+        f, g = ref[0, rows], ref[1, rows]
+        for b in range(3):
+            places = pl.ds((SOURCES * b + entry) * 16 + top, 8)
+            a, c = dense[0, places, lanes], dense[1, places, lanes]
+            sums[b] = (sums[b][0] + (a * f - c * g), sums[b][1] + (a * g + c * f))
+    return sums
+
+
+def second_kernel(next_ref, distant_ref, dense, part, out_ref):
+    sources = [(next_ref, 32 * s, s) for s in range(6)] + [(distant_ref, 32 * s, 6 + s) for s in range(6)]
+    for half in range(2):
+        for top in (0, 8):
+            lanes, lines = pl.ds(128 * half, 128), pl.ds(top, 8)
+            sums = dense_sums(part, dense, sources, lines, lanes, half, top)
+            for b in range(3):
+                for x in range(2):
+                    out_ref[x, b, lines, lanes] = sums[b][x]
 
 
 def far_kernel(other, dense, part, out, value_ref, sems):
+    sources = [(other, 32 * s, SIDE + s) for s in range(9)]
     copies = []
     for half in range(2):
         for top in (0, 8):
             lanes, lines = pl.ds(128 * half, 128), pl.ds(top, 8)
-            sums = [(part[0, b, lines, lanes], part[1, b, lines, lanes]) for b in range(3)]
-            for s in range(12):
-                rows = pl.ds(32 * s + 16 * half + top, 8)
-                f, g = other[0, rows], other[1, rows]
-                for b in range(3):
-                    places = pl.ds((12 * b + s) * 16 + top, 8)
-                    a, c = dense[0, places, lanes], dense[1, places, lanes]
-                    sums[b] = (sums[b][0] + (a * f - c * g), sums[b][1] + (a * g + c * f))
+            sums = dense_sums(part, dense, sources, lines, lanes, half, top)
             for b in range(3):
                 for x in range(2):
                     value_ref[x, b, lines, lanes] = sums[b][x]
@@ -385,7 +387,7 @@
         first_kernel,
         out_shape=(
             jax.ShapeDtypeStruct((2, 3, 16, 256), jnp.float32),
-            jax.ShapeDtypeStruct((2, 37 * 16, 256), jnp.float32),
+            jax.ShapeDtypeStruct((2, (3 * SOURCES + 1) * 16, 256), jnp.float32),
         ),
         in_specs=[spec(SMEM)] * 3 + [spec(VMEM)] * 2,
         out_specs=(spec(VMEM), spec(VMEM)),
@@ -393,14 +395,14 @@
     )(*lists, table, pair)
 
 
-def second_translate(lists, table, sides, part):
+def second_translate(next_to, distant, dense, part):
     return pl.pallas_call(
         second_kernel,
         out_shape=jax.ShapeDtypeStruct((2, 3, 16, 256), jnp.float32),
-        in_specs=[spec(SMEM)] * 3 + [spec(VMEM)] * 3,
+        in_specs=[spec(VMEM)] * 4,
         out_specs=spec(VMEM),
         compiler_params=PARAMS,
-    )(*lists, table, sides, part)
+    )(next_to, distant, dense, part)
 
 
 def far_translate(other, dense, part):
@@ -446,9 +448,8 @@
     part, dense = first_translate(lists, coarse_table, pair)
     distant, fine_incoming, part, dense = lax.optimization_barrier((distant, fine_incoming, part, dense))
     next_to, distant = lax.optimization_barrier((next_to, distant))
-    sides = jnp.concatenate([next_to, distant], axis=1)
-    other = swap_cores(sides)
-    part = second_translate(lists, coarse_table, sides, part)
+    other = swap_cores(jnp.concatenate([next_to, distant[:, :96]], axis=1))
+    part = second_translate(next_to, distant, dense, part)
     coarse_incoming = far_translate(other, dense, part)
     return (fine_incoming, coarse_incoming)
 

time: 38.1 us -> 37.8 us (level)
  Pallas kernels: 9.56 us -> 8.6 us
  waiting for transfers between devices: 0.33 us -> 1.04 us
    pallas_call x1, Pallas kernels: 1.33 us -> 0.24 us  [second_translate(): pl.pallas_call(second_kernel, out_shape=jax.ShapeDtypeStruct((2, 3, 16, 2...]
    ppermute x7, waiting for transfers between devices: 0.33 us -> 1.04 us  [matched(): return lax.ppermute(x, axis, pairs + [(j, i) for i, j in pairs])]
  transfers between devices with their start and end apart: 7 -> 7, of which waited for: 1 -> 1; matrix products, arithmetic and copies ran while one was open for 0% -> 0% of each run, Pallas kernels for 23% -> 21%
where the time goes in v8:
time: 37.8 us; the launch traced here: 37.4 us
  starting transfers between devices  26.9 us (71%)
  Pallas kernels  8.6 us (23%)
  waiting for transfers between devices  1.04 us (3%)
  between operations  0.83 us (2%)
    ppermute x7, starting transfers between devices, matched(): return lax.ppermute(x, axis, pairs + [(j, i) for i, j in pairs])  26.9 us
    pallas_call x1, Pallas kernels, fine_translate(): pl.pallas_call(fine_kernel, out_shape=jax.ShapeDtypeStruct((2, 24, 8, 128...  2.96 us
    pallas_call x1, Pallas kernels, first_translate(): pl.pallas_call(first_kernel, out_shape=(jax.ShapeDtypeStruct((2, 3, 16, 2...  1.8 us
    pallas_call x1, Pallas kernels, aggregate(): pl.pallas_call(aggregate_kernel, out_shape=jax.ShapeDtypeStruct((2, 192,...  1.57 us
    pallas_call x1, Pallas kernels, prepare(): pl.pallas_call(prepare_kernel, out_shape=tuple((jax.ShapeDtypeStruct(*s)...  1.21 us
    ppermute x7, waiting for transfers between devices, matched(): return lax.ppermute(x, axis, pairs + [(j, i) for i, j in pairs])  1.04 us
    pallas_call x1, Pallas kernels, far_translate(): pl.pallas_call(far_kernel, out_shape=jax.ShapeDtypeStruct((2, 3, 16, 256)...  0.79 us
  transfers between devices with their start and end apart: 7, of which 1 were waited for; matrix products, arithmetic and copies ran while one was open for 0% of the time, Pallas kernels for 21%

profile of v8, /device:TPU:199, one launch (start us, length us, event | category | flops | bytes accessed | tf_op | source)
XLA Modules:
  0.0 37.4 jit_solution(11183492164952557797)
XLA Ops:
  0.6 0.0 copy-start
  0.6 0.0 copy-start.3
  0.7 0.0 copy-start.2
  0.7 0.0 copy-start.1
  0.7 2.7 %collective-permute-start = (f32[2,192,128]{2,1,0:T(8,128)}, f32[2,192,128]{2,1,0:T(8,128)S(1)}, u32[]{:S(2)}, u32[]{:S(2)}) collective-permute-start(f32[2,192,128]{2,1,0:T(8,128)} %bitcast.6), channel_id=1, source_target_pairs={{0,8},{16,24},{32,40},{48,56},{64,72},{80,88},{96,104},{112,120},{... | collective-permute-start | bytes 589832 | tf_op jit(solution)/shard_map/ppermute | solution.py:20
  3.4 1.2 %shard_map.140 = (f32[2,192,128]{2,1,0:T(8,128)S(1)}, bf16[128,192]{1,0:T(8,128)(2,1)S(1)}, bf16[128,96]{1,0:T(8,128)(2,1)S(1)}, bf16[256,256]{1,0:T(8,128)(2,1)...) custom-call(s32[16]{0:T(128)} %start.1, f32[4,16]{1,0:T(4,128)} %bitcast.12, ...), custom_call_target="tpu_custom_call" | custom-call | tf_op jit(solution)/shard_map/pallas_call | solution.py:153
  4.6 0.0 collective-permute-done.inner_ref.inner
  4.7 1.9 %collective-permute-start.1 = (f32[2,2,48,128]{3,2,1,0:T(8,128)S(1)}, f32[2,2,48,128]{3,2,1,0:T(8,128)S(1)}, u32[]{:S(2)}, u32[]{:S(2)}) collective-permute-start(f32[2,2,48,128]{3,2,1,0:T(8,128)S(1)} %get-tuple-element.41), channel_id=1, source_target_pairs={{0,1},{2,3},{4,5},{6,7},{1,0},{3,2},{5,4},{7,6},{8,9},{10,11},{12,... | collective-permute-start | bytes 294920 | tf_op jit(solution)/shard_map/ppermute | solution.py:20
  6.6 6.4 %collective-permute-start.2 = (f32[2,2,48,128]{3,2,1,0:T(8,128)S(1)}, f32[2,2,48,128]{3,2,1,0:T(8,128)S(1)}, u32[]{:S(2)}, u32[]{:S(2)}) collective-permute-start(f32[2,2,48,128]{3,2,1,0:T(8,128)S(1)} %get-tuple-element.42), channel_id=1, source_target_pairs={{1,2},{3,4},{5,6},{2,1},{4,3},{6,5},{9,10},{11,12},{13,14},{10,9},... | collective-permute-start | bytes 294920 | tf_op jit(solution)/shard_map/ppermute | solution.py:20
  13.0 4.0 %collective-permute-start.4 = (f32[2,192,128]{2,1,0:T(8,128)S(1)}, f32[2,192,128]{2,1,0:T(8,128)S(1)}, u32[]{:S(2)}, u32[]{:S(2)}) collective-permute-start(f32[2,192,128]{2,1,0:T(8,128)S(1)} %get-tuple-element.49.own_ref.own), channel_id=1, source_target_pairs={{8,16},{24,32},{40,48},{56,64},{72,80},{88,96},{104,112},{120,128}... | collective-permute-start | bytes 589832 | tf_op jit(solution)/shard_map/ppermute | solution.py:20
  17.1 0.0 collective-permute-done.1.even_ref
  17.1 0.0 collective-permute-done.2.odd_ref
  17.1 1.6 %shard_map.142.pair_ref = f32[2,192,128]{2,1,0:T(8,128)S(1)} custom-call(f32[2,192,128]{2,1,0:T(8,128)S(1)} %get-tuple-element.49.own_ref.own, f32[2,192,128]{2,1,0:T(8,128)S(1)} %collective-permute-done.inner_ref.inner, f32[2,2,48,128]{3,2,1,0:T(8,128)S(1)} %collective-permute-done.1.even_ref, f32[2,2,48,128]{3,2,1,0:T(8,128)S(1)} %collective-permute-done.2.odd_ref, ...), custom_call_target="tpu_custom_call" | custom-call | tf_op jit(solution)/shard_map/pallas_call | solution.py:200
  18.6 3.8 %collective-permute-start.3 = (f32[2,192,128]{2,1,0:T(8,128)S(1)}, f32[2,192,128]{2,1,0:T(8,128)S(1)}, u32[]{:S(2)}, u32[]{:S(2)}) collective-permute-start(f32[2,192,128]{2,1,0:T(8,128)S(1)} %shard_map.142.pair_ref), channel_id=1, source_target_pairs={{8,32},{24,48},{40,64},{56,80},{72,96},{88,112},{104,128},{120,144... | collective-permute-start | bytes 589832 | tf_op jit(solution)/shard_map/ppermute | solution.py:20
  22.4 3.8 %collective-permute-start.5 = (f32[2,192,128]{2,1,0:T(8,128)S(1)}, f32[2,192,128]{2,1,0:T(8,128)S(1)}, u32[]{:S(2)}, u32[]{:S(2)}) collective-permute-start(f32[2,192,128]{2,1,0:T(8,128)S(1)} %shard_map.142.pair_ref), channel_id=1, source_target_pairs={{8,16},{24,32},{40,48},{56,64},{72,80},{88,96},{104,112},{120,128}... | collective-permute-start | bytes 589832 | tf_op jit(solution)/shard_map/ppermute | solution.py:20
  26.2 0.0 copy-done
  26.2 0.0 copy-done.3
  26.2 0.0 copy-done.2
  26.3 0.0 copy-done.1
  26.3 1.8 %shard_map.144 = (f32[2,3,16,256]{3,2,1,0:T(8,128)S(1)}, f32[2,1024,256]{2,1,0:T(8,128)S(1)}) custom-call(s32[3,16]{1,0:T(4,128)S(1)} %copy-done.1, s32[3,16]{1,0:T(4,128)S(1)} %copy-done.2, s32[3]{0:T(128)S(1)} %copy-done.3, f32[2,16,16,256]{3,2,1,0:T(8,128)S(1)} %copy-done, f32[2,192,128]{2,1,0:T(8,128)S(1)} %shard_map.142.pair_ref), custom_call_target="tpu_custom_call" | custom-call | tf_op jit(solution)/shard_map/pallas_call | solution.py:386
  28.1 0.0 collective-permute-done.4.outer
  28.1 3.0 %shard_map.143 = f32[2,24,8,128]{3,2,1,0:T(8,128)} custom-call(s32[16,24]{1,0:T(8,128)} %bitcast.10, s32[16,24]{1,0:T(8,128)} %bitcast.11, s32[24]{0:T(128)} %count.1, f32[2,128,128]{2,1,0:T(8,128)} %bitcast.8, f32[2,192,128]{2,1,0:T(8,128)S(1)} %get-tuple-element.49.own_ref.own, f32[2,192,128]{2,1,0:T(8,128)S(1)} %collective-permute-done.inner_ref.inner, ...), custom_call_target="tpu_custom_call" | custom-call | flops 4000000 | bytes 4000000 | tf_op jit(solution)/shard_map/pallas_call | solution.py:274
  31.0 0.0 collective-permute-done.3.distant_ref
  31.1 0.0 collective-permute-done.5.next_ref
  31.1 4.3 %collective-permute-start.6 = (f32[2,288,128]{2,1,0:T(8,128)S(1)}, f32[2,288,128]{2,1,0:T(8,128)S(1)}, u32[]{:S(2)}, u32[]{:S(2)}) collective-permute-start(f32[2,288,128]{2,1,0:T(8,128)S(1)} %pad_maximum_fusion), channel_id=1, source_target_pairs={{0,8},{16,24},{32,40},{48,56},{64,72},{80,88},{96,104},{112,120},{... | collective-permute-start | bytes 884744 | tf_op jit(solution)/shard_map/ppermute | solution.py:20
  35.5 0.2 shard_map.145.part
  35.7 0.9 %collective-permute-done.6.other = f32[2,288,128]{2,1,0:T(8,128)S(1)} collective-permute-done((f32[2,288,128]{2,1,0:T(8,128)S(1)}, f32[2,288,128]{2,1,0:T(8,128)S(1)}, u32[]{:S(2)}, u32[]{:S(2)}) %collective-permute-start.6) | collective-permute-done | bytes 294944 | tf_op jit(solution)/shard_map/ppermute | solution.py:20
  36.6 0.8 %shard_map.146 = f32[2,3,16,256]{3,2,1,0:T(8,128)} custom-call(f32[2,288,128]{2,1,0:T(8,128)S(1)} %collective-permute-done.6.other, f32[2,1024,256]{2,1,0:T(8,128)S(1)} %get-tuple-element.56.dense, f32[2,3,16,256]{3,2,1,0:T(8,128)S(1)} %shard_map.145.part), custom_call_target="tpu_custom_call" | custom-call | tf_op jit(solution)/shard_map/pallas_call | solution.py:409
  (3 shorter events, 0.1 us)
Async XLA Ops:
  0.6 25.6 %copy-start = (f32[2,16,16,256]{3,2,1,0:T(8,128)S(1)}, f32[2,16,16,256]{3,2,1,0:T(8,128)}, u32[]{:S(2)}) copy-start(f32[2,16,16,256]{3,2,1,0:T(8,128)} %table.1) | copy-start | bytes 1572868
  0.6 25.6 %copy-start.3 = (s32[3]{0:T(128)S(1)}, s32[3]{0:T(128)}, u32[]{:S(2)}) copy-start(s32[3]{0:T(128)} %count_ref.1) | copy-start | bytes 40
  0.7 25.6 %copy-start.2 = (s32[3,16]{1,0:T(4,128)S(1)}, s32[3,16]{1,0:T(4,128)}, u32[]{:S(2)}) copy-start(s32[3,16]{1,0:T(4,128)} %offset_ref.1) | copy-start | bytes 580
  0.7 25.6 %copy-start.1 = (s32[3,16]{1,0:T(4,128)S(1)}, s32[3,16]{1,0:T(4,128)}, u32[]{:S(2)}) copy-start(s32[3,16]{1,0:T(4,128)} %partner_ref.1) | copy-start | bytes 580
  0.7 4.0 %collective-permute-start = (f32[2,192,128]{2,1,0:T(8,128)}, f32[2,192,128]{2,1,0:T(8,128)S(1)}, u32[]{:S(2)}, u32[]{:S(2)}) collective-permute-start(f32[2,192,128]{2,1,0:T(8,128)} %bitcast.6), channel_id=1, source_target_pairs={{0,8},{16,24},{32,40},{48,56},{64,72},{80,88},{96,104},{112,120},{... | collective-permute-start | bytes 589832 | tf_op jit(solution)/shard_map/ppermute | solution.py:20
  4.7 12.4 %collective-permute-start.1 = (f32[2,2,48,128]{3,2,1,0:T(8,128)S(1)}, f32[2,2,48,128]{3,2,1,0:T(8,128)S(1)}, u32[]{:S(2)}, u32[]{:S(2)}) collective-permute-start(f32[2,2,48,128]{3,2,1,0:T(8,128)S(1)} %get-tuple-element.41), channel_id=1, source_target_pairs={{0,1},{2,3},{4,5},{6,7},{1,0},{3,2},{5,4},{7,6},{8,9},{10,11},{12,... | collective-permute-start | bytes 294920 | tf_op jit(solution)/shard_map/ppermute | solution.py:20
  6.6 10.4 %collective-permute-start.2 = (f32[2,2,48,128]{3,2,1,0:T(8,128)S(1)}, f32[2,2,48,128]{3,2,1,0:T(8,128)S(1)}, u32[]{:S(2)}, u32[]{:S(2)}) collective-permute-start(f32[2,2,48,128]{3,2,1,0:T(8,128)S(1)} %get-tuple-element.42), channel_id=1, source_target_pairs={{1,2},{3,4},{5,6},{2,1},{4,3},{6,5},{9,10},{11,12},{13,14},{10,9},... | collective-permute-start | bytes 294920 | tf_op jit(solution)/shard_map/ppermute | solution.py:20
  13.0 15.1 %collective-permute-start.4 = (f32[2,192,128]{2,1,0:T(8,128)S(1)}, f32[2,192,128]{2,1,0:T(8,128)S(1)}, u32[]{:S(2)}, u32[]{:S(2)}) collective-permute-start(f32[2,192,128]{2,1,0:T(8,128)S(1)} %get-tuple-element.49.own_ref.own), channel_id=1, source_target_pairs={{8,16},{24,32},{40,48},{56,64},{72,80},{88,96},{104,112},{120,128}... | collective-permute-start | bytes 589832 | tf_op jit(solution)/shard_map/ppermute | solution.py:20
  18.6 12.4 %collective-permute-start.3 = (f32[2,192,128]{2,1,0:T(8,128)S(1)}, f32[2,192,128]{2,1,0:T(8,128)S(1)}, u32[]{:S(2)}, u32[]{:S(2)}) collective-permute-start(f32[2,192,128]{2,1,0:T(8,128)S(1)} %shard_map.142.pair_ref), channel_id=1, source_target_pairs={{8,32},{24,48},{40,64},{56,80},{72,96},{88,112},{104,128},{120,144... | collective-permute-start | bytes 589832 | tf_op jit(solution)/shard_map/ppermute | solution.py:20
  22.4 8.7 %collective-permute-start.5 = (f32[2,192,128]{2,1,0:T(8,128)S(1)}, f32[2,192,128]{2,1,0:T(8,128)S(1)}, u32[]{:S(2)}, u32[]{:S(2)}) collective-permute-start(f32[2,192,128]{2,1,0:T(8,128)S(1)} %shard_map.142.pair_ref), channel_id=1, source_target_pairs={{8,16},{24,32},{40,48},{56,64},{72,80},{88,96},{104,112},{120,128}... | collective-permute-start | bytes 589832 | tf_op jit(solution)/shard_map/ppermute | solution.py:20
  31.1 5.5 %collective-permute-start.6 = (f32[2,288,128]{2,1,0:T(8,128)S(1)}, f32[2,288,128]{2,1,0:T(8,128)S(1)}, u32[]{:S(2)}, u32[]{:S(2)}) collective-permute-start(f32[2,288,128]{2,1,0:T(8,128)S(1)} %pad_maximum_fusion), channel_id=1, source_target_pairs={{0,8},{16,24},{32,40},{48,56},{64,72},{80,88},{96,104},{112,120},{... | collective-permute-start | bytes 884744 | tf_op jit(solution)/shard_map/ppermute | solution.py:20

commit v9 on v8

--- a/solution.py
+++ b/solution.py
@@ -170,30 +170,45 @@
 ):
     theta, theta_low = theta_ref[...], theta_low_ref[...]
     phi, phi_low = phi_ref[...], phi_low_ref[...]
-    for which, ref in enumerate((own_ref, inner_ref)):
-        for k in range(3):
-            columns = []
-            for x in range(2):
-                parts = [ref[x, 64 * k : 64 * k + 64]]
-                for rim_ref in (even_ref, odd_ref):
-                    parts += [rim_ref[x, r, pl.ds(24 * which + 8 * k, 8)] for r in range(2)]
-                columns.append(jnp.concatenate(parts, axis=0))
-            high, low = split(jnp.concatenate(columns, axis=1))
-            narrow = dot(theta, jnp.concatenate([high, low], axis=0)) + dot(theta_low, high)
-            high, low = split(narrow)
-            wide = []
-            for x in range(2):
-                part = slice(128 * x, 128 * x + 128)
-                both = jnp.concatenate([high[:, part], low[:, part]], axis=1)
-                wide.append(dot(both, phi) + dot(high[:, part], phi_low))
-            cosine, sine = cos_ref[...], sin_ref[...]
-            real_part = (cosine * wide[0] - sine * wide[1]).reshape(8, 16, 256)
-            imag_part = (cosine * wide[1] + sine * wide[0]).reshape(8, 16, 256)
-            for x, value in enumerate((real_part, imag_part)):
-                value = jnp.sum(value, axis=0)
-                for half in range(2):
-                    rows = pl.ds(96 * which + 32 * k + 16 * half, 16)
-                    pair_ref[x, rows] = value[:, 128 * half : 128 * half + 128]
+
+    def narrow_of(box):
+        ref, k = (own_ref, inner_ref)[box // 3], box % 3
+        columns = []
+        for x in range(2):
+            parts = [ref[x, 64 * k : 64 * k + 64]]
+            for rim_ref in (even_ref, odd_ref):
+                parts += [rim_ref[x, r, pl.ds(8 * box, 8)] for r in range(2)]
+            columns.append(jnp.concatenate(parts, axis=0))
+        high, low = split(jnp.concatenate(columns, axis=1))
+        return dot(theta, jnp.concatenate([high, low], axis=0)) + dot(theta_low, high)
+
+    def wide_of(narrow):
+        high, low = split(narrow)
+        wide = []
+        for x in range(2):
+            part = slice(128 * x, 128 * x + 128)
+            both = jnp.concatenate([high[:, part], low[:, part]], axis=1)
+            wide.append(dot(both, phi) + dot(high[:, part], phi_low))
+        return wide
+
+    def store(box, wide):
+        cosine, sine = cos_ref[...], sin_ref[...]
+        real_part = (cosine * wide[0] - sine * wide[1]).reshape(8, 16, 256)
+        imag_part = (cosine * wide[1] + sine * wide[0]).reshape(8, 16, 256)
+        for x, value in enumerate((real_part, imag_part)):
+            value = jnp.sum(value, axis=0)
+            for half in range(2):
+                rows = pl.ds(32 * box + 16 * half, 16)
+                pair_ref[x, rows] = value[:, 128 * half : 128 * half + 128]
+
+    narrow = [narrow_of(0), narrow_of(1)]
+    wide = wide_of(narrow[0])
+    for box in range(6):
+        if box < 4:
+            narrow.append(narrow_of(box + 2))
+        ahead = wide_of(narrow[box + 1]) if box < 5 else None
+        store(box, wide)
+        wide = ahead
 
 
 def aggregate(own, inner, even, odd, mats):

time: 37.8 us -> 37.2 us (0.984)
  Pallas kernels: 8.6 us -> 7.98 us
    pallas_call x1, Pallas kernels: 1.57 us -> 0.95 us  [aggregate(): pl.pallas_call(aggregate_kernel, out_shape=jax.ShapeDtypeStruct((2, 192,...]
  transfers between devices with their start and end apart: 7 -> 7, of which waited for: 1 -> 1; matrix products, arithmetic and copies ran while one was open for 0% -> 0% of each run, Pallas kernels for 21% -> 19%
where the time goes in v9:
time: 37.2 us; the launch traced here: 36.8 us
  starting transfers between devices  26.9 us (72%)
  Pallas kernels  7.98 us (21%)
  waiting for transfers between devices  1.04 us (3%)
  between operations  0.83 us (2%)
    ppermute x7, starting transfers between devices, matched(): return lax.ppermute(x, axis, pairs + [(j, i) for i, j in pairs])  26.9 us
    pallas_call x1, Pallas kernels, fine_translate(): pl.pallas_call(fine_kernel, out_shape=jax.ShapeDtypeStruct((2, 24, 8, 128...  2.96 us
    pallas_call x1, Pallas kernels, first_translate(): pl.pallas_call(first_kernel, out_shape=(jax.ShapeDtypeStruct((2, 3, 16, 2...  1.8 us
    pallas_call x1, Pallas kernels, prepare(): pl.pallas_call(prepare_kernel, out_shape=tuple((jax.ShapeDtypeStruct(*s)...  1.21 us
    ppermute x7, waiting for transfers between devices, matched(): return lax.ppermute(x, axis, pairs + [(j, i) for i, j in pairs])  1.04 us
    pallas_call x1, Pallas kernels, aggregate(): pl.pallas_call(aggregate_kernel, out_shape=jax.ShapeDtypeStruct((2, 192,...  0.95 us
    pallas_call x1, Pallas kernels, far_translate(): pl.pallas_call(far_kernel, out_shape=jax.ShapeDtypeStruct((2, 3, 16, 256)...  0.79 us
  transfers between devices with their start and end apart: 7, of which 1 were waited for; matrix products, arithmetic and copies ran while one was open for 0% of the time, Pallas kernels for 19%

profile of v9, /device:TPU:199, one launch (start us, length us, event | category | flops | bytes accessed | tf_op | source)
XLA Modules:
  0.0 36.8 jit_solution(339160660092567894)
XLA Ops:
  0.6 0.0 copy-start
  0.6 0.0 copy-start.3
  0.7 0.0 copy-start.2
  0.7 0.0 copy-start.1
  0.7 2.7 %collective-permute-start = (f32[2,192,128]{2,1,0:T(8,128)}, f32[2,192,128]{2,1,0:T(8,128)S(1)}, u32[]{:S(2)}, u32[]{:S(2)}) collective-permute-start(f32[2,192,128]{2,1,0:T(8,128)} %bitcast.6), channel_id=1, source_target_pairs={{0,8},{16,24},{32,40},{48,56},{64,72},{80,88},{96,104},{112,120},{... | collective-permute-start | bytes 589832 | tf_op jit(solution)/shard_map/ppermute | solution.py:20
  3.4 1.2 %shard_map.140 = (f32[2,192,128]{2,1,0:T(8,128)S(1)}, bf16[128,192]{1,0:T(8,128)(2,1)S(1)}, bf16[128,96]{1,0:T(8,128)(2,1)S(1)}, bf16[256,256]{1,0:T(8,128)(2,1)...) custom-call(s32[16]{0:T(128)} %start.1, f32[4,16]{1,0:T(4,128)} %bitcast.12, ...), custom_call_target="tpu_custom_call" | custom-call | tf_op jit(solution)/shard_map/pallas_call | solution.py:153
  4.6 0.0 collective-permute-done.inner_ref.inner
  4.7 1.9 %collective-permute-start.1 = (f32[2,2,48,128]{3,2,1,0:T(8,128)S(1)}, f32[2,2,48,128]{3,2,1,0:T(8,128)S(1)}, u32[]{:S(2)}, u32[]{:S(2)}) collective-permute-start(f32[2,2,48,128]{3,2,1,0:T(8,128)S(1)} %get-tuple-element.41), channel_id=1, source_target_pairs={{0,1},{2,3},{4,5},{6,7},{1,0},{3,2},{5,4},{7,6},{8,9},{10,11},{12,... | collective-permute-start | bytes 294920 | tf_op jit(solution)/shard_map/ppermute | solution.py:20
  6.6 6.4 %collective-permute-start.2 = (f32[2,2,48,128]{3,2,1,0:T(8,128)S(1)}, f32[2,2,48,128]{3,2,1,0:T(8,128)S(1)}, u32[]{:S(2)}, u32[]{:S(2)}) collective-permute-start(f32[2,2,48,128]{3,2,1,0:T(8,128)S(1)} %get-tuple-element.42), channel_id=1, source_target_pairs={{1,2},{3,4},{5,6},{2,1},{4,3},{6,5},{9,10},{11,12},{13,14},{10,9},... | collective-permute-start | bytes 294920 | tf_op jit(solution)/shard_map/ppermute | solution.py:20
  13.0 4.0 %collective-permute-start.4 = (f32[2,192,128]{2,1,0:T(8,128)S(1)}, f32[2,192,128]{2,1,0:T(8,128)S(1)}, u32[]{:S(2)}, u32[]{:S(2)}) collective-permute-start(f32[2,192,128]{2,1,0:T(8,128)S(1)} %get-tuple-element.49.own_ref.own), channel_id=1, source_target_pairs={{8,16},{24,32},{40,48},{56,64},{72,80},{88,96},{104,112},{120,128}... | collective-permute-start | bytes 589832 | tf_op jit(solution)/shard_map/ppermute | solution.py:20
  17.1 0.0 collective-permute-done.1.even_ref
  17.1 0.0 collective-permute-done.2.odd_ref
  17.1 1.0 %shard_map.142.pair_ref = f32[2,192,128]{2,1,0:T(8,128)S(1)} custom-call(f32[2,192,128]{2,1,0:T(8,128)S(1)} %get-tuple-element.49.own_ref.own, f32[2,192,128]{2,1,0:T(8,128)S(1)} %collective-permute-done.inner_ref.inner, f32[2,2,48,128]{3,2,1,0:T(8,128)S(1)} %collective-permute-done.1.even_ref, f32[2,2,48,128]{3,2,1,0:T(8,128)S(1)} %collective-permute-done.2.odd_ref, ...), custom_call_target="tpu_custom_call" | custom-call | tf_op jit(solution)/shard_map/pallas_call | solution.py:215
  18.0 3.8 %collective-permute-start.3 = (f32[2,192,128]{2,1,0:T(8,128)S(1)}, f32[2,192,128]{2,1,0:T(8,128)S(1)}, u32[]{:S(2)}, u32[]{:S(2)}) collective-permute-start(f32[2,192,128]{2,1,0:T(8,128)S(1)} %shard_map.142.pair_ref), channel_id=1, source_target_pairs={{8,32},{24,48},{40,64},{56,80},{72,96},{88,112},{104,128},{120,144... | collective-permute-start | bytes 589832 | tf_op jit(solution)/shard_map/ppermute | solution.py:20
  21.8 3.8 %collective-permute-start.5 = (f32[2,192,128]{2,1,0:T(8,128)S(1)}, f32[2,192,128]{2,1,0:T(8,128)S(1)}, u32[]{:S(2)}, u32[]{:S(2)}) collective-permute-start(f32[2,192,128]{2,1,0:T(8,128)S(1)} %shard_map.142.pair_ref), channel_id=1, source_target_pairs={{8,16},{24,32},{40,48},{56,64},{72,80},{88,96},{104,112},{120,128}... | collective-permute-start | bytes 589832 | tf_op jit(solution)/shard_map/ppermute | solution.py:20
  25.6 0.0 copy-done
  25.6 0.0 copy-done.3
  25.6 0.0 copy-done.2
  25.6 0.0 copy-done.1
  25.6 1.8 %shard_map.144 = (f32[2,3,16,256]{3,2,1,0:T(8,128)S(1)}, f32[2,1024,256]{2,1,0:T(8,128)S(1)}) custom-call(s32[3,16]{1,0:T(4,128)S(1)} %copy-done.1, s32[3,16]{1,0:T(4,128)S(1)} %copy-done.2, s32[3]{0:T(128)S(1)} %copy-done.3, f32[2,16,16,256]{3,2,1,0:T(8,128)S(1)} %copy-done, f32[2,192,128]{2,1,0:T(8,128)S(1)} %shard_map.142.pair_ref), custom_call_target="tpu_custom_call" | custom-call | tf_op jit(solution)/shard_map/pallas_call | solution.py:401
  27.5 0.0 collective-permute-done.4.outer
  27.5 3.0 %shard_map.143 = f32[2,24,8,128]{3,2,1,0:T(8,128)} custom-call(s32[16,24]{1,0:T(8,128)} %bitcast.10, s32[16,24]{1,0:T(8,128)} %bitcast.11, s32[24]{0:T(128)} %count.1, f32[2,128,128]{2,1,0:T(8,128)} %bitcast.8, f32[2,192,128]{2,1,0:T(8,128)S(1)} %get-tuple-element.49.own_ref.own, f32[2,192,128]{2,1,0:T(8,128)S(1)} %collective-permute-done.inner_ref.inner, ...), custom_call_target="tpu_custom_call" | custom-call | flops 4000000 | bytes 4000000 | tf_op jit(solution)/shard_map/pallas_call | solution.py:289
  30.4 0.0 collective-permute-done.3.distant_ref
  30.4 0.0 collective-permute-done.5.next_ref
  30.5 4.3 %collective-permute-start.6 = (f32[2,288,128]{2,1,0:T(8,128)S(1)}, f32[2,288,128]{2,1,0:T(8,128)S(1)}, u32[]{:S(2)}, u32[]{:S(2)}) collective-permute-start(f32[2,288,128]{2,1,0:T(8,128)S(1)} %pad_maximum_fusion), channel_id=1, source_target_pairs={{0,8},{16,24},{32,40},{48,56},{64,72},{80,88},{96,104},{112,120},{... | collective-permute-start | bytes 884744 | tf_op jit(solution)/shard_map/ppermute | solution.py:20
  34.8 0.2 shard_map.145.part
  35.1 0.9 %collective-permute-done.6.other = f32[2,288,128]{2,1,0:T(8,128)S(1)} collective-permute-done((f32[2,288,128]{2,1,0:T(8,128)S(1)}, f32[2,288,128]{2,1,0:T(8,128)S(1)}, u32[]{:S(2)}, u32[]{:S(2)}) %collective-permute-start.6) | collective-permute-done | bytes 294944 | tf_op jit(solution)/shard_map/ppermute | solution.py:20
  36.0 0.8 %shard_map.146 = f32[2,3,16,256]{3,2,1,0:T(8,128)} custom-call(f32[2,288,128]{2,1,0:T(8,128)S(1)} %collective-permute-done.6.other, f32[2,1024,256]{2,1,0:T(8,128)S(1)} %get-tuple-element.56.dense, f32[2,3,16,256]{3,2,1,0:T(8,128)S(1)} %shard_map.145.part), custom_call_target="tpu_custom_call" | custom-call | tf_op jit(solution)/shard_map/pallas_call | solution.py:424
  (3 shorter events, 0.1 us)
Async XLA Ops:
  0.6 25.0 %copy-start = (f32[2,16,16,256]{3,2,1,0:T(8,128)S(1)}, f32[2,16,16,256]{3,2,1,0:T(8,128)}, u32[]{:S(2)}) copy-start(f32[2,16,16,256]{3,2,1,0:T(8,128)} %table.1) | copy-start | bytes 1572868
  0.6 25.0 %copy-start.3 = (s32[3]{0:T(128)S(1)}, s32[3]{0:T(128)}, u32[]{:S(2)}) copy-start(s32[3]{0:T(128)} %count_ref.1) | copy-start | bytes 40
  0.7 25.0 %copy-start.2 = (s32[3,16]{1,0:T(4,128)S(1)}, s32[3,16]{1,0:T(4,128)}, u32[]{:S(2)}) copy-start(s32[3,16]{1,0:T(4,128)} %offset_ref.1) | copy-start | bytes 580
  0.7 25.0 %copy-start.1 = (s32[3,16]{1,0:T(4,128)S(1)}, s32[3,16]{1,0:T(4,128)}, u32[]{:S(2)}) copy-start(s32[3,16]{1,0:T(4,128)} %partner_ref.1) | copy-start | bytes 580
  0.7 4.0 %collective-permute-start = (f32[2,192,128]{2,1,0:T(8,128)}, f32[2,192,128]{2,1,0:T(8,128)S(1)}, u32[]{:S(2)}, u32[]{:S(2)}) collective-permute-start(f32[2,192,128]{2,1,0:T(8,128)} %bitcast.6), channel_id=1, source_target_pairs={{0,8},{16,24},{32,40},{48,56},{64,72},{80,88},{96,104},{112,120},{... | collective-permute-start | bytes 589832 | tf_op jit(solution)/shard_map/ppermute | solution.py:20
  4.7 12.4 %collective-permute-start.1 = (f32[2,2,48,128]{3,2,1,0:T(8,128)S(1)}, f32[2,2,48,128]{3,2,1,0:T(8,128)S(1)}, u32[]{:S(2)}, u32[]{:S(2)}) collective-permute-start(f32[2,2,48,128]{3,2,1,0:T(8,128)S(1)} %get-tuple-element.41), channel_id=1, source_target_pairs={{0,1},{2,3},{4,5},{6,7},{1,0},{3,2},{5,4},{7,6},{8,9},{10,11},{12,... | collective-permute-start | bytes 294920 | tf_op jit(solution)/shard_map/ppermute | solution.py:20
  6.6 10.4 %collective-permute-start.2 = (f32[2,2,48,128]{3,2,1,0:T(8,128)S(1)}, f32[2,2,48,128]{3,2,1,0:T(8,128)S(1)}, u32[]{:S(2)}, u32[]{:S(2)}) collective-permute-start(f32[2,2,48,128]{3,2,1,0:T(8,128)S(1)} %get-tuple-element.42), channel_id=1, source_target_pairs={{1,2},{3,4},{5,6},{2,1},{4,3},{6,5},{9,10},{11,12},{13,14},{10,9},... | collective-permute-start | bytes 294920 | tf_op jit(solution)/shard_map/ppermute | solution.py:20
  13.0 14.4 %collective-permute-start.4 = (f32[2,192,128]{2,1,0:T(8,128)S(1)}, f32[2,192,128]{2,1,0:T(8,128)S(1)}, u32[]{:S(2)}, u32[]{:S(2)}) collective-permute-start(f32[2,192,128]{2,1,0:T(8,128)S(1)} %get-tuple-element.49.own_ref.own), channel_id=1, source_target_pairs={{8,16},{24,32},{40,48},{56,64},{72,80},{88,96},{104,112},{120,128}... | collective-permute-start | bytes 589832 | tf_op jit(solution)/shard_map/ppermute | solution.py:20
  18.0 12.4 %collective-permute-start.3 = (f32[2,192,128]{2,1,0:T(8,128)S(1)}, f32[2,192,128]{2,1,0:T(8,128)S(1)}, u32[]{:S(2)}, u32[]{:S(2)}) collective-permute-start(f32[2,192,128]{2,1,0:T(8,128)S(1)} %shard_map.142.pair_ref), channel_id=1, source_target_pairs={{8,32},{24,48},{40,64},{56,80},{72,96},{88,112},{104,128},{120,144... | collective-permute-start | bytes 589832 | tf_op jit(solution)/shard_map/ppermute | solution.py:20
  21.8 8.7 %collective-permute-start.5 = (f32[2,192,128]{2,1,0:T(8,128)S(1)}, f32[2,192,128]{2,1,0:T(8,128)S(1)}, u32[]{:S(2)}, u32[]{:S(2)}) collective-permute-start(f32[2,192,128]{2,1,0:T(8,128)S(1)} %shard_map.142.pair_ref), channel_id=1, source_target_pairs={{8,16},{24,32},{40,48},{56,64},{72,80},{88,96},{104,112},{120,128}... | collective-permute-start | bytes 589832 | tf_op jit(solution)/shard_map/ppermute | solution.py:20
  30.5 5.5 %collective-permute-start.6 = (f32[2,288,128]{2,1,0:T(8,128)S(1)}, f32[2,288,128]{2,1,0:T(8,128)S(1)}, u32[]{:S(2)}, u32[]{:S(2)}) collective-permute-start(f32[2,288,128]{2,1,0:T(8,128)S(1)} %pad_maximum_fusion), channel_id=1, source_target_pairs={{0,8},{16,24},{32,40},{48,56},{64,72},{80,88},{96,104},{112,120},{... | collective-permute-start | bytes 884744 | tf_op jit(solution)/shard_map/ppermute | solution.py:20

commit v10 on v9

--- a/solution.py
+++ b/solution.py
@@ -29,6 +29,11 @@
     n = lax.axis_size("box")
     pairs = [(i + core, i + 2 * distance + 1 - core) for i in range(0, n - 2 * distance, 2)]
     return matched(x, "box", pairs)
+
+
+def swap_next(x):
+    n = lax.axis_size("box")
+    return matched(x, "box", [(i, i + 2) for i in range(0, n - 2, 4)] + [(i, i + 2) for i in range(3, n - 2, 4)])
 
 
 def swap_rims(x, start):
@@ -313,8 +318,9 @@
     me = lax.axis_index("box")
     odd = lax.rem(me, 2) == 1
     base = (me // 2 - 2) * 6
-    firsts = [jnp.where(odd, *of) for of in ((18, 6), (12, 0), (0, 12), (6, 18))]
-    turned = jnp.where(odd, 18, 12)
+    after = lax.rem(me // 2, 2) == lax.rem(me, 2)
+    firsts = [jnp.where(odd, 18, 6), jnp.where(after, 12, 0), jnp.where(after, 0, 12), jnp.where(odd, 6, 18)]
+    turns = [jnp.where(odd, 1, 0), jnp.where(odd == after, 0, 1), jnp.where(odd == after, 1, 0)]
     dense_ref[...] = jnp.zeros(dense_ref.shape, jnp.float32)
 
     def pick(box, values):
@@ -328,7 +334,8 @@
             box, which = partner_ref[b, j] - base, offset_ref[b, j]
             here = jnp.logical_and(box >= 12, box < 18)
             place = box - jnp.where(here, 12, pick(box, (0, 6, 18, 24)))
-            place = jnp.where(box < turned, jnp.where(place < 3, place + 3, place - 3), place)
+            turned = jnp.where(here, turns[0], pick(box, (1, turns[1], turns[2], 0))) == 1
+            place = jnp.where(turned, jnp.where(place < 3, place + 3, place - 3), place)
             away = jnp.logical_and(live, jnp.logical_not(here))
             entry = jnp.where(away, b * SOURCES + pick(box, firsts) + place, 3 * SOURCES)
             row = pl.multiple_of(entry * 16, 16)
@@ -455,7 +462,7 @@
     outer = swap_chips(late, 1, 1)
     even, odd = swap_rims(even, 0), swap_rims(odd, 1)
     pair = aggregate(own, inner, even, odd, mats)
-    next_to, distant = swap_chips(pair, 1, 1), swap_chips(pair, 1, 2)
+    next_to, distant = swap_next(pair), swap_chips(pair, 1, 2)
     fine_incoming = fine_translate(
         own, inner, outer, fine_table, fine_partner, fine_offset, fine_count
     )

time: 37.2 us -> 36 us (0.968)
  starting transfers between devices: 26.9 us -> 24.9 us
  waiting for transfers between devices: 1.04 us -> 1.79 us
    ppermute x7, starting transfers between devices: 26.9 us -> 24.9 us  [matched(): return lax.ppermute(x, axis, pairs + [(j, i) for i, j in pairs])]
    ppermute x7, waiting for transfers between devices: 1.04 us -> 1.79 us  [matched(): return lax.ppermute(x, axis, pairs + [(j, i) for i, j in pairs])]
  transfers between devices with their start and end apart: 7 -> 7, of which waited for: 1 -> 2; matrix products, arithmetic and copies ran while one was open for 0% -> 0% of each run, Pallas kernels for 19% -> 20%
where the time goes in v10:
time: 36 us; the launch traced here: 35.7 us
  starting transfers between devices  24.9 us (69%)
  Pallas kernels  8.04 us (22%)
  waiting for transfers between devices  1.79 us (5%)
  between operations  0.83 us (2%)
    ppermute x7, starting transfers between devices, matched(): return lax.ppermute(x, axis, pairs + [(j, i) for i, j in pairs])  24.9 us
    pallas_call x1, Pallas kernels, fine_translate(): pl.pallas_call(fine_kernel, out_shape=jax.ShapeDtypeStruct((2, 24, 8, 128...  2.96 us
    pallas_call x1, Pallas kernels, first_translate(): pl.pallas_call(first_kernel, out_shape=(jax.ShapeDtypeStruct((2, 3, 16, 2...  1.86 us
    ppermute x7, waiting for transfers between devices, matched(): return lax.ppermute(x, axis, pairs + [(j, i) for i, j in pairs])  1.79 us
    pallas_call x1, Pallas kernels, prepare(): pl.pallas_call(prepare_kernel, out_shape=tuple((jax.ShapeDtypeStruct(*s)...  1.21 us
    pallas_call x1, Pallas kernels, aggregate(): pl.pallas_call(aggregate_kernel, out_shape=jax.ShapeDtypeStruct((2, 192,...  0.95 us
    pallas_call x1, Pallas kernels, far_translate(): pl.pallas_call(far_kernel, out_shape=jax.ShapeDtypeStruct((2, 3, 16, 256)...  0.79 us
  transfers between devices with their start and end apart: 7, of which 2 were waited for; matrix products, arithmetic and copies ran while one was open for 0% of the time, Pallas kernels for 20%

profile of v10, /device:TPU:199, one launch (start us, length us, event | category | flops | bytes accessed | tf_op | source)
XLA Modules:
  0.0 35.7 jit_solution(4825164728889797270)
XLA Ops:
  0.6 0.0 copy-start
  0.6 0.0 copy-start.3
  0.7 0.0 copy-start.2
  0.7 0.0 copy-start.1
  0.7 2.7 %collective-permute-start = (f32[2,192,128]{2,1,0:T(8,128)}, f32[2,192,128]{2,1,0:T(8,128)S(1)}, u32[]{:S(2)}, u32[]{:S(2)}) collective-permute-start(f32[2,192,128]{2,1,0:T(8,128)} %bitcast.6), channel_id=1, source_target_pairs={{0,8},{16,24},{32,40},{48,56},{64,72},{80,88},{96,104},{112,120},{... | collective-permute-start | bytes 589832 | tf_op jit(solution)/shard_map/ppermute | solution.py:20
  3.4 1.2 %shard_map.140 = (f32[2,192,128]{2,1,0:T(8,128)S(1)}, bf16[128,192]{1,0:T(8,128)(2,1)S(1)}, bf16[128,96]{1,0:T(8,128)(2,1)S(1)}, bf16[256,256]{1,0:T(8,128)(2,1)...) custom-call(s32[16]{0:T(128)} %start.1, f32[4,16]{1,0:T(4,128)} %bitcast.12, ...), custom_call_target="tpu_custom_call" | custom-call | tf_op jit(solution)/shard_map/pallas_call | solution.py:158
  4.6 0.0 collective-permute-done.inner_ref.inner
  4.7 1.9 %collective-permute-start.1 = (f32[2,2,48,128]{3,2,1,0:T(8,128)S(1)}, f32[2,2,48,128]{3,2,1,0:T(8,128)S(1)}, u32[]{:S(2)}, u32[]{:S(2)}) collective-permute-start(f32[2,2,48,128]{3,2,1,0:T(8,128)S(1)} %get-tuple-element.41), channel_id=1, source_target_pairs={{0,1},{2,3},{4,5},{6,7},{1,0},{3,2},{5,4},{7,6},{8,9},{10,11},{12,... | collective-permute-start | bytes 294920 | tf_op jit(solution)/shard_map/ppermute | solution.py:20
  6.6 6.4 %collective-permute-start.2 = (f32[2,2,48,128]{3,2,1,0:T(8,128)S(1)}, f32[2,2,48,128]{3,2,1,0:T(8,128)S(1)}, u32[]{:S(2)}, u32[]{:S(2)}) collective-permute-start(f32[2,2,48,128]{3,2,1,0:T(8,128)S(1)} %get-tuple-element.42), channel_id=1, source_target_pairs={{1,2},{3,4},{5,6},{2,1},{4,3},{6,5},{9,10},{11,12},{13,14},{10,9},... | collective-permute-start | bytes 294920 | tf_op jit(solution)/shard_map/ppermute | solution.py:20
  13.0 4.0 %collective-permute-start.4 = (f32[2,192,128]{2,1,0:T(8,128)S(1)}, f32[2,192,128]{2,1,0:T(8,128)S(1)}, u32[]{:S(2)}, u32[]{:S(2)}) collective-permute-start(f32[2,192,128]{2,1,0:T(8,128)S(1)} %get-tuple-element.49.own_ref.own), channel_id=1, source_target_pairs={{8,16},{24,32},{40,48},{56,64},{72,80},{88,96},{104,112},{120,128}... | collective-permute-start | bytes 589832 | tf_op jit(solution)/shard_map/ppermute | solution.py:20
  17.1 0.0 collective-permute-done.1.even_ref
  17.1 0.0 collective-permute-done.2.odd_ref
  17.1 1.0 %shard_map.142.pair_ref = f32[2,192,128]{2,1,0:T(8,128)S(1)} custom-call(f32[2,192,128]{2,1,0:T(8,128)S(1)} %get-tuple-element.49.own_ref.own, f32[2,192,128]{2,1,0:T(8,128)S(1)} %collective-permute-done.inner_ref.inner, f32[2,2,48,128]{3,2,1,0:T(8,128)S(1)} %collective-permute-done.1.even_ref, f32[2,2,48,128]{3,2,1,0:T(8,128)S(1)} %collective-permute-done.2.odd_ref, ...), custom_call_target="tpu_custom_call" | custom-call | tf_op jit(solution)/shard_map/pallas_call | solution.py:220
  18.0 3.8 %collective-permute-start.3 = (f32[2,192,128]{2,1,0:T(8,128)S(1)}, f32[2,192,128]{2,1,0:T(8,128)S(1)}, u32[]{:S(2)}, u32[]{:S(2)}) collective-permute-start(f32[2,192,128]{2,1,0:T(8,128)S(1)} %shard_map.142.pair_ref), channel_id=1, source_target_pairs={{8,32},{24,48},{40,64},{56,80},{72,96},{88,112},{104,128},{120,144... | collective-permute-start | bytes 589832 | tf_op jit(solution)/shard_map/ppermute | solution.py:20
  21.8 4.2 %collective-permute-start.5 = (f32[2,192,128]{2,1,0:T(8,128)S(1)}, f32[2,192,128]{2,1,0:T(8,128)S(1)}, u32[]{:S(2)}, u32[]{:S(2)}) collective-permute-start(f32[2,192,128]{2,1,0:T(8,128)S(1)} %shard_map.142.pair_ref), channel_id=1, source_target_pairs={{0,16},{32,48},{64,80},{96,112},{128,144},{160,176},{192,208},{224... | collective-permute-start | bytes 589832 | tf_op jit(solution)/shard_map/ppermute | solution.py:20
  26.0 0.0 copy-done
  26.0 0.0 copy-done.3
  26.0 0.0 copy-done.2
  26.0 0.0 copy-done.1
  26.1 1.9 %shard_map.144 = (f32[2,3,16,256]{3,2,1,0:T(8,128)S(1)}, f32[2,1024,256]{2,1,0:T(8,128)S(1)}) custom-call(s32[3,16]{1,0:T(4,128)S(1)} %copy-done.1, s32[3,16]{1,0:T(4,128)S(1)} %copy-done.2, s32[3]{0:T(128)S(1)} %copy-done.3, f32[2,16,16,256]{3,2,1,0:T(8,128)S(1)} %copy-done, f32[2,192,128]{2,1,0:T(8,128)S(1)} %shard_map.142.pair_ref), custom_call_target="tpu_custom_call" | custom-call | tf_op jit(solution)/shard_map/pallas_call | solution.py:408
  27.9 0.0 collective-permute-done.4.outer
  27.9 3.0 %shard_map.143 = f32[2,24,8,128]{3,2,1,0:T(8,128)} custom-call(s32[16,24]{1,0:T(8,128)} %bitcast.10, s32[16,24]{1,0:T(8,128)} %bitcast.11, s32[24]{0:T(128)} %count.1, f32[2,128,128]{2,1,0:T(8,128)} %bitcast.8, f32[2,192,128]{2,1,0:T(8,128)S(1)} %get-tuple-element.49.own_ref.own, f32[2,192,128]{2,1,0:T(8,128)S(1)} %collective-permute-done.inner_ref.inner, ...), custom_call_target="tpu_custom_call" | custom-call | flops 4000000 | bytes 4000000 | tf_op jit(solution)/shard_map/pallas_call | solution.py:294
  30.9 0.0 collective-permute-done.3.distant_ref
  30.9 0.4 %collective-permute-done.5.next_ref = f32[2,192,128]{2,1,0:T(8,128)S(1)} collective-permute-done((f32[2,192,128]{2,1,0:T(8,128)S(1)}, f32[2,192,128]{2,1,0:T(8,128)S(1)}, u32[]{:S(2)}, u32[]{:S(2)}) %collective-permute-start.5) | collective-permute-done | bytes 196640 | tf_op jit(solution)/shard_map/ppermute | solution.py:20
  31.4 1.9 %collective-permute-start.6 = (f32[2,288,128]{2,1,0:T(8,128)S(1)}, f32[2,288,128]{2,1,0:T(8,128)S(1)}, u32[]{:S(2)}, u32[]{:S(2)}) collective-permute-start(f32[2,288,128]{2,1,0:T(8,128)S(1)} %pad_maximum_fusion), channel_id=1, source_target_pairs={{0,8},{16,24},{32,40},{48,56},{64,72},{80,88},{96,104},{112,120},{... | collective-permute-start | bytes 884744 | tf_op jit(solution)/shard_map/ppermute | solution.py:20
  33.3 0.2 shard_map.145.part
  33.6 1.3 %collective-permute-done.6.other = f32[2,288,128]{2,1,0:T(8,128)S(1)} collective-permute-done((f32[2,288,128]{2,1,0:T(8,128)S(1)}, f32[2,288,128]{2,1,0:T(8,128)S(1)}, u32[]{:S(2)}, u32[]{:S(2)}) %collective-permute-start.6) | collective-permute-done | bytes 294944 | tf_op jit(solution)/shard_map/ppermute | solution.py:20
  34.9 0.8 %shard_map.146 = f32[2,3,16,256]{3,2,1,0:T(8,128)} custom-call(f32[2,288,128]{2,1,0:T(8,128)S(1)} %collective-permute-done.6.other, f32[2,1024,256]{2,1,0:T(8,128)S(1)} %get-tuple-element.56.dense, f32[2,3,16,256]{3,2,1,0:T(8,128)S(1)} %shard_map.145.part), custom_call_target="tpu_custom_call" | custom-call | tf_op jit(solution)/shard_map/pallas_call | solution.py:431
  (3 shorter events, 0.1 us)
Async XLA Ops:
  0.6 25.4 %copy-start = (f32[2,16,16,256]{3,2,1,0:T(8,128)S(1)}, f32[2,16,16,256]{3,2,1,0:T(8,128)}, u32[]{:S(2)}) copy-start(f32[2,16,16,256]{3,2,1,0:T(8,128)} %table.1) | copy-start | bytes 1572868
  0.6 25.4 %copy-start.3 = (s32[3]{0:T(128)S(1)}, s32[3]{0:T(128)}, u32[]{:S(2)}) copy-start(s32[3]{0:T(128)} %count_ref.1) | copy-start | bytes 40
  0.7 25.4 %copy-start.2 = (s32[3,16]{1,0:T(4,128)S(1)}, s32[3,16]{1,0:T(4,128)}, u32[]{:S(2)}) copy-start(s32[3,16]{1,0:T(4,128)} %offset_ref.1) | copy-start | bytes 580
  0.7 25.4 %copy-start.1 = (s32[3,16]{1,0:T(4,128)S(1)}, s32[3,16]{1,0:T(4,128)}, u32[]{:S(2)}) copy-start(s32[3,16]{1,0:T(4,128)} %partner_ref.1) | copy-start | bytes 580
  0.7 4.0 %collective-permute-start = (f32[2,192,128]{2,1,0:T(8,128)}, f32[2,192,128]{2,1,0:T(8,128)S(1)}, u32[]{:S(2)}, u32[]{:S(2)}) collective-permute-start(f32[2,192,128]{2,1,0:T(8,128)} %bitcast.6), channel_id=1, source_target_pairs={{0,8},{16,24},{32,40},{48,56},{64,72},{80,88},{96,104},{112,120},{... | collective-permute-start | bytes 589832 | tf_op jit(solution)/shard_map/ppermute | solution.py:20
  4.7 12.4 %collective-permute-start.1 = (f32[2,2,48,128]{3,2,1,0:T(8,128)S(1)}, f32[2,2,48,128]{3,2,1,0:T(8,128)S(1)}, u32[]{:S(2)}, u32[]{:S(2)}) collective-permute-start(f32[2,2,48,128]{3,2,1,0:T(8,128)S(1)} %get-tuple-element.41), channel_id=1, source_target_pairs={{0,1},{2,3},{4,5},{6,7},{1,0},{3,2},{5,4},{7,6},{8,9},{10,11},{12,... | collective-permute-start | bytes 294920 | tf_op jit(solution)/shard_map/ppermute | solution.py:20
  6.6 10.4 %collective-permute-start.2 = (f32[2,2,48,128]{3,2,1,0:T(8,128)S(1)}, f32[2,2,48,128]{3,2,1,0:T(8,128)S(1)}, u32[]{:S(2)}, u32[]{:S(2)}) collective-permute-start(f32[2,2,48,128]{3,2,1,0:T(8,128)S(1)} %get-tuple-element.42), channel_id=1, source_target_pairs={{1,2},{3,4},{5,6},{2,1},{4,3},{6,5},{9,10},{11,12},{13,14},{10,9},... | collective-permute-start | bytes 294920 | tf_op jit(solution)/shard_map/ppermute | solution.py:20
  13.0 14.9 %collective-permute-start.4 = (f32[2,192,128]{2,1,0:T(8,128)S(1)}, f32[2,192,128]{2,1,0:T(8,128)S(1)}, u32[]{:S(2)}, u32[]{:S(2)}) collective-permute-start(f32[2,192,128]{2,1,0:T(8,128)S(1)} %get-tuple-element.49.own_ref.own), channel_id=1, source_target_pairs={{8,16},{24,32},{40,48},{56,64},{72,80},{88,96},{104,112},{120,128}... | collective-permute-start | bytes 589832 | tf_op jit(solution)/shard_map/ppermute | solution.py:20
  18.0 12.9 %collective-permute-start.3 = (f32[2,192,128]{2,1,0:T(8,128)S(1)}, f32[2,192,128]{2,1,0:T(8,128)S(1)}, u32[]{:S(2)}, u32[]{:S(2)}) collective-permute-start(f32[2,192,128]{2,1,0:T(8,128)S(1)} %shard_map.142.pair_ref), channel_id=1, source_target_pairs={{8,32},{24,48},{40,64},{56,80},{72,96},{88,112},{104,128},{120,144... | collective-permute-start | bytes 589832 | tf_op jit(solution)/shard_map/ppermute | solution.py:20
  21.8 9.5 %collective-permute-start.5 = (f32[2,192,128]{2,1,0:T(8,128)S(1)}, f32[2,192,128]{2,1,0:T(8,128)S(1)}, u32[]{:S(2)}, u32[]{:S(2)}) collective-permute-start(f32[2,192,128]{2,1,0:T(8,128)S(1)} %shard_map.142.pair_ref), channel_id=1, source_target_pairs={{0,16},{32,48},{64,80},{96,112},{128,144},{160,176},{192,208},{224... | collective-permute-start | bytes 589832 | tf_op jit(solution)/shard_map/ppermute | solution.py:20
  31.4 3.5 %collective-permute-start.6 = (f32[2,288,128]{2,1,0:T(8,128)S(1)}, f32[2,288,128]{2,1,0:T(8,128)S(1)}, u32[]{:S(2)}, u32[]{:S(2)}) collective-permute-start(f32[2,288,128]{2,1,0:T(8,128)S(1)} %pad_maximum_fusion), channel_id=1, source_target_pairs={{0,8},{16,24},{32,40},{48,56},{64,72},{80,88},{96,104},{112,120},{... | collective-permute-start | bytes 884744 | tf_op jit(solution)/shard_map/ppermute | solution.py:20

commit v11 on v10

--- a/solution.py
+++ b/solution.py
@@ -34,6 +34,12 @@
 def swap_next(x):
     n = lax.axis_size("box")
     return matched(x, "box", [(i, i + 2) for i in range(0, n - 2, 4)] + [(i, i + 2) for i in range(3, n - 2, 4)])
+
+
+def swap_rims_across(x, start):
+    n, m = lax.axis_size("box"), lax.axis_size("samp")
+    pairs = [(i * m + z, (i ^ 1) * m + z + 1) for i in range(n) for z in range(start, m - 1, 2)]
+    return matched(x, ("box", "samp"), pairs)
 
 
 def swap_rims(x, start):
@@ -181,8 +187,8 @@
         columns = []
         for x in range(2):
             parts = [ref[x, 64 * k : 64 * k + 64]]
-            for rim_ref in (even_ref, odd_ref):
-                parts += [rim_ref[x, r, pl.ds(8 * box, 8)] for r in range(2)]
+            for rim_ref, first in ((even_ref, 8 * box), (odd_ref, 8 * ((box + 3) % 6))):
+                parts += [rim_ref[x, r, pl.ds(first, 8)] for r in range(2)]
             columns.append(jnp.concatenate(parts, axis=0))
         high, low = split(jnp.concatenate(columns, axis=1))
         return dot(theta, jnp.concatenate([high, low], axis=0)) + dot(theta_low, high)
@@ -460,7 +466,7 @@
     even, odd = rims(own, inner)
     even, odd, late = lax.optimization_barrier((even, odd, own))
     outer = swap_chips(late, 1, 1)
-    even, odd = swap_rims(even, 0), swap_rims(odd, 1)
+    even, odd = swap_rims(even, 0), swap_rims_across(odd, 1)
     pair = aggregate(own, inner, even, odd, mats)
     next_to, distant = swap_next(pair), swap_chips(pair, 1, 2)
     fine_incoming = fine_translate(

time: 36 us -> 36.4 us (1.011)
  waiting for transfers between devices: 1.79 us -> 2.16 us
    ppermute x7, waiting for transfers between devices: 1.79 us -> 2.16 us  [matched(): return lax.ppermute(x, axis, pairs + [(j, i) for i, j in pairs])]
where the time goes in v11:
time: 36.4 us; the launch traced here: 36 us
  starting transfers between devices  24.9 us (68%)
  Pallas kernels  8.04 us (22%)
  waiting for transfers between devices  2.16 us (6%)
  between operations  0.83 us (2%)
    ppermute x7, starting transfers between devices, matched(): return lax.ppermute(x, axis, pairs + [(j, i) for i, j in pairs])  24.9 us
    pallas_call x1, Pallas kernels, fine_translate(): pl.pallas_call(fine_kernel, out_shape=jax.ShapeDtypeStruct((2, 24, 8, 128...  2.96 us
    ppermute x7, waiting for transfers between devices, matched(): return lax.ppermute(x, axis, pairs + [(j, i) for i, j in pairs])  2.16 us
    pallas_call x1, Pallas kernels, first_translate(): pl.pallas_call(first_kernel, out_shape=(jax.ShapeDtypeStruct((2, 3, 16, 2...  1.86 us
    pallas_call x1, Pallas kernels, prepare(): pl.pallas_call(prepare_kernel, out_shape=tuple((jax.ShapeDtypeStruct(*s)...  1.21 us
    pallas_call x1, Pallas kernels, aggregate(): pl.pallas_call(aggregate_kernel, out_shape=jax.ShapeDtypeStruct((2, 192,...  0.95 us
    pallas_call x1, Pallas kernels, far_translate(): pl.pallas_call(far_kernel, out_shape=jax.ShapeDtypeStruct((2, 3, 16, 256)...  0.79 us
  transfers between devices with their start and end apart: 7, of which 2 were waited for; matrix products, arithmetic and copies ran while one was open for 0% of the time, Pallas kernels for 20%

profile of v11, /device:TPU:199, one launch (start us, length us, event | category | flops | bytes accessed | tf_op | source)
XLA Modules:
  0.0 36.0 jit_solution(3969412530560315941)
XLA Ops:
  0.6 0.0 copy-start
  0.6 0.0 copy-start.3
  0.7 0.0 copy-start.2
  0.7 0.0 copy-start.1
  0.7 2.7 %collective-permute-start = (f32[2,192,128]{2,1,0:T(8,128)}, f32[2,192,128]{2,1,0:T(8,128)S(1)}, u32[]{:S(2)}, u32[]{:S(2)}) collective-permute-start(f32[2,192,128]{2,1,0:T(8,128)} %bitcast.6), channel_id=1, source_target_pairs={{0,8},{16,24},{32,40},{48,56},{64,72},{80,88},{96,104},{112,120},{... | collective-permute-start | bytes 589832 | tf_op jit(solution)/shard_map/ppermute | solution.py:20
  3.4 1.2 %shard_map.140 = (f32[2,192,128]{2,1,0:T(8,128)S(1)}, bf16[128,192]{1,0:T(8,128)(2,1)S(1)}, bf16[128,96]{1,0:T(8,128)(2,1)S(1)}, bf16[256,256]{1,0:T(8,128)(2,1)...) custom-call(s32[16]{0:T(128)} %start.1, f32[4,16]{1,0:T(4,128)} %bitcast.12, ...), custom_call_target="tpu_custom_call" | custom-call | tf_op jit(solution)/shard_map/pallas_call | solution.py:164
  4.6 0.0 collective-permute-done.inner_ref.inner
  4.7 1.9 %collective-permute-start.1 = (f32[2,2,48,128]{3,2,1,0:T(8,128)S(1)}, f32[2,2,48,128]{3,2,1,0:T(8,128)S(1)}, u32[]{:S(2)}, u32[]{:S(2)}) collective-permute-start(f32[2,2,48,128]{3,2,1,0:T(8,128)S(1)} %get-tuple-element.41), channel_id=1, source_target_pairs={{0,1},{2,3},{4,5},{6,7},{1,0},{3,2},{5,4},{7,6},{8,9},{10,11},{12,... | collective-permute-start | bytes 294920 | tf_op jit(solution)/shard_map/ppermute | solution.py:20
  6.6 6.9 %collective-permute-start.2 = (f32[2,2,48,128]{3,2,1,0:T(8,128)S(1)}, f32[2,2,48,128]{3,2,1,0:T(8,128)S(1)}, u32[]{:S(2)}, u32[]{:S(2)}) collective-permute-start(f32[2,2,48,128]{3,2,1,0:T(8,128)S(1)} %get-tuple-element.42), channel_id=1, source_target_pairs={{1,10},{3,12},{5,14},{9,2},{11,4},{13,6},{17,26},{19,28},{21,30},{... | collective-permute-start | bytes 294920 | tf_op jit(solution)/shard_map/ppermute | solution.py:20
  13.6 2.9 %collective-permute-start.4 = (f32[2,192,128]{2,1,0:T(8,128)S(1)}, f32[2,192,128]{2,1,0:T(8,128)S(1)}, u32[]{:S(2)}, u32[]{:S(2)}) collective-permute-start(f32[2,192,128]{2,1,0:T(8,128)S(1)} %get-tuple-element.49.own_ref.own), channel_id=1, source_target_pairs={{8,16},{24,32},{40,48},{56,64},{72,80},{88,96},{104,112},{120,128}... | collective-permute-start | bytes 589832 | tf_op jit(solution)/shard_map/ppermute | solution.py:20
  16.5 0.0 collective-permute-done.1.even_ref
  16.5 0.0 collective-permute-done.2.odd_ref
  16.5 1.0 %shard_map.142.pair_ref = f32[2,192,128]{2,1,0:T(8,128)S(1)} custom-call(f32[2,192,128]{2,1,0:T(8,128)S(1)} %get-tuple-element.49.own_ref.own, f32[2,192,128]{2,1,0:T(8,128)S(1)} %collective-permute-done.inner_ref.inner, f32[2,2,48,128]{3,2,1,0:T(8,128)S(1)} %collective-permute-done.1.even_ref, f32[2,2,48,128]{3,2,1,0:T(8,128)S(1)} %collective-permute-done.2.odd_ref, ...), custom_call_target="tpu_custom_call" | custom-call | tf_op jit(solution)/shard_map/pallas_call | solution.py:226
  17.5 4.1 %collective-permute-start.3 = (f32[2,192,128]{2,1,0:T(8,128)S(1)}, f32[2,192,128]{2,1,0:T(8,128)S(1)}, u32[]{:S(2)}, u32[]{:S(2)}) collective-permute-start(f32[2,192,128]{2,1,0:T(8,128)S(1)} %shard_map.142.pair_ref), channel_id=1, source_target_pairs={{8,32},{24,48},{40,64},{56,80},{72,96},{88,112},{104,128},{120,144... | collective-permute-start | bytes 589832 | tf_op jit(solution)/shard_map/ppermute | solution.py:20
  21.6 4.2 %collective-permute-start.5 = (f32[2,192,128]{2,1,0:T(8,128)S(1)}, f32[2,192,128]{2,1,0:T(8,128)S(1)}, u32[]{:S(2)}, u32[]{:S(2)}) collective-permute-start(f32[2,192,128]{2,1,0:T(8,128)S(1)} %shard_map.142.pair_ref), channel_id=1, source_target_pairs={{0,16},{32,48},{64,80},{96,112},{128,144},{160,176},{192,208},{224... | collective-permute-start | bytes 589832 | tf_op jit(solution)/shard_map/ppermute | solution.py:20
  25.8 0.0 copy-done
  25.8 0.0 copy-done.3
  25.9 0.0 copy-done.2
  25.9 0.0 copy-done.1
  25.9 1.9 %shard_map.144 = (f32[2,3,16,256]{3,2,1,0:T(8,128)S(1)}, f32[2,1024,256]{2,1,0:T(8,128)S(1)}) custom-call(s32[3,16]{1,0:T(4,128)S(1)} %copy-done.1, s32[3,16]{1,0:T(4,128)S(1)} %copy-done.2, s32[3]{0:T(128)S(1)} %copy-done.3, f32[2,16,16,256]{3,2,1,0:T(8,128)S(1)} %copy-done, f32[2,192,128]{2,1,0:T(8,128)S(1)} %shard_map.142.pair_ref), custom_call_target="tpu_custom_call" | custom-call | tf_op jit(solution)/shard_map/pallas_call | solution.py:414
  27.7 0.0 collective-permute-done.4.outer
  27.8 3.0 %shard_map.143 = f32[2,24,8,128]{3,2,1,0:T(8,128)} custom-call(s32[16,24]{1,0:T(8,128)} %bitcast.10, s32[16,24]{1,0:T(8,128)} %bitcast.11, s32[24]{0:T(128)} %count.1, f32[2,128,128]{2,1,0:T(8,128)} %bitcast.8, f32[2,192,128]{2,1,0:T(8,128)S(1)} %get-tuple-element.49.own_ref.own, f32[2,192,128]{2,1,0:T(8,128)S(1)} %collective-permute-done.inner_ref.inner, ...), custom_call_target="tpu_custom_call" | custom-call | flops 4000000 | bytes 4000000 | tf_op jit(solution)/shard_map/pallas_call | solution.py:300
  30.7 0.0 collective-permute-done.3.distant_ref
  30.7 1.0 %collective-permute-done.5.next_ref = f32[2,192,128]{2,1,0:T(8,128)S(1)} collective-permute-done((f32[2,192,128]{2,1,0:T(8,128)S(1)}, f32[2,192,128]{2,1,0:T(8,128)S(1)}, u32[]{:S(2)}, u32[]{:S(2)}) %collective-permute-start.5) | collective-permute-done | bytes 196640 | tf_op jit(solution)/shard_map/ppermute | solution.py:20
  31.8 2.1 %collective-permute-start.6 = (f32[2,288,128]{2,1,0:T(8,128)S(1)}, f32[2,288,128]{2,1,0:T(8,128)S(1)}, u32[]{:S(2)}, u32[]{:S(2)}) collective-permute-start(f32[2,288,128]{2,1,0:T(8,128)S(1)} %pad_maximum_fusion), channel_id=1, source_target_pairs={{0,8},{16,24},{32,40},{48,56},{64,72},{80,88},{96,104},{112,120},{... | collective-permute-start | bytes 884744 | tf_op jit(solution)/shard_map/ppermute | solution.py:20
  33.9 0.2 shard_map.145.part
  34.1 1.1 %collective-permute-done.6.other = f32[2,288,128]{2,1,0:T(8,128)S(1)} collective-permute-done((f32[2,288,128]{2,1,0:T(8,128)S(1)}, f32[2,288,128]{2,1,0:T(8,128)S(1)}, u32[]{:S(2)}, u32[]{:S(2)}) %collective-permute-start.6) | collective-permute-done | bytes 294944 | tf_op jit(solution)/shard_map/ppermute | solution.py:20
  35.2 0.8 %shard_map.146 = f32[2,3,16,256]{3,2,1,0:T(8,128)} custom-call(f32[2,288,128]{2,1,0:T(8,128)S(1)} %collective-permute-done.6.other, f32[2,1024,256]{2,1,0:T(8,128)S(1)} %get-tuple-element.56.dense, f32[2,3,16,256]{3,2,1,0:T(8,128)S(1)} %shard_map.145.part), custom_call_target="tpu_custom_call" | custom-call | tf_op jit(solution)/shard_map/pallas_call | solution.py:437
  (3 shorter events, 0.1 us)
Async XLA Ops:
  0.6 25.2 %copy-start = (f32[2,16,16,256]{3,2,1,0:T(8,128)S(1)}, f32[2,16,16,256]{3,2,1,0:T(8,128)}, u32[]{:S(2)}) copy-start(f32[2,16,16,256]{3,2,1,0:T(8,128)} %table.1) | copy-start | bytes 1572868
  0.6 25.2 %copy-start.3 = (s32[3]{0:T(128)S(1)}, s32[3]{0:T(128)}, u32[]{:S(2)}) copy-start(s32[3]{0:T(128)} %count_ref.1) | copy-start | bytes 40
  0.7 25.2 %copy-start.2 = (s32[3,16]{1,0:T(4,128)S(1)}, s32[3,16]{1,0:T(4,128)}, u32[]{:S(2)}) copy-start(s32[3,16]{1,0:T(4,128)} %offset_ref.1) | copy-start | bytes 580
  0.7 25.2 %copy-start.1 = (s32[3,16]{1,0:T(4,128)S(1)}, s32[3,16]{1,0:T(4,128)}, u32[]{:S(2)}) copy-start(s32[3,16]{1,0:T(4,128)} %partner_ref.1) | copy-start | bytes 580
  0.7 4.0 %collective-permute-start = (f32[2,192,128]{2,1,0:T(8,128)}, f32[2,192,128]{2,1,0:T(8,128)S(1)}, u32[]{:S(2)}, u32[]{:S(2)}) collective-permute-start(f32[2,192,128]{2,1,0:T(8,128)} %bitcast.6), channel_id=1, source_target_pairs={{0,8},{16,24},{32,40},{48,56},{64,72},{80,88},{96,104},{112,120},{... | collective-permute-start | bytes 589832 | tf_op jit(solution)/shard_map/ppermute | solution.py:20
  4.7 11.8 %collective-permute-start.1 = (f32[2,2,48,128]{3,2,1,0:T(8,128)S(1)}, f32[2,2,48,128]{3,2,1,0:T(8,128)S(1)}, u32[]{:S(2)}, u32[]{:S(2)}) collective-permute-start(f32[2,2,48,128]{3,2,1,0:T(8,128)S(1)} %get-tuple-element.41), channel_id=1, source_target_pairs={{0,1},{2,3},{4,5},{6,7},{1,0},{3,2},{5,4},{7,6},{8,9},{10,11},{12,... | collective-permute-start | bytes 294920 | tf_op jit(solution)/shard_map/ppermute | solution.py:20
  6.6 9.9 %collective-permute-start.2 = (f32[2,2,48,128]{3,2,1,0:T(8,128)S(1)}, f32[2,2,48,128]{3,2,1,0:T(8,128)S(1)}, u32[]{:S(2)}, u32[]{:S(2)}) collective-permute-start(f32[2,2,48,128]{3,2,1,0:T(8,128)S(1)} %get-tuple-element.42), channel_id=1, source_target_pairs={{1,10},{3,12},{5,14},{9,2},{11,4},{13,6},{17,26},{19,28},{21,30},{... | collective-permute-start | bytes 294920 | tf_op jit(solution)/shard_map/ppermute | solution.py:20
  13.6 14.2 %collective-permute-start.4 = (f32[2,192,128]{2,1,0:T(8,128)S(1)}, f32[2,192,128]{2,1,0:T(8,128)S(1)}, u32[]{:S(2)}, u32[]{:S(2)}) collective-permute-start(f32[2,192,128]{2,1,0:T(8,128)S(1)} %get-tuple-element.49.own_ref.own), channel_id=1, source_target_pairs={{8,16},{24,32},{40,48},{56,64},{72,80},{88,96},{104,112},{120,128}... | collective-permute-start | bytes 589832 | tf_op jit(solution)/shard_map/ppermute | solution.py:20
  17.5 13.2 %collective-permute-start.3 = (f32[2,192,128]{2,1,0:T(8,128)S(1)}, f32[2,192,128]{2,1,0:T(8,128)S(1)}, u32[]{:S(2)}, u32[]{:S(2)}) collective-permute-start(f32[2,192,128]{2,1,0:T(8,128)S(1)} %shard_map.142.pair_ref), channel_id=1, source_target_pairs={{8,32},{24,48},{40,64},{56,80},{72,96},{88,112},{104,128},{120,144... | collective-permute-start | bytes 589832 | tf_op jit(solution)/shard_map/ppermute | solution.py:20
  21.6 10.1 %collective-permute-start.5 = (f32[2,192,128]{2,1,0:T(8,128)S(1)}, f32[2,192,128]{2,1,0:T(8,128)S(1)}, u32[]{:S(2)}, u32[]{:S(2)}) collective-permute-start(f32[2,192,128]{2,1,0:T(8,128)S(1)} %shard_map.142.pair_ref), channel_id=1, source_target_pairs={{0,16},{32,48},{64,80},{96,112},{128,144},{160,176},{192,208},{224... | collective-permute-start | bytes 589832 | tf_op jit(solution)/shard_map/ppermute | solution.py:20
  31.8 3.5 %collective-permute-start.6 = (f32[2,288,128]{2,1,0:T(8,128)S(1)}, f32[2,288,128]{2,1,0:T(8,128)S(1)}, u32[]{:S(2)}, u32[]{:S(2)}) collective-permute-start(f32[2,288,128]{2,1,0:T(8,128)S(1)} %pad_maximum_fusion), channel_id=1, source_target_pairs={{0,8},{16,24},{32,40},{48,56},{64,72},{80,88},{96,104},{112,120},{... | collective-permute-start | bytes 884744 | tf_op jit(solution)/shard_map/ppermute | solution.py:20
